TPU v7x, 256 devices: a whole 4x4x8 slice. The times are simulated.
256 devices in a mesh: grid: 16 (over z, core), tm: 16 (over y, x).
Axes of the slice: x: 4, y: 4, z: 8, core: 2. Of those that a mesh axis runs over, the one named last changes fastest.
Arguments:
- anomaly: bfloat16 [262144, 4096], P('grid', 'tm'), may hold values from -2000 to 2000
- start_basis: bfloat16 [32, 4096], P(None, 'tm'), may hold values from -6 to 6
Outputs:
- row_basis: float32 [32, 262144], P(None, 'grid')
- col_basis: float32 [32, 4096], P(None, 'tm')
All inputs are finite; a program needn't handle non-finite values.
Results may differ from a plain program's by a relative error of at most 0.035.
Values may be sent and summed in bfloat16 or wider, within the bound.
No kernel may reach another device: no remote copies, remote signals or barrier semaphores. Data moves between devices by JAX's collectives and lax.ppermute only.
A program may use at most 64 MiB of HBM per device.

v0:
```python
import jax
import jax.numpy as jnp
from jax import lax
from jax.sharding import PartitionSpec as P

ITERS = 6


def factor_solve(gram, block):
    lower = jnp.linalg.cholesky(gram)
    return jax.scipy.linalg.solve_triangular(lower, block, lower=True)


def upper_solve(gram, block):
    return factor_solve(gram[::-1, ::-1], block[::-1])[::-1]


def self_gram(block):
    return jnp.dot(
        block, block.T, precision=lax.Precision.HIGHEST, preferred_element_type=jnp.float32
    )


def shards(anomaly, start_basis):
    points = anomaly.shape[0] * lax.axis_size("grid")
    hour_count = anomaly.shape[1] * lax.axis_size("tm")
    current = start_basis
    row_basis = None
    col_basis = None
    for step in range(ITERS):
        partial_value = lax.dot_general(
            current, anomaly, (((1,), (1,)), ((), ())), preferred_element_type=jnp.float32
        )
        share = lax.psum_scatter(
            partial_value.astype(jnp.bfloat16), "tm", scatter_dimension=1, tiled=True
        ).astype(jnp.float32)
        gram = lax.psum(self_gram(share), ("grid", "tm")) / points
        basis_share = factor_solve(gram, share)
        row_basis = lax.all_gather(basis_share, "tm", axis=1, tiled=True)
        row_cast = row_basis.astype(jnp.bfloat16)
        hour_part = jnp.dot(row_cast, anomaly, preferred_element_type=jnp.float32)
        hour_piece = lax.psum_scatter(hour_part, "grid", scatter_dimension=1, tiled=True)
        hgram = lax.psum(self_gram(hour_piece), ("grid", "tm")) / hour_count
        col_piece = upper_solve(hgram, hour_piece)
        col_basis = lax.all_gather(col_piece, "grid", axis=1, tiled=True)
        current = col_basis.astype(jnp.bfloat16)
    return (row_basis, col_basis)


def solution(mesh):
    in_specs = (P("grid", "tm"), P(None, "tm"))
    out_specs = (P(None, "grid"), P(None, "tm"))
    return jax.shard_map(shards, mesh=mesh, in_specs=in_specs, out_specs=out_specs, check_vma=False)
```

profile of v0, /device:TPU:13, one launch (start us, length us, event | category | flops | bytes accessed | tf_op | source)
XLA Modules:
  0.0 2269.9 jit_solution(15815621228273958606)
XLA Ops:
  14.8 77.4 %reduce-scatter.13.cloned.1.call-done = bf16[32,1024]{1,0:T(8,128)(2,1)} async-done(((bf16[32,16384]{1,0:T(8,128)(2,1)}), bf16[32,1024]{1,0:T(8,128)(2,1)}) %reduce-scatter.13.cloned.1.call-update) | async-done | bytes 65552 | tf_op jit(solution)/shard_map/reduce_scatter | solution.py:34
  93.3 75.5 %psum.84 = f32[32,32]{0,1:T(8,128)S(1)} all-reduce(f32[32,32]{0,1:T(8,128)S(1)} %fusion.91), channel_id=1, replica_groups=mesh['grid'=16,'tm'=16] {'grid','tm'}, use_global_device_ids=true, to_apply=%region_1.0 | all-reduce | flops 1024 | bytes 8192 | tf_op jit(solution)/shard_map/psum | solution.py:37
  177.5 45.0 %all-gather.7.cloned.1.call-done = bf16[32,16384]{1,0:T(8,128)(2,1)} async-done(((bf16[32,1024]{1,0:T(8,128)(2,1)}), bf16[32,16384]{1,0:T(8,128)(2,1)}) %all-gather.7.cloned.1.call-update) | async-done | bytes 1048592 | tf_op jit(solution)/shard_map/all_gather | solution.py:39
  230.3 55.4 %reduce-scatter.15.cloned.1.call-done = f32[32,16]{0,1:T(8,128)} async-done(((f32[32,256]{0,1:T(8,128)}), f32[32,16]{0,1:T(8,128)}) %reduce-scatter.15.cloned.1.call-update) | async-done | bytes 2064 | tf_op jit(solution)/shard_map/reduce_scatter | solution.py:42
  286.7 76.4 %psum.85 = f32[32,32]{0,1:T(8,128)S(1)} all-reduce(f32[32,32]{0,1:T(8,128)S(1)} %reverse.18), channel_id=1, replica_groups=mesh['grid'=16,'tm'=16] {'grid','tm'}, use_global_device_ids=true, to_apply=%region_5.8 | all-reduce | flops 1024 | bytes 8192 | tf_op jit(solution)/shard_map/psum | solution.py:43
  393.5 72.9 %reduce-scatter.17.cloned.1.call-done = bf16[32,1024]{1,0:T(8,128)(2,1)} async-done(((bf16[32,16384]{1,0:T(8,128)(2,1)}), bf16[32,1024]{1,0:T(8,128)(2,1)}) %reduce-scatter.17.cloned.1.call-update) | async-done | bytes 65552 | tf_op jit(solution)/shard_map/reduce_scatter | solution.py:34
  467.4 75.5 %psum.86 = f32[32,32]{0,1:T(8,128)S(1)} all-reduce(f32[32,32]{0,1:T(8,128)S(1)} %fusion.93), channel_id=1, replica_groups=mesh['grid'=16,'tm'=16] {'grid','tm'}, use_global_device_ids=true, to_apply=%region_7.0 | all-reduce | flops 1024 | bytes 8192 | tf_op jit(solution)/shard_map/psum | solution.py:37
  552.1 44.5 %all-gather.9.cloned.1.call-done = bf16[32,16384]{1,0:T(8,128)(2,1)} async-done(((bf16[32,1024]{1,0:T(8,128)(2,1)}), bf16[32,16384]{1,0:T(8,128)(2,1)}) %all-gather.9.cloned.1.call-update) | async-done | bytes 1048592 | tf_op jit(solution)/shard_map/all_gather | solution.py:39
  604.4 55.4 %reduce-scatter.19.cloned.1.call-done = f32[32,16]{0,1:T(8,128)} async-done(((f32[32,256]{0,1:T(8,128)}), f32[32,16]{0,1:T(8,128)}) %reduce-scatter.19.cloned.1.call-update) | async-done | bytes 2064 | tf_op jit(solution)/shard_map/reduce_scatter | solution.py:42
  660.9 76.4 %psum.87 = f32[32,32]{0,1:T(8,128)S(1)} all-reduce(f32[32,32]{0,1:T(8,128)S(1)} %reverse.19), channel_id=1, replica_groups=mesh['grid'=16,'tm'=16] {'grid','tm'}, use_global_device_ids=true, to_apply=%region_9.0 | all-reduce | flops 1024 | bytes 8192 | tf_op jit(solution)/shard_map/psum | solution.py:43
  745.1 15.5 all_gather.39
  767.6 72.9 %reduce-scatter.21.cloned.1.call-done = bf16[32,1024]{1,0:T(8,128)(2,1)} async-done(((bf16[32,16384]{1,0:T(8,128)(2,1)}), bf16[32,1024]{1,0:T(8,128)(2,1)}) %reduce-scatter.21.cloned.1.call-update) | async-done | bytes 65552 | tf_op jit(solution)/shard_map/reduce_scatter | solution.py:34
  841.6 75.5 %psum.88 = f32[32,32]{0,1:T(8,128)S(1)} all-reduce(f32[32,32]{0,1:T(8,128)S(1)} %fusion.95), channel_id=1, replica_groups=mesh['grid'=16,'tm'=16] {'grid','tm'}, use_global_device_ids=true, to_apply=%region_11.0 | all-reduce | flops 1024 | bytes 8192 | tf_op jit(solution)/shard_map/psum | solution.py:37
  925.8 45.0 %all-gather.11.cloned.1.call-done = bf16[32,16384]{1,0:T(8,128)(2,1)} async-done(((bf16[32,1024]{1,0:T(8,128)(2,1)}), bf16[32,16384]{1,0:T(8,128)(2,1)}) %all-gather.11.cloned.1.call-update) | async-done | bytes 1048592 | tf_op jit(solution)/shard_map/all_gather | solution.py:39
  978.5 55.4 %reduce-scatter.23.cloned.1.call-done = f32[32,16]{0,1:T(8,128)} async-done(((f32[32,256]{0,1:T(8,128)}), f32[32,16]{0,1:T(8,128)}) %reduce-scatter.23.cloned.1.call-update) | async-done | bytes 2064 | tf_op jit(solution)/shard_map/reduce_scatter | solution.py:42
  1035.0 76.6 %psum.89 = f32[32,32]{0,1:T(8,128)S(1)} all-reduce(f32[32,32]{0,1:T(8,128)S(1)} %reverse.20), channel_id=1, replica_groups=mesh['grid'=16,'tm'=16] {'grid','tm'}, use_global_device_ids=true, to_apply=%region_13.0 | all-reduce | flops 1024 | bytes 8192 | tf_op jit(solution)/shard_map/psum | solution.py:43
  1141.9 72.9 %reduce-scatter.25.cloned.1.call-done = bf16[32,1024]{1,0:T(8,128)(2,1)} async-done(((bf16[32,16384]{1,0:T(8,128)(2,1)}), bf16[32,1024]{1,0:T(8,128)(2,1)}) %reduce-scatter.25.cloned.1.call-update) | async-done | bytes 65552 | tf_op jit(solution)/shard_map/reduce_scatter | solution.py:34
  1215.9 75.5 %psum.90 = f32[32,32]{0,1:T(8,128)S(1)} all-reduce(f32[32,32]{0,1:T(8,128)S(1)} %fusion.97), channel_id=1, replica_groups=mesh['grid'=16,'tm'=16] {'grid','tm'}, use_global_device_ids=true, to_apply=%region_15.0 | all-reduce | flops 1024 | bytes 8192 | tf_op jit(solution)/shard_map/psum | solution.py:37
  1300.1 45.0 %all-gather.13.cloned.1.call-done = bf16[32,16384]{1,0:T(8,128)(2,1)} async-done(((bf16[32,1024]{1,0:T(8,128)(2,1)}), bf16[32,16384]{1,0:T(8,128)(2,1)}) %all-gather.13.cloned.1.call-update) | async-done | bytes 1048592 | tf_op jit(solution)/shard_map/all_gather | solution.py:39
  1352.9 55.4 %reduce-scatter.27.cloned.1.call-done = f32[32,16]{0,1:T(8,128)} async-done(((f32[32,256]{0,1:T(8,128)}), f32[32,16]{0,1:T(8,128)}) %reduce-scatter.27.cloned.1.call-update) | async-done | bytes 2064 | tf_op jit(solution)/shard_map/reduce_scatter | solution.py:42
  1409.4 76.4 %psum.91 = f32[32,32]{0,1:T(8,128)S(1)} all-reduce(f32[32,32]{0,1:T(8,128)S(1)} %reverse.21), channel_id=1, replica_groups=mesh['grid'=16,'tm'=16] {'grid','tm'}, use_global_device_ids=true, to_apply=%region_17.0 | all-reduce | flops 1024 | bytes 8192 | tf_op jit(solution)/shard_map/psum | solution.py:43
  1516.1 73.0 %reduce-scatter.29.cloned.1.call-done = bf16[32,1024]{1,0:T(8,128)(2,1)} async-done(((bf16[32,16384]{1,0:T(8,128)(2,1)}), bf16[32,1024]{1,0:T(8,128)(2,1)}) %reduce-scatter.29.cloned.1.call-update) | async-done | bytes 65552 | tf_op jit(solution)/shard_map/reduce_scatter | solution.py:34
  1590.1 75.7 %psum.92 = f32[32,32]{0,1:T(8,128)S(1)} all-reduce(f32[32,32]{0,1:T(8,128)S(1)} %fusion.99), channel_id=1, replica_groups=mesh['grid'=16,'tm'=16] {'grid','tm'}, use_global_device_ids=true, to_apply=%region_19.0 | all-reduce | flops 1024 | bytes 8192 | tf_op jit(solution)/shard_map/psum | solution.py:37
  1674.6 44.9 %all-gather.15.cloned.1.call-done = bf16[32,16384]{1,0:T(8,128)(2,1)} async-done(((bf16[32,1024]{1,0:T(8,128)(2,1)}), bf16[32,16384]{1,0:T(8,128)(2,1)}) %all-gather.15.cloned.1.call-update) | async-done | bytes 1048592 | tf_op jit(solution)/shard_map/all_gather | solution.py:39
  1727.3 55.4 %reduce-scatter.31.cloned.1.call-done = f32[32,16]{0,1:T(8,128)} async-done(((f32[32,256]{0,1:T(8,128)}), f32[32,16]{0,1:T(8,128)}) %reduce-scatter.31.cloned.1.call-update) | async-done | bytes 2064 | tf_op jit(solution)/shard_map/reduce_scatter | solution.py:42
  1783.7 76.6 %psum.93 = f32[32,32]{0,1:T(8,128)S(1)} all-reduce(f32[32,32]{0,1:T(8,128)S(1)} %reverse.22), channel_id=1, replica_groups=mesh['grid'=16,'tm'=16] {'grid','tm'}, use_global_device_ids=true, to_apply=%region_21.0 | all-reduce | flops 1024 | bytes 8192 | tf_op jit(solution)/shard_map/psum | solution.py:43
  1890.5 72.9 %reduce-scatter.33.cloned.1.call-done = bf16[32,1024]{1,0:T(8,128)(2,1)} async-done(((bf16[32,16384]{1,0:T(8,128)(2,1)}), bf16[32,1024]{1,0:T(8,128)(2,1)}) %reduce-scatter.33.cloned.1.call-update) | async-done | bytes 65552 | tf_op jit(solution)/shard_map/reduce_scatter | solution.py:34
  1964.5 75.5 %psum.94 = f32[32,32]{0,1:T(8,128)S(1)} all-reduce(f32[32,32]{0,1:T(8,128)S(1)} %fusion.101), channel_id=1, replica_groups=mesh['grid'=16,'tm'=16] {'grid','tm'}, use_global_device_ids=true, to_apply=%region_23.0 | all-reduce | flops 1024 | bytes 8192 | tf_op jit(solution)/shard_map/psum | solution.py:37
  2049.0 47.2 %all-gather.17.cloned.1.call-done = f32[32,16384]{1,0:T(8,128)} async-done(((f32[32,1024]{1,0:T(8,128)}), f32[32,16384]{1,0:T(8,128)}) %all-gather.17.cloned.1.call-update) | async-done | bytes 2097168 | tf_op jit(solution)/shard_map/all_gather | solution.py:39
  2104.4 55.2 %reduce-scatter.35.cloned.1.call-done = f32[32,16]{0,1:T(8,128)} async-done(((f32[32,256]{0,1:T(8,128)}), f32[32,16]{0,1:T(8,128)}) %reduce-scatter.35.cloned.1.call-update) | async-done | bytes 2064 | tf_op jit(solution)/shard_map/reduce_scatter | solution.py:42
  2160.7 76.4 %psum.95 = f32[32,32]{0,1:T(8,128)S(1)} all-reduce(f32[32,32]{0,1:T(8,128)S(1)} %reverse.23), channel_id=1, replica_groups=mesh['grid'=16,'tm'=16] {'grid','tm'}, use_global_device_ids=true, to_apply=%region_25.29 | all-reduce | flops 1024 | bytes 8192 | tf_op jit(solution)/shard_map/psum | solution.py:43
  2244.9 15.7 all_gather.47
  (196 shorter events, 265.6 us)
Async XLA Ops:
  7.2 0.7 copy-start
  7.2 85.1 %reduce-scatter.13.cloned.1.call-start = ((), (), s32[]{:S(2)}) async-start(), calls=%async_computation.12 | async-start | bytes 1114112 | tf_op jit(solution)/shard_map/reduce_scatter | solution.py:34
  14.8 207.7 %all-gather.7.cloned.1.call-start = ((), (), s32[]{:S(2)}) async-start(), calls=%async_computation.13 | async-start | bytes 1114112 | tf_op jit(solution)/shard_map/all_gather | solution.py:39
  177.5 108.2 %reduce-scatter.15.cloned.1.call-start = ((), (), s32[]{:S(2)}) async-start(), calls=%async_computation.14 | async-start | bytes 139264 | tf_op jit(solution)/shard_map/reduce_scatter | solution.py:42
  230.2 236.2 %reduce-scatter.17.cloned.1.call-start = ((), (), s32[]{:S(2)}) async-start(), calls=%async_computation.15 | async-start | bytes 1114112 | tf_op jit(solution)/shard_map/reduce_scatter | solution.py:34
  393.4 203.2 %all-gather.9.cloned.1.call-start = ((), (), s32[]{:S(2)}) async-start(), calls=%async_computation.16 | async-start | bytes 1114112 | tf_op jit(solution)/shard_map/all_gather | solution.py:39
  551.6 108.2 %reduce-scatter.19.cloned.1.call-start = ((), (), s32[]{:S(2)}) async-start(), calls=%async_computation.17 | async-start | bytes 139264 | tf_op jit(solution)/shard_map/reduce_scatter | solution.py:42
  604.4 236.2 %reduce-scatter.21.cloned.1.call-start = ((), (), s32[]{:S(2)}) async-start(), calls=%async_computation.18 | async-start | bytes 1114112 | tf_op jit(solution)/shard_map/reduce_scatter | solution.py:34
  767.6 203.2 %all-gather.11.cloned.1.call-start = ((), (), s32[]{:S(2)}) async-start(), calls=%async_computation.19 | async-start | bytes 1114112 | tf_op jit(solution)/shard_map/all_gather | solution.py:39
  925.7 108.2 %reduce-scatter.23.cloned.1.call-start = ((), (), s32[]{:S(2)}) async-start(), calls=%async_computation.20 | async-start | bytes 139264 | tf_op jit(solution)/shard_map/reduce_scatter | solution.py:42
  978.5 236.4 %reduce-scatter.25.cloned.1.call-start = ((), (), s32[]{:S(2)}) async-start(), calls=%async_computation.21 | async-start | bytes 1114112 | tf_op jit(solution)/shard_map/reduce_scatter | solution.py:34
  1141.9 203.2 %all-gather.13.cloned.1.call-start = ((), (), s32[]{:S(2)}) async-start(), calls=%async_computation.22 | async-start | bytes 1114112 | tf_op jit(solution)/shard_map/all_gather | solution.py:39
  1300.1 108.2 %reduce-scatter.27.cloned.1.call-start = ((), (), s32[]{:S(2)}) async-start(), calls=%async_computation.23 | async-start | bytes 139264 | tf_op jit(solution)/shard_map/reduce_scatter | solution.py:42
  1352.9 236.2 %reduce-scatter.29.cloned.1.call-start = ((), (), s32[]{:S(2)}) async-start(), calls=%async_computation.24 | async-start | bytes 1114112 | tf_op jit(solution)/shard_map/reduce_scatter | solution.py:34
  1516.1 203.4 %all-gather.15.cloned.1.call-start = ((), (), s32[]{:S(2)}) async-start(), calls=%async_computation.25 | async-start | bytes 1114112 | tf_op jit(solution)/shard_map/all_gather | solution.py:39
  1674.5 108.2 %reduce-scatter.31.cloned.1.call-start = ((), (), s32[]{:S(2)}) async-start(), calls=%async_computation.26 | async-start | bytes 139264 | tf_op jit(solution)/shard_map/reduce_scatter | solution.py:42
  1727.2 236.2 %reduce-scatter.33.cloned.1.call-start = ((), (), s32[]{:S(2)}) async-start(), calls=%async_computation.27 | async-start | bytes 1114112 | tf_op jit(solution)/shard_map/reduce_scatter | solution.py:34
  1890.5 205.7 %all-gather.17.cloned.1.call-start = ((), (), s32[]{:S(2)}) async-start(), calls=%async_computation.28 | async-start | bytes 2228224 | tf_op jit(solution)/shard_map/all_gather | solution.py:39
  2048.7 110.9 %reduce-scatter.35.cloned.1.call-start = ((), (), s32[]{:S(2)}) async-start(), calls=%async_computation.29 | async-start | bytes 139264 | tf_op jit(solution)/shard_map/reduce_scatter | solution.py:42
  2096.2 165.1 %copy-start.1 = (f32[32,16384]{1,0:T(8,128)S(1)}, f32[32,16384]{1,0:T(8,128)}, u32[]{:S(2)}) copy-start(f32[32,16384]{1,0:T(8,128)} %all-gather.17.cloned.1.call-done) | copy-start | bytes 6291460
Sparse Core Ops, SparseCore 0:
  14.9 77.3 reduce-scatter.12
  177.6 44.8 all-gather.6
  230.3 55.2 reduce-scatter.14
  393.6 72.7 reduce-scatter.16
  551.7 44.8 all-gather.8
  604.5 55.2 reduce-scatter.18
  767.7 72.7 reduce-scatter.20
  925.8 44.8 all-gather.10
  978.6 55.2 reduce-scatter.22
  1142.0 72.8 reduce-scatter.24
  1300.2 44.8 all-gather.12
  1353.0 55.2 reduce-scatter.26
  1516.2 72.8 reduce-scatter.28
  1674.6 44.7 all-gather.14
  1727.4 55.2 reduce-scatter.30
  1890.6 72.8 reduce-scatter.32
  2048.8 47.3 all-gather.16
  2104.5 55.0 reduce-scatter.34
where the time goes:
time: 2290 us; the launch traced here: 2270 us
  waiting for transfers between devices  1050 us (46%)
  blocking collectives  1010 us (44%)
  matrix products  112 us (5%)
  other arithmetic  80.3 us (4%)
    psum x6, blocking collectives, shards(): hgram = lax.psum(self_gram(hour_piece), ('grid', 'tm')) / hour_count  459 us
    psum x6, blocking collectives, shards(): gram = lax.psum(self_gram(share), ('grid', 'tm')) / points  453 us
    reduce_scatter x6, waiting for transfers between devices, shards(): lax.psum_scatter(partial_value.astype(jnp.bfloat16), 'tm', scatter_dimens...  442 us
    reduce_scatter x6, waiting for transfers between devices, shards(): lax.psum_scatter(hour_part, 'grid', scatter_dimension=1, tiled=True)  332 us
    all_gather x6, waiting for transfers between devices, shards(): row_basis = lax.all_gather(basis_share, 'tm', axis=1, tiled=True)  272 us
    all_gather x6, blocking collectives, shards(): col_basis = lax.all_gather(col_piece, 'grid', axis=1, tiled=True)  93 us
    dot_general x6, matrix products, shards(): hour_part = jnp.dot(row_cast, anomaly, preferred_element_type=jnp.float32)  46.8 us
  transfers between devices with their start and end apart: 18, of which 18 were waited for; matrix products, arithmetic and copies ran while one was open for 0% of the time, Pallas kernels for 0%

commit v1 on v0

v1 whole, which is shorter than its diff:
```python
import jax
import jax.numpy as jnp
from jax import lax
from jax.experimental import pallas as pl
from jax.experimental.pallas import tpu as pltpu
from jax.sharding import Mesh, PartitionSpec as P

ITERS = 6
RANK = 32
LANES = 128
EXTRA = RANK * RANK // LANES
ROWS = RANK + EXTRA
F32 = jnp.float32
BF16 = jnp.bfloat16
HIGH = lax.Precision.HIGHEST
NT = (((1,), (1,)), ((), ()))


def split_bf16(value):
    high = value.astype(BF16)
    low = (value - high.astype(F32)).astype(BF16)
    return jnp.concatenate([high, low], axis=0)


def packed_gram(block):
    tiled = jnp.concatenate([block] * (LANES // RANK), axis=0)
    wide = lax.dot_general(block, tiled, NT, precision=HIGH, preferred_element_type=F32)
    lane = lax.broadcasted_iota(jnp.int32, (EXTRA, LANES), 1) // RANK
    out = wide[0:EXTRA]
    for b in range(1, LANES // RANK):
        out = jnp.where(lane == b, wide[b * EXTRA : (b + 1) * EXTRA], out)
    return out


def inverse_factor(packed, upper):
    parts = RANK // EXTRA
    shape = (EXTRA, LANES)
    lane = lax.broadcasted_iota(jnp.int32, shape, 1)
    sub = lax.broadcasted_iota(jnp.int32, shape, 0)
    work = []
    for b in range(parts):
        shift = (RANK - b * RANK) % LANES
        gram = pltpu.roll(packed, shift, 1) if shift else packed
        gram = jnp.where(lane < 2 * RANK, gram, 0.0)
        work.append(jnp.where(lane < RANK, (lane == sub + b * EXTRA).astype(F32), gram))
    scale = []
    places = range(EXTRA - 1, -1, -1) if upper else range(EXTRA)
    for block in range(parts - 1, -1, -1) if upper else range(parts):
        beyond = range(block) if upper else range(block + 1, parts)
        cols = {
            b: [jnp.broadcast_to(work[b][:, c : c + 1], shape) for c in [RANK + block * EXTRA + r for r in places]]
            for b in (block, *beyond)
        }
        rows = [jnp.broadcast_to(work[block][r : r + 1, :], shape) for r in places]
        pivots = [[jnp.broadcast_to(col[r : r + 1, :], shape) for col in cols[block]] for r in places]
        scaled = []
        final = work[block]
        diagonal = pivots[0][0]
        for i, r in enumerate(places):
            inverse = 1.0 / pivots[i][i]
            for j in range(i + 1, EXTRA):
                factor = pivots[i][j] * inverse
                for k in range(j, EXTRA):
                    pivots[j][k] = pivots[j][k] - factor * pivots[i][k]
                rows[j] = rows[j] - factor * rows[i]
                for b in beyond:
                    cols[b][j] = cols[b][j] - factor * cols[b][i]
            scaled.append(rows[i] * inverse)
            final = jnp.where(sub == r, rows[i], final)
            diagonal = jnp.where(sub == r, pivots[i][i], diagonal)
        work[block] = final
        scale.append((block, diagonal))
        for b in beyond:
            for i in range(EXTRA):
                work[b] = work[b] - cols[b][i] * scaled[i]
    rows = [work[b] / jnp.sqrt(diagonal) for b, diagonal in sorted(scale, key=lambda item: item[0])]
    return jnp.concatenate(rows, axis=0)[:, :RANK]


def main_kernel(points, hours, first, keep, h_ref, a_ref, out_ref, s_ref, a_vmem, acc, sems):
    blocks, depth, width = a_vmem.shape
    for t in range(blocks):
        pltpu.make_async_copy(a_ref.at[t], a_vmem.at[t], sems.at[t]).start()
    if not first:
        total = h_ref[0, RANK:ROWS, :]
        for k in range(1, 2 * blocks):
            total = total + h_ref[k, RANK:ROWS, :]
        u_inv = inverse_factor(total, True) * float(hours) ** 0.5
    for t in range(blocks):
        if first:
            left = h_ref[t]
        else:
            left = split_bf16(jnp.concatenate([h_ref[t, 0:RANK, :], h_ref[blocks + t, 0:RANK, :]], axis=1))
        pltpu.make_async_copy(a_ref.at[t], a_vmem.at[t], sems.at[t]).wait()
        term = lax.dot_general(left, a_vmem[t], NT, preferred_element_type=F32)
        if t == 0:
            acc[0 : left.shape[0], :] = term
        else:
            acc[0 : left.shape[0], :] += term
    if first:
        sketch = acc[0:RANK, :]
    else:
        sketch = jnp.dot(
            u_inv, acc[0:RANK, :] + acc[RANK : 2 * RANK, :], precision=HIGH, preferred_element_type=F32
        )
    if keep:
        s_ref[...] = sketch.astype(BF16)
    gram = packed_gram(sketch)
    left = split_bf16(sketch)
    for t in range(blocks):
        both = jnp.dot(left, a_vmem[t], preferred_element_type=F32)
        part = both[0:RANK] + both[RANK : 2 * RANK]
        out_ref[t, 0:RANK, :] = part[:, 0:LANES]
        out_ref[blocks + t, 0:RANK, :] = part[:, LANES : 2 * LANES]
        out_ref[t, RANK:ROWS, :] = gram
        out_ref[blocks + t, RANK:ROWS, :] = gram


def main_step(points, hours, first, keep, h, a):
    blocks, depth, width = a.shape

    def kernel(h_ref, a_ref, out_ref, *rest):
        s_ref, rest = (rest[0], rest[1:]) if keep else (None, rest)
        main_kernel(points, hours, first, keep, h_ref, a_ref, out_ref, s_ref, *rest)

    out_shape = [jax.ShapeDtypeStruct((2 * blocks, ROWS, LANES), F32)]
    if keep:
        out_shape.append(jax.ShapeDtypeStruct((RANK, depth), BF16))
    return pl.pallas_call(
        kernel,
        out_shape=out_shape,
        in_specs=[pl.BlockSpec(memory_space=pltpu.VMEM), pl.BlockSpec(memory_space=pl.ANY)],
        out_specs=[pl.BlockSpec(memory_space=pltpu.VMEM)] * len(out_shape),
        scratch_shapes=[
            pltpu.VMEM(a.shape, BF16),
            pltpu.VMEM((2 * RANK, depth), F32),
            pltpu.SemaphoreType.DMA((blocks,)),
        ],
        compiler_params=pltpu.CompilerParams(vmem_limit_bytes=52 * 1024 * 1024),
        name="sketch_and_hours",
    )(h, a)


def sum_step(parts, copies):
    def kernel(in_ref, out_ref):
        total = in_ref[0]
        for k in range(1, parts.shape[0]):
            total = total + in_ref[k]
        for k in range(copies):
            out_ref[k] = total

    return pl.pallas_call(
        kernel,
        out_shape=jax.ShapeDtypeStruct((copies,) + parts.shape[1:], F32),
        in_specs=[pl.BlockSpec(memory_space=pltpu.VMEM)],
        out_specs=pl.BlockSpec(memory_space=pltpu.VMEM),
        name="sum_parts",
    )(parts)


def hour_step(parts, copies, points):
    def kernel(in_ref, out_ref, l_ref):
        total = in_ref[0]
        for k in range(1, parts.shape[0]):
            total = total + in_ref[k]
        l_inv = inverse_factor(total[RANK:ROWS], False) * float(points) ** 0.5
        hours = jnp.dot(l_inv, total[0:RANK], precision=HIGH, preferred_element_type=F32)
        gram = packed_gram(hours)
        for k in range(copies):
            out_ref[k, 0:RANK, :] = hours
            out_ref[k, RANK:ROWS, :] = gram
        l_ref[...] = l_inv

    return pl.pallas_call(
        kernel,
        out_shape=[
            jax.ShapeDtypeStruct((copies, ROWS, LANES), F32),
            jax.ShapeDtypeStruct((RANK, RANK), F32),
        ],
        in_specs=[pl.BlockSpec(memory_space=pltpu.VMEM)],
        out_specs=[pl.BlockSpec(memory_space=pltpu.VMEM)] * 2,
        name="row_factor",
    )(parts)


def column_step(h, mine, hours):
    def kernel(h_ref, mine_ref, out_ref):
        total = h_ref[0, RANK:ROWS, :]
        for k in range(1, h_ref.shape[0]):
            total = total + h_ref[k, RANK:ROWS, :]
        u_inv = inverse_factor(total, True) * float(hours) ** 0.5
        block = jnp.concatenate([mine_ref[0, 0:RANK, :], mine_ref[1, 0:RANK, :]], axis=1)
        out_ref[...] = jnp.dot(u_inv, block, precision=HIGH, preferred_element_type=F32)

    return pl.pallas_call(
        kernel,
        out_shape=jax.ShapeDtypeStruct((RANK, 2 * LANES), F32),
        in_specs=[pl.BlockSpec(memory_space=pltpu.VMEM)] * 2,
        out_specs=pl.BlockSpec(memory_space=pltpu.VMEM),
        name="column_factor",
    )(h, mine)


def row_step(l_inv, sketch):
    def kernel(l_ref, s_ref, out_ref):
        value = l_ref[...]
        pieces = []
        for _ in range(3):
            piece = value.astype(BF16)
            pieces.append(piece)
            value = value - piece.astype(F32)
        left = jnp.concatenate(pieces, axis=0)
        out = jnp.dot(left, s_ref[0], preferred_element_type=F32)
        out_ref[...] = out[0:RANK] + out[RANK : 2 * RANK] + out[2 * RANK : 3 * RANK]

    blocks, _, depth = sketch.shape
    return pl.pallas_call(
        kernel,
        grid=(blocks,),
        out_shape=jax.ShapeDtypeStruct((RANK, blocks * depth), F32),
        in_specs=[
            pl.BlockSpec((RANK, RANK), lambda i: (0, 0)),
            pl.BlockSpec((1, RANK, depth), lambda i: (i, 0, 0)),
        ],
        out_specs=pl.BlockSpec((RANK, depth), lambda i: (0, i)),
        cost_estimate=pl.CostEstimate(
            flops=6 * RANK * RANK * blocks * depth, bytes_accessed=6 * RANK * blocks * depth, transcendentals=0
        ),
        name="row_basis",
    )(l_inv, sketch)


def solution(mesh):
    grid_size, tm_size = mesh.devices.shape
    fine = Mesh(mesh.devices.reshape(grid_size // 2, 2, tm_size), ("z", "c", "t"))

    def shards(anomaly, start_basis):
        points = anomaly.shape[0] * grid_size
        hours = anomaly.shape[1] * tm_size
        depth = anomaly.shape[0] // tm_size
        basis = jnp.broadcast_to(start_basis[None], (tm_size,) + start_basis.shape)
        h = lax.all_to_all(basis, "t", 0, 0)
        a = lax.all_to_all(anomaly.reshape(tm_size, depth, anomaly.shape[1]), "t", 0, 0)
        for step in range(ITERS):
            last = step == ITERS - 1
            out = main_step(points, hours, step == 0, last, h, a)
            if last:
                rows = lax.all_gather(out[1], "t", axis=0)
            part = lax.all_to_all(out[0], ("c", "t"), 0, 0)
            part = sum_step(part, grid_size // 2)
            part = lax.all_to_all(part, "z", 0, 0)
            h, l_inv = hour_step(part, 2 * tm_size, points)
            h = lax.all_to_all(h, ("c", "t"), 0, 0)
        place = lax.axis_index("t")
        mine = lax.dynamic_index_in_dim(h.reshape(2, tm_size, ROWS, LANES), place, 1, False)
        return row_step(l_inv, rows), column_step(h, mine, hours)

    return jax.shard_map(
        shards,
        mesh=fine,
        in_specs=(P(("z", "c"), "t"), P(None, "t")),
        out_specs=(P(None, ("z", "c")), P(None, "t")),
        check_vma=False,
    )
```

time: 2290 us -> 511 us (0.22)
  waiting for transfers between devices: 1050 us -> 9.97 us
  blocking collectives: 1010 us -> 389 us
  matrix products: 112 us -> 0 us
  Pallas kernels: 0 us -> 82.6 us
  other arithmetic: 80.3 us -> 0 us
    psum x12 -> x0, blocking collectives: 912 us -> none  [the longest x6 459 us: shards(): hgram = lax.psum(self_gram(hour_piece), ('grid', 'tm')) / hour_count]
    reduce_scatter x12 -> x0, waiting for transfers between devices: 774 us -> none  [the longest x6 442 us: shards(): lax.psum_scatter(partial_value.astype(jnp.bfloat16), 'tm', scatter_dimens...]
    all_to_all x0 -> x19, blocking collectives: none -> 389 us  [the longest x6 105 us: shards(): part = lax.all_to_all(out[0], ('c', 't'), 0, 0)]
    all_gather x6 -> x1, waiting for transfers between devices: 272 us -> 0.01 us  [shards(): rows = lax.all_gather(out[1], 't', axis=0)]
    dot_general x24 -> x0, matrix products: 101 us -> none  [the longest x6 46.8 us: shards(): hour_part = jnp.dot(row_cast, anomaly, preferred_element_type=jnp.float32)]
    all_gather x6 -> x0, blocking collectives: 93 us -> none  [shards(): col_basis = lax.all_gather(col_piece, 'grid', axis=1, tiled=True)]
    pallas_call x0 -> x20, Pallas kernels: none -> 82.6 us  [the longest x6 40.8 us: main_step(): pl.pallas_call(kernel, out_shape=out_shape, in_specs=[pl.BlockSpec(memory...]
    another operation x60 -> x0, other arithmetic: 80.2 us -> none  [the longest x36 43.1 us: factor_solve(): lower = jnp.linalg.cholesky(gram)]
  transfers between devices with their start and end apart: 18 -> 2, of which waited for: 18 -> 1; matrix products, arithmetic and copies ran while one was open for 0% -> 0% of each run, Pallas kernels for 0% -> 2%
where the time goes in v1:
time: 511 us; the launch traced here: 505 us
  blocking collectives  389 us (76%)
  Pallas kernels  82.6 us (16%)
  between operations  14.1 us (3%)
  waiting for transfers between devices  9.97 us (2%)
  starting transfers between devices  8.08 us (2%)
    all_to_all x6, blocking collectives, shards(): part = lax.all_to_all(out[0], ('c', 't'), 0, 0)  105 us
    all_to_all x1, blocking collectives, shards(): lax.all_to_all(anomaly.reshape(tm_size, depth, anomaly.shape[1]), 't', 0, 0)  99.6 us
    all_to_all x5, blocking collectives, shards(): h = lax.all_to_all(h, ('c', 't'), 0, 0)  90.5 us
    all_to_all x6, blocking collectives, shards(): part = lax.all_to_all(part, 'z', 0, 0)  82.2 us
    pallas_call x6, Pallas kernels, main_step(): pl.pallas_call(kernel, out_shape=out_shape, in_specs=[pl.BlockSpec(memory...  40.8 us
    pallas_call x6, Pallas kernels, hour_step(): pl.pallas_call(kernel, out_shape=[jax.ShapeDtypeStruct((copies, ROWS, LAN...  18.1 us
    all_to_all x1, blocking collectives, shards(): h = lax.all_to_all(basis, 't', 0, 0)  11.3 us
    pallas_call x6, Pallas kernels, sum_step(): pl.pallas_call(kernel, out_shape=jax.ShapeDtypeStruct((copies,) + parts.s...  10.8 us
  transfers between devices with their start and end apart: 2, of which 1 were waited for; matrix products, arithmetic and copies ran while one was open for 0% of the time, Pallas kernels for 2%

profile of v1, /device:TPU:13, one launch (start us, length us, event | category | flops | bytes accessed | tf_op | source)
XLA Modules:
  0.0 505.1 jit_solution(14135134733396639281)
XLA Ops:
  8.0 11.3 %all_to_all.100.h_ref = bf16[16,32,256]{2,1,0:T(8,128)(2,1)S(1)} all-to-all(bf16[16,32,256]{2,1,0:T(8,128)(2,1)S(1)} %broadcast_in_dim.2), channel_id=1, replica_groups=mesh['z'=8,'c'=2,'t'=16] {'t'}, dimensions={0} | all-to-all | bytes 524288 | tf_op jit(solution)/shard_map/all_to_all | solution.py:242
  19.2 99.6 %all_to_all.101.a_ref = bf16[16,1024,256]{2,1,0:T(8,128)(2,1)} all-to-all(bf16[16,1024,256]{2,1,0:T(8,128)(2,1)} %bitcast.7), channel_id=1, replica_groups=mesh['z'=8,'c'=2,'t'=16] {'t'}, dimensions={0} | all-to-all | bytes 16777216 | tf_op jit(solution)/shard_map/all_to_all | solution.py:243
  118.8 5.9 %sketch_and_hours.6 = f32[32,40,128]{2,1,0:T(8,128)S(1)} custom-call(bf16[16,32,256]{2,1,0:T(8,128)(2,1)S(1)} %all_to_all.100.h_ref, bf16[16,1024,256]{2,1,0:T(8,128)(2,1)} %all_to_all.101.a_ref), custom_call_target="tpu_custom_call" | custom-call | tf_op jit(solution)/shard_map/sketch_and_hours/pallas_call | solution.py:129
  124.7 19.7 %all_to_all.102.in_ref = f32[32,40,128]{2,1,0:T(8,128)} all-to-all(f32[32,40,128]{2,1,0:T(8,128)S(1)} %sketch_and_hours.6), channel_id=1, replica_groups=mesh['z'=8,'c'=2,'t'=16] {'c','t'}, dimensions={0} | all-to-all | bytes 1310720 | tf_op jit(solution)/shard_map/all_to_all | solution.py:249
  146.1 16.9 %all_to_all.103.in_ref = f32[8,40,128]{2,1,0:T(8,128)} all-to-all(f32[8,40,128]{2,1,0:T(8,128)} %sum_parts.6), channel_id=1, replica_groups=mesh['z'=8,'c'=2,'t'=16] {'z'}, dimensions={0} | all-to-all | bytes 327680 | tf_op jit(solution)/shard_map/all_to_all | solution.py:251
  163.0 3.0 row_factor.6
  166.0 18.5 %all_to_all.104.h_ref = f32[32,40,128]{2,1,0:T(8,128)S(1)} all-to-all(f32[32,40,128]{2,1,0:T(8,128)} %get-tuple-element.11), channel_id=1, replica_groups=mesh['z'=8,'c'=2,'t'=16] {'c','t'}, dimensions={0} | all-to-all | bytes 1310720 | tf_op jit(solution)/shard_map/all_to_all | solution.py:253
  184.5 7.0 %sketch_and_hours.7 = f32[32,40,128]{2,1,0:T(8,128)S(1)} custom-call(f32[32,40,128]{2,1,0:T(8,128)S(1)} %all_to_all.104.h_ref, bf16[16,1024,256]{2,1,0:T(8,128)(2,1)} %all_to_all.101.a_ref), custom_call_target="tpu_custom_call" | custom-call | tf_op jit(solution)/shard_map/sketch_and_hours/pallas_call | solution.py:129
  191.5 17.0 %all_to_all.105.in_ref = f32[32,40,128]{2,1,0:T(8,128)} all-to-all(f32[32,40,128]{2,1,0:T(8,128)S(1)} %sketch_and_hours.7), channel_id=1, replica_groups=mesh['z'=8,'c'=2,'t'=16] {'c','t'}, dimensions={0} | all-to-all | bytes 1310720 | tf_op jit(solution)/shard_map/all_to_all | solution.py:249
  210.3 13.1 %all_to_all.106.in_ref = f32[8,40,128]{2,1,0:T(8,128)} all-to-all(f32[8,40,128]{2,1,0:T(8,128)} %sum_parts.7), channel_id=1, replica_groups=mesh['z'=8,'c'=2,'t'=16] {'z'}, dimensions={0} | all-to-all | bytes 327680 | tf_op jit(solution)/shard_map/all_to_all | solution.py:251
  226.4 18.0 %all_to_all.107.h_ref = f32[32,40,128]{2,1,0:T(8,128)S(1)} all-to-all(f32[32,40,128]{2,1,0:T(8,128)} %get-tuple-element.12), channel_id=1, replica_groups=mesh['z'=8,'c'=2,'t'=16] {'c','t'}, dimensions={0} | all-to-all | bytes 1310720 | tf_op jit(solution)/shard_map/all_to_all | solution.py:253
  244.4 7.0 %sketch_and_hours.8 = f32[32,40,128]{2,1,0:T(8,128)S(1)} custom-call(f32[32,40,128]{2,1,0:T(8,128)S(1)} %all_to_all.107.h_ref, bf16[16,1024,256]{2,1,0:T(8,128)(2,1)} %all_to_all.101.a_ref), custom_call_target="tpu_custom_call" | custom-call | tf_op jit(solution)/shard_map/sketch_and_hours/pallas_call | solution.py:129
  251.4 17.0 %all_to_all.108.in_ref = f32[32,40,128]{2,1,0:T(8,128)} all-to-all(f32[32,40,128]{2,1,0:T(8,128)S(1)} %sketch_and_hours.8), channel_id=1, replica_groups=mesh['z'=8,'c'=2,'t'=16] {'c','t'}, dimensions={0} | all-to-all | bytes 1310720 | tf_op jit(solution)/shard_map/all_to_all | solution.py:249
  270.2 13.1 %all_to_all.109.in_ref = f32[8,40,128]{2,1,0:T(8,128)} all-to-all(f32[8,40,128]{2,1,0:T(8,128)} %sum_parts.8), channel_id=1, replica_groups=mesh['z'=8,'c'=2,'t'=16] {'z'}, dimensions={0} | all-to-all | bytes 327680 | tf_op jit(solution)/shard_map/all_to_all | solution.py:251
  286.2 18.0 %all_to_all.110.h_ref = f32[32,40,128]{2,1,0:T(8,128)S(1)} all-to-all(f32[32,40,128]{2,1,0:T(8,128)} %get-tuple-element.13), channel_id=1, replica_groups=mesh['z'=8,'c'=2,'t'=16] {'c','t'}, dimensions={0} | all-to-all | bytes 1310720 | tf_op jit(solution)/shard_map/all_to_all | solution.py:253
  304.2 7.0 %sketch_and_hours.9 = f32[32,40,128]{2,1,0:T(8,128)S(1)} custom-call(f32[32,40,128]{2,1,0:T(8,128)S(1)} %all_to_all.110.h_ref, bf16[16,1024,256]{2,1,0:T(8,128)(2,1)} %all_to_all.101.a_ref), custom_call_target="tpu_custom_call" | custom-call | tf_op jit(solution)/shard_map/sketch_and_hours/pallas_call | solution.py:129
  311.2 17.0 %all_to_all.111.in_ref = f32[32,40,128]{2,1,0:T(8,128)} all-to-all(f32[32,40,128]{2,1,0:T(8,128)S(1)} %sketch_and_hours.9), channel_id=1, replica_groups=mesh['z'=8,'c'=2,'t'=16] {'c','t'}, dimensions={0} | all-to-all | bytes 1310720 | tf_op jit(solution)/shard_map/all_to_all | solution.py:249
  330.0 13.1 %all_to_all.112.in_ref = f32[8,40,128]{2,1,0:T(8,128)} all-to-all(f32[8,40,128]{2,1,0:T(8,128)} %sum_parts.9), channel_id=1, replica_groups=mesh['z'=8,'c'=2,'t'=16] {'z'}, dimensions={0} | all-to-all | bytes 327680 | tf_op jit(solution)/shard_map/all_to_all | solution.py:251
  343.1 3.0 row_factor.9
  346.1 18.0 %all_to_all.113.h_ref = f32[32,40,128]{2,1,0:T(8,128)S(1)} all-to-all(f32[32,40,128]{2,1,0:T(8,128)} %get-tuple-element.14), channel_id=1, replica_groups=mesh['z'=8,'c'=2,'t'=16] {'c','t'}, dimensions={0} | all-to-all | bytes 1310720 | tf_op jit(solution)/shard_map/all_to_all | solution.py:253
  364.1 7.0 %sketch_and_hours.10 = f32[32,40,128]{2,1,0:T(8,128)S(1)} custom-call(f32[32,40,128]{2,1,0:T(8,128)S(1)} %all_to_all.113.h_ref, bf16[16,1024,256]{2,1,0:T(8,128)(2,1)} %all_to_all.101.a_ref), custom_call_target="tpu_custom_call" | custom-call | tf_op jit(solution)/shard_map/sketch_and_hours/pallas_call | solution.py:129
  371.1 17.0 %all_to_all.114.in_ref = f32[32,40,128]{2,1,0:T(8,128)} all-to-all(f32[32,40,128]{2,1,0:T(8,128)S(1)} %sketch_and_hours.10), channel_id=1, replica_groups=mesh['z'=8,'c'=2,'t'=16] {'c','t'}, dimensions={0} | all-to-all | bytes 1310720 | tf_op jit(solution)/shard_map/all_to_all | solution.py:249
  389.9 13.1 %all_to_all.115.in_ref = f32[8,40,128]{2,1,0:T(8,128)} all-to-all(f32[8,40,128]{2,1,0:T(8,128)} %sum_parts.10), channel_id=1, replica_groups=mesh['z'=8,'c'=2,'t'=16] {'z'}, dimensions={0} | all-to-all | bytes 327680 | tf_op jit(solution)/shard_map/all_to_all | solution.py:251
  403.0 3.0 row_factor.10
  406.0 18.0 %all_to_all.116.h_ref = f32[32,40,128]{2,1,0:T(8,128)S(1)} all-to-all(f32[32,40,128]{2,1,0:T(8,128)} %get-tuple-element.15), channel_id=1, replica_groups=mesh['z'=8,'c'=2,'t'=16] {'c','t'}, dimensions={0} | all-to-all | bytes 1310720 | tf_op jit(solution)/shard_map/all_to_all | solution.py:253
  424.0 7.0 %sketch_and_hours.11 = (f32[32,40,128]{2,1,0:T(8,128)S(1)}, bf16[32,1024]{1,0:T(8,128)(2,1)}) custom-call(f32[32,40,128]{2,1,0:T(8,128)S(1)} %all_to_all.116.h_ref, bf16[16,1024,256]{2,1,0:T(8,128)(2,1)} %all_to_all.101.a_ref), custom_call_target="tpu_custom_call" | custom-call | tf_op jit(solution)/shard_map/sketch_and_hours/pallas_call | solution.py:129
  431.0 17.7 %all_to_all.117.in_ref = f32[32,40,128]{2,1,0:T(8,128)} all-to-all(f32[32,40,128]{2,1,0:T(8,128)S(1)} %get-tuple-element.16), channel_id=1, replica_groups=mesh['z'=8,'c'=2,'t'=16] {'c','t'}, dimensions={0} | all-to-all | bytes 1310720 | tf_op jit(solution)/shard_map/all_to_all | solution.py:249
  450.5 13.1 %all_to_all.118.in_ref = f32[8,40,128]{2,1,0:T(8,128)} all-to-all(f32[8,40,128]{2,1,0:T(8,128)} %sum_parts.11), channel_id=1, replica_groups=mesh['z'=8,'c'=2,'t'=16] {'z'}, dimensions={0} | all-to-all | bytes 327680 | tf_op jit(solution)/shard_map/all_to_all | solution.py:251
  463.5 3.0 row_factor.11
  466.6 8.0 %all-to-all-start.19 = ((f32[32,40,128]{2,1,0:T(8,128)}), f32[32,40,128]{2,1,0:T(8,128)S(1)}, u32[]{:S(2)}, u32[]{:S(2)}) async-start(f32[32,40,128]{2,1,0:T(8,128)} %get-tuple-element.19), calls=%async_computation.19 | async-start | bytes 1310720 | tf_op jit(solution)/shard_map/all_to_all | solution.py:253
  474.6 10.0 %all-to-all-done.19.h_ref = f32[32,40,128]{2,1,0:T(8,128)S(1)} async-done(((f32[32,40,128]{2,1,0:T(8,128)}), f32[32,40,128]{2,1,0:T(8,128)S(1)}, u32[]{:S(2)}, u32[]{:S(2)}) %all-to-all-start.19) | async-done | bytes 655392 | tf_op jit(solution)/shard_map/all_to_all | solution.py:253
  488.2 10.1 %row_basis.1 = f32[32,16384]{1,0:T(8,128)} custom-call(f32[32,32]{1,0:T(8,128)} %get-tuple-element.17.l_ref, bf16[16,32,1024]{2,1,0:T(8,128)(2,1)} %bitcast.9), custom_call_target="tpu_custom_call" | custom-call | flops 100663296 | bytes 3145728 | tf_op jit(solution)/shard_map/row_basis/pallas_call | solution.py:217
  (16 shorter events, 21.3 us)
Async XLA Ops:
  7.2 481.0 %all-gather.3.cloned.1.call-start = ((), (), s32[]{:S(2)}) async-start(), calls=%async_computation.20 | async-start | bytes 1114112 | tf_op jit(solution)/shard_map/all_gather | solution.py:248
  466.6 18.0 %all-to-all-start.19 = ((f32[32,40,128]{2,1,0:T(8,128)}), f32[32,40,128]{2,1,0:T(8,128)S(1)}, u32[]{:S(2)}, u32[]{:S(2)}) async-start(f32[32,40,128]{2,1,0:T(8,128)} %get-tuple-element.19), calls=%async_computation.19 | async-start | bytes 1310720 | tf_op jit(solution)/shard_map/all_to_all | solution.py:253
  484.6 0.8 copy-start
Sparse Core Ops, SparseCore 0:
  431.1 40.4 all-gather.2

commit v2 on v1

v2 whole, which is shorter than its diff:
```python
import jax
import jax.numpy as jnp
from jax import lax
from jax.experimental import pallas as pl
from jax.experimental.pallas import tpu as pltpu
from jax.sharding import Mesh, PartitionSpec as P

ITERS = 6
RANK = 32
LANES = 128
EXTRA = RANK * RANK // LANES
ROWS = RANK + EXTRA
F32 = jnp.float32
BF16 = jnp.bfloat16
HIGH = lax.Precision.HIGHEST
NT = (((1,), (1,)), ((), ()))
TN = (((0,), (0,)), ((), ()))


def split_bf16(value):
    high = value.astype(BF16)
    low = (value - high.astype(F32)).astype(BF16)
    return jnp.concatenate([high, low], axis=0)


def pack(wide):
    lane = lax.broadcasted_iota(jnp.int32, (EXTRA, LANES), 1) // RANK
    out = wide[0:EXTRA]
    for b in range(1, LANES // RANK):
        out = jnp.where(lane == b, wide[b * EXTRA : (b + 1) * EXTRA], out)
    return out


def packed_gram(block):
    tiled = jnp.concatenate([block] * (LANES // RANK), axis=0)
    return pack(lax.dot_general(block, tiled, NT, precision=HIGH, preferred_element_type=F32))


def inverse_factor(packed, upper):
    parts = RANK // EXTRA
    shape = (EXTRA, LANES)
    lane = lax.broadcasted_iota(jnp.int32, shape, 1)
    sub = lax.broadcasted_iota(jnp.int32, shape, 0)
    work = []
    for b in range(parts):
        shift = (RANK - b * RANK) % LANES
        gram = pltpu.roll(packed, shift, 1) if shift else packed
        gram = jnp.where(lane < 2 * RANK, gram, 0.0)
        work.append(jnp.where(lane < RANK, (lane == sub + b * EXTRA).astype(F32), gram))
    scale = []
    places = range(EXTRA - 1, -1, -1) if upper else range(EXTRA)
    for block in range(parts - 1, -1, -1) if upper else range(parts):
        beyond = range(block) if upper else range(block + 1, parts)
        cols = {
            b: [jnp.broadcast_to(work[b][:, c : c + 1], shape) for c in [RANK + block * EXTRA + r for r in places]]
            for b in (block, *beyond)
        }
        rows = [jnp.broadcast_to(work[block][r : r + 1, :], shape) for r in places]
        pivots = [[jnp.broadcast_to(col[r : r + 1, :], shape) for col in cols[block]] for r in places]
        scaled = []
        final = work[block]
        diagonal = pivots[0][0]
        for i, r in enumerate(places):
            inverse = 1.0 / pivots[i][i]
            for j in range(i + 1, EXTRA):
                factor = pivots[i][j] * inverse
                for k in range(j, EXTRA):
                    pivots[j][k] = pivots[j][k] - factor * pivots[i][k]
                rows[j] = rows[j] - factor * rows[i]
                for b in beyond:
                    cols[b][j] = cols[b][j] - factor * cols[b][i]
            scaled.append(rows[i] * inverse)
            final = jnp.where(sub == r, rows[i], final)
            diagonal = jnp.where(sub == r, pivots[i][i], diagonal)
        work[block] = final
        scale.append((block, diagonal))
        for b in beyond:
            for i in range(EXTRA):
                work[b] = work[b] - cols[b][i] * scaled[i]
    rows = [work[b] / jnp.sqrt(diagonal) for b, diagonal in sorted(scale, key=lambda item: item[0])]
    return jnp.concatenate(rows, axis=0)[:, :RANK]


def append_basis(a, basis):
    blocks, depth, width = a.shape

    def kernel(a_ref, basis_ref, out_ref, held, in_sems, out_sems):
        def load(t):
            return pltpu.make_async_copy(a_ref.at[t], held.at[t, 0:depth, :], in_sems.at[t])

        def store(t):
            return pltpu.make_async_copy(held.at[t], out_ref.at[t], out_sems.at[t])

        for t in range(blocks):
            load(t).start()
        for t in range(blocks):
            held[t, depth : depth + RANK, :] = basis_ref[...]
            load(t).wait()
            store(t).start()
        for t in range(blocks):
            store(t).wait()

    return pl.pallas_call(
        kernel,
        out_shape=jax.ShapeDtypeStruct((blocks, depth + RANK, width), BF16),
        in_specs=[pl.BlockSpec(memory_space=pl.ANY), pl.BlockSpec(memory_space=pltpu.VMEM)],
        out_specs=pl.BlockSpec(memory_space=pl.ANY),
        scratch_shapes=[
            pltpu.VMEM((blocks, depth + RANK, width), BF16),
            pltpu.SemaphoreType.DMA((blocks,)),
            pltpu.SemaphoreType.DMA((blocks,)),
        ],
        compiler_params=pltpu.CompilerParams(vmem_limit_bytes=52 * 1024 * 1024),
        name="append_basis",
    )(a, basis)


def main_step(hours, first, keep, h, a):
    blocks, depth, width = a.shape
    depth -= RANK

    def kernel(*refs):
        h_ref, a_ref, out_ref, *refs = ([None] if first else []) + list(refs)
        s_ref = refs[0] if keep else None
        a_vmem, acc, sems = refs[-3:]
        length = a_vmem.shape[1]

        def copy(t):
            return pltpu.make_async_copy(a_ref.at[t, 0:length, :], a_vmem.at[t], sems.at[t])

        for t in range(blocks):
            copy(t).start()
        if not first:
            parts = [jnp.concatenate([h_ref[t], h_ref[blocks + t]], axis=1) for t in range(blocks)]
        for t in range(blocks):
            copy(t).wait()
            part = a_vmem[t, depth : depth + RANK, :] if first else parts[t]
            term = lax.dot_general(part, a_vmem[t, 0:depth, :], NT, preferred_element_type=F32)
            if t == 0:
                acc[...] = term
            else:
                acc[...] += term
        sketch = acc[...]
        if not first:
            whole = jnp.concatenate(parts, axis=1)
            tiled = jnp.concatenate([whole] * (LANES // RANK), axis=0)
            gram = pack(lax.dot_general(whole, tiled, NT, preferred_element_type=F32))
            v_inv = inverse_factor(gram, True) * float(hours) ** 0.5
            sketch = jnp.dot(v_inv, sketch, precision=HIGH, preferred_element_type=F32)
        if keep:
            s_ref[...] = sketch.astype(BF16)
        gram = packed_gram(sketch)
        left = split_bf16(sketch)
        for t in range(blocks):
            both = jnp.dot(left, a_vmem[t, 0:depth, :], preferred_element_type=F32)
            part = both[0:RANK] + both[RANK : 2 * RANK]
            out_ref[t, 0:RANK, :] = part[:, 0:LANES]
            out_ref[blocks + t, 0:RANK, :] = part[:, LANES : 2 * LANES]
            out_ref[t, RANK:ROWS, :] = gram
            out_ref[blocks + t, RANK:ROWS, :] = gram

    operands = (a,) if first else (h, a)
    out_shape = [jax.ShapeDtypeStruct((2 * blocks, ROWS, LANES), F32)]
    if keep:
        out_shape.append(jax.ShapeDtypeStruct((RANK, depth), BF16))
    return pl.pallas_call(
        kernel,
        out_shape=out_shape,
        in_specs=[pl.BlockSpec(memory_space=pltpu.VMEM)] * len(operands[1:]) + [pl.BlockSpec(memory_space=pl.ANY)],
        out_specs=[pl.BlockSpec(memory_space=pltpu.VMEM)] * len(out_shape),
        scratch_shapes=[
            pltpu.VMEM((blocks, depth + (RANK if first else 0), width), BF16),
            pltpu.VMEM((RANK, depth), F32),
            pltpu.SemaphoreType.DMA((blocks,)),
        ],
        compiler_params=pltpu.CompilerParams(vmem_limit_bytes=52 * 1024 * 1024),
        name="sketch_and_hours",
    )(*operands)


def sum_step(parts, copies):
    def kernel(in_ref, out_ref):
        total = in_ref[0]
        for k in range(1, parts.shape[0]):
            total = total + in_ref[k]
        for k in range(copies):
            out_ref[k] = total

    return pl.pallas_call(
        kernel,
        out_shape=jax.ShapeDtypeStruct((copies,) + parts.shape[1:], F32),
        in_specs=[pl.BlockSpec(memory_space=pltpu.VMEM)],
        out_specs=pl.BlockSpec(memory_space=pltpu.VMEM),
        name="sum_parts",
    )(parts)


def hour_step(parts, copies, points, last):
    def kernel(in_ref, *outs):
        total = in_ref[0]
        for k in range(1, parts.shape[0]):
            total = total + in_ref[k]
        l_inv = inverse_factor(total[RANK:ROWS], False) * float(points) ** 0.5
        hours = jnp.dot(l_inv, total[0:RANK], precision=HIGH, preferred_element_type=F32)
        hours = lax.dot_general(l_inv, hours, TN, precision=HIGH, preferred_element_type=F32)
        if last:
            gram = packed_gram(hours)
            for k in range(copies):
                outs[0][k] = gram
            outs[1][...] = hours
            outs[2][...] = l_inv
        else:
            rounded = hours.astype(BF16)
            for k in range(copies):
                outs[0][k] = rounded

    out_shape = [jax.ShapeDtypeStruct((copies, RANK, LANES), BF16)]
    if last:
        out_shape = [
            jax.ShapeDtypeStruct((copies, EXTRA, LANES), F32),
            jax.ShapeDtypeStruct((RANK, LANES), F32),
            jax.ShapeDtypeStruct((RANK, RANK), F32),
        ]
    return pl.pallas_call(
        kernel,
        out_shape=out_shape,
        in_specs=[pl.BlockSpec(memory_space=pltpu.VMEM)],
        out_specs=[pl.BlockSpec(memory_space=pltpu.VMEM)] * len(out_shape),
        name="row_factor",
    )(parts)


def column_step(grams, mine, other, core, hours):
    def kernel(core_ref, gram_ref, mine_ref, other_ref, out_ref):
        total = gram_ref[0]
        for k in range(1, grams.shape[0]):
            total = total + gram_ref[k]
        v_inv = inverse_factor(total, True) * float(hours) ** 0.5
        first = core_ref[0] == 0
        low = jnp.where(first, mine_ref[...], other_ref[...])
        high = jnp.where(first, other_ref[...], mine_ref[...])
        block = jnp.concatenate([low, high], axis=1)
        out_ref[...] = jnp.dot(v_inv, block, precision=HIGH, preferred_element_type=F32)

    return pl.pallas_call(
        kernel,
        out_shape=jax.ShapeDtypeStruct((RANK, 2 * LANES), F32),
        in_specs=[pl.BlockSpec(memory_space=pltpu.SMEM)] + [pl.BlockSpec(memory_space=pltpu.VMEM)] * 3,
        out_specs=pl.BlockSpec(memory_space=pltpu.VMEM),
        name="column_factor",
    )(core, grams, mine, other)


def row_step(l_inv, sketch):
    blocks, _, depth = sketch.shape
    group = 4

    def kernel(l_ref, s_ref, out_ref):
        value = l_ref[...]
        pieces = []
        for _ in range(3):
            piece = value.astype(BF16)
            pieces.append(piece)
            value = value - piece.astype(F32)
        left = jnp.concatenate(pieces, axis=0)
        for k in range(group):
            out = jnp.dot(left, s_ref[k], preferred_element_type=F32)
            out = out[0:RANK] + out[RANK : 2 * RANK] + out[2 * RANK : 3 * RANK]
            out_ref[:, k * depth : (k + 1) * depth] = out

    return pl.pallas_call(
        kernel,
        grid=(blocks // group,),
        out_shape=jax.ShapeDtypeStruct((RANK, blocks * depth), F32),
        in_specs=[
            pl.BlockSpec((RANK, RANK), lambda i: (0, 0)),
            pl.BlockSpec((group, RANK, depth), lambda i: (i, 0, 0)),
        ],
        out_specs=pl.BlockSpec((RANK, group * depth), lambda i: (0, i)),
        cost_estimate=pl.CostEstimate(
            flops=6 * RANK * RANK * blocks * depth, bytes_accessed=6 * RANK * blocks * depth, transcendentals=0
        ),
        name="row_basis",
    )(l_inv, sketch)


def ring(size, shift):
    return [(i, (i + shift) % size) for i in range(size)]


def solution(mesh):
    grid_size, tm_size = mesh.devices.shape
    fine = Mesh(mesh.devices.reshape(grid_size // 2, 2, tm_size), ("z", "c", "t"))

    def shards(anomaly, start_basis):
        points = anomaly.shape[0] * grid_size
        hours = anomaly.shape[1] * tm_size
        depth = anomaly.shape[0] // tm_size
        core = lax.axis_index("c").reshape(1).astype(jnp.int32)
        a = append_basis(anomaly.reshape(tm_size, depth, anomaly.shape[1]), start_basis)
        a = lax.all_to_all(a, "t", 0, 0)
        for step in range(ITERS):
            last = step == ITERS - 1
            out = main_step(hours, step == 0, last, a if step == 0 else h, a)
            if last:
                rows = lax.all_gather(out[1], "t", axis=0)
            part = lax.all_to_all(out[0], ("c", "t"), 0, 0)
            part = sum_step(part, grid_size // 2)
            part = lax.all_to_all(part, "z", 0, 0)
            out = hour_step(part, 2 * tm_size, points, last)
            h = lax.all_to_all(out[0], ("c", "t"), 0, 0)
        mine = out[1]
        other = lax.ppermute(mine, "c", ring(2, 1))
        return row_step(out[2], rows), column_step(h, mine, other, core, hours)

    return jax.shard_map(
        shards,
        mesh=fine,
        in_specs=(P(("z", "c"), "t"), P(None, "t")),
        out_specs=(P(None, ("z", "c")), P(None, "t")),
        check_vma=False,
    )
```

time: 511 us -> 475 us (0.930)
  blocking collectives: 389 us -> 357 us
  waiting for transfers between devices: 9.97 us -> 4.12 us
    all_to_all x7 -> x6, blocking collectives: 201 us -> 171 us  [the longest x1 102 us: shards(): a = lax.all_to_all(a, 't', 0, 0)]
    all_to_all x1, waiting for transfers between devices: 9.95 us -> 3.05 us  [shards(): h = lax.all_to_all(out[0], ('c', 't'), 0, 0)]
    pallas_call x7 -> x8, Pallas kernels: 28.2 us -> 28 us  [the longest x6 17.2 us: hour_step(): pl.pallas_call(kernel, out_shape=out_shape, in_specs=[pl.BlockSpec(memory...]
  transfers between devices with their start and end apart: 2 -> 3, of which waited for: 1 -> 2; matrix products, arithmetic and copies ran while one was open for 0% -> 0% of each run, Pallas kernels for 2% -> 2%
where the time goes in v2:
time: 475 us; the launch traced here: 469 us
  blocking collectives  357 us (75%)
  Pallas kernels  83.7 us (18%)
  between operations  14.1 us (3%)
  starting transfers between devices  8.54 us (2%)
    all_to_all x6, blocking collectives, shards(): part = lax.all_to_all(out[0], ('c', 't'), 0, 0)  104 us
    all_to_all x1, blocking collectives, shards(): a = lax.all_to_all(a, 't', 0, 0)  102 us
    all_to_all x6, blocking collectives, shards(): part = lax.all_to_all(part, 'z', 0, 0)  82.2 us
    all_to_all x5, blocking collectives, shards(): h = lax.all_to_all(out[0], ('c', 't'), 0, 0)  69.2 us
    pallas_call x6, Pallas kernels, main_step(): pl.pallas_call(kernel, out_shape=out_shape, in_specs=[pl.BlockSpec(memory...  42.1 us
    pallas_call x6, Pallas kernels, hour_step(): pl.pallas_call(kernel, out_shape=out_shape, in_specs=[pl.BlockSpec(memory...  17.2 us
    pallas_call x6, Pallas kernels, sum_step(): pl.pallas_call(kernel, out_shape=jax.ShapeDtypeStruct((copies,) + parts.s...  10.8 us
  transfers between devices with their start and end apart: 3, of which 2 were waited for; matrix products, arithmetic and copies ran while one was open for 0% of the time, Pallas kernels for 2%

profile of v2, /device:TPU:13, one launch (start us, length us, event | category | flops | bytes accessed | tf_op | source)
XLA Modules:
  0.0 469.3 jit_solution(16861913033340539123)
XLA Ops:
  7.9 6.6 %append_basis.1 = bf16[16,1056,256]{2,1,0:T(8,128)(2,1)} custom-call(bf16[16,1024,256]{2,1,0:T(8,128)(2,1)} %bitcast.3, bf16[32,256]{1,0:T(8,128)(2,1)S(1)} %copy-done), custom_call_target="tpu_custom_call" | custom-call | tf_op jit(solution)/shard_map/append_basis/pallas_call | solution.py:103
  14.5 101.6 %all_to_all.95.refs_0_.refs_1_ = bf16[16,1056,256]{2,1,0:T(8,128)(2,1)} all-to-all(bf16[16,1056,256]{2,1,0:T(8,128)(2,1)} %append_basis.1), channel_id=1, replica_groups=mesh['z'=8,'c'=2,'t'=16] {'t'}, dimensions={0} | all-to-all | bytes 17301504 | tf_op jit(solution)/shard_map/all_to_all | solution.py:301
  116.1 5.9 %sketch_and_hours.6 = f32[32,40,128]{2,1,0:T(8,128)S(1)} custom-call(bf16[16,1056,256]{2,1,0:T(8,128)(2,1)} %all_to_all.95.refs_0_.refs_1_), custom_call_target="tpu_custom_call" | custom-call | tf_op jit(solution)/shard_map/sketch_and_hours/pallas_call | solution.py:166
  122.0 18.3 %all_to_all.96.in_ref = f32[32,40,128]{2,1,0:T(8,128)} all-to-all(f32[32,40,128]{2,1,0:T(8,128)S(1)} %sketch_and_hours.6), channel_id=1, replica_groups=mesh['z'=8,'c'=2,'t'=16] {'c','t'}, dimensions={0} | all-to-all | bytes 1310720 | tf_op jit(solution)/shard_map/all_to_all | solution.py:307
  142.1 16.9 %all_to_all.97.in_ref = f32[8,40,128]{2,1,0:T(8,128)} all-to-all(f32[8,40,128]{2,1,0:T(8,128)} %sum_parts.6), channel_id=1, replica_groups=mesh['z'=8,'c'=2,'t'=16] {'z'}, dimensions={0} | all-to-all | bytes 327680 | tf_op jit(solution)/shard_map/all_to_all | solution.py:309
  158.9 2.8 row_factor.6
  161.8 14.2 %all_to_all.98.refs_0_ = bf16[32,32,128]{2,1,0:T(8,128)(2,1)S(1)} all-to-all(bf16[32,32,128]{2,1,0:T(8,128)(2,1)} %row_factor.6), channel_id=1, replica_groups=mesh['z'=8,'c'=2,'t'=16] {'c','t'}, dimensions={0} | all-to-all | bytes 524288 | tf_op jit(solution)/shard_map/all_to_all | solution.py:311
  176.0 7.3 %sketch_and_hours.7 = f32[32,40,128]{2,1,0:T(8,128)S(1)} custom-call(bf16[32,32,128]{2,1,0:T(8,128)(2,1)S(1)} %all_to_all.98.refs_0_, bf16[16,1056,256]{2,1,0:T(8,128)(2,1)} %all_to_all.95.refs_0_.refs_1_), custom_call_target="tpu_custom_call" | custom-call | tf_op jit(solution)/shard_map/sketch_and_hours/pallas_call | solution.py:166
  183.3 17.1 %all_to_all.99.in_ref = f32[32,40,128]{2,1,0:T(8,128)} all-to-all(f32[32,40,128]{2,1,0:T(8,128)S(1)} %sketch_and_hours.7), channel_id=1, replica_groups=mesh['z'=8,'c'=2,'t'=16] {'c','t'}, dimensions={0} | all-to-all | bytes 1310720 | tf_op jit(solution)/shard_map/all_to_all | solution.py:307
  202.2 13.1 %all_to_all.100.in_ref = f32[8,40,128]{2,1,0:T(8,128)} all-to-all(f32[8,40,128]{2,1,0:T(8,128)} %sum_parts.7), channel_id=1, replica_groups=mesh['z'=8,'c'=2,'t'=16] {'z'}, dimensions={0} | all-to-all | bytes 327680 | tf_op jit(solution)/shard_map/all_to_all | solution.py:309
  218.1 13.7 %all_to_all.101.refs_0_ = bf16[32,32,128]{2,1,0:T(8,128)(2,1)S(1)} all-to-all(bf16[32,32,128]{2,1,0:T(8,128)(2,1)} %row_factor.7), channel_id=1, replica_groups=mesh['z'=8,'c'=2,'t'=16] {'c','t'}, dimensions={0} | all-to-all | bytes 524288 | tf_op jit(solution)/shard_map/all_to_all | solution.py:311
  231.9 7.3 %sketch_and_hours.8 = f32[32,40,128]{2,1,0:T(8,128)S(1)} custom-call(bf16[32,32,128]{2,1,0:T(8,128)(2,1)S(1)} %all_to_all.101.refs_0_, bf16[16,1056,256]{2,1,0:T(8,128)(2,1)} %all_to_all.95.refs_0_.refs_1_), custom_call_target="tpu_custom_call" | custom-call | tf_op jit(solution)/shard_map/sketch_and_hours/pallas_call | solution.py:166
  239.1 17.1 %all_to_all.102.in_ref = f32[32,40,128]{2,1,0:T(8,128)} all-to-all(f32[32,40,128]{2,1,0:T(8,128)S(1)} %sketch_and_hours.8), channel_id=1, replica_groups=mesh['z'=8,'c'=2,'t'=16] {'c','t'}, dimensions={0} | all-to-all | bytes 1310720 | tf_op jit(solution)/shard_map/all_to_all | solution.py:307
  258.0 13.1 %all_to_all.103.in_ref = f32[8,40,128]{2,1,0:T(8,128)} all-to-all(f32[8,40,128]{2,1,0:T(8,128)} %sum_parts.8), channel_id=1, replica_groups=mesh['z'=8,'c'=2,'t'=16] {'z'}, dimensions={0} | all-to-all | bytes 327680 | tf_op jit(solution)/shard_map/all_to_all | solution.py:309
  273.9 13.7 %all_to_all.104.refs_0_ = bf16[32,32,128]{2,1,0:T(8,128)(2,1)S(1)} all-to-all(bf16[32,32,128]{2,1,0:T(8,128)(2,1)} %row_factor.8), channel_id=1, replica_groups=mesh['z'=8,'c'=2,'t'=16] {'c','t'}, dimensions={0} | all-to-all | bytes 524288 | tf_op jit(solution)/shard_map/all_to_all | solution.py:311
  287.7 7.3 %sketch_and_hours.9 = f32[32,40,128]{2,1,0:T(8,128)S(1)} custom-call(bf16[32,32,128]{2,1,0:T(8,128)(2,1)S(1)} %all_to_all.104.refs_0_, bf16[16,1056,256]{2,1,0:T(8,128)(2,1)} %all_to_all.95.refs_0_.refs_1_), custom_call_target="tpu_custom_call" | custom-call | tf_op jit(solution)/shard_map/sketch_and_hours/pallas_call | solution.py:166
  294.9 17.1 %all_to_all.105.in_ref = f32[32,40,128]{2,1,0:T(8,128)} all-to-all(f32[32,40,128]{2,1,0:T(8,128)S(1)} %sketch_and_hours.9), channel_id=1, replica_groups=mesh['z'=8,'c'=2,'t'=16] {'c','t'}, dimensions={0} | all-to-all | bytes 1310720 | tf_op jit(solution)/shard_map/all_to_all | solution.py:307
  313.8 13.1 %all_to_all.106.in_ref = f32[8,40,128]{2,1,0:T(8,128)} all-to-all(f32[8,40,128]{2,1,0:T(8,128)} %sum_parts.9), channel_id=1, replica_groups=mesh['z'=8,'c'=2,'t'=16] {'z'}, dimensions={0} | all-to-all | bytes 327680 | tf_op jit(solution)/shard_map/all_to_all | solution.py:309
  326.9 2.8 row_factor.9
  329.8 13.7 %all_to_all.107.refs_0_ = bf16[32,32,128]{2,1,0:T(8,128)(2,1)S(1)} all-to-all(bf16[32,32,128]{2,1,0:T(8,128)(2,1)} %row_factor.9), channel_id=1, replica_groups=mesh['z'=8,'c'=2,'t'=16] {'c','t'}, dimensions={0} | all-to-all | bytes 524288 | tf_op jit(solution)/shard_map/all_to_all | solution.py:311
  343.5 7.3 %sketch_and_hours.10 = f32[32,40,128]{2,1,0:T(8,128)S(1)} custom-call(bf16[32,32,128]{2,1,0:T(8,128)(2,1)S(1)} %all_to_all.107.refs_0_, bf16[16,1056,256]{2,1,0:T(8,128)(2,1)} %all_to_all.95.refs_0_.refs_1_), custom_call_target="tpu_custom_call" | custom-call | tf_op jit(solution)/shard_map/sketch_and_hours/pallas_call | solution.py:166
  350.8 17.1 %all_to_all.108.in_ref = f32[32,40,128]{2,1,0:T(8,128)} all-to-all(f32[32,40,128]{2,1,0:T(8,128)S(1)} %sketch_and_hours.10), channel_id=1, replica_groups=mesh['z'=8,'c'=2,'t'=16] {'c','t'}, dimensions={0} | all-to-all | bytes 1310720 | tf_op jit(solution)/shard_map/all_to_all | solution.py:307
  369.7 13.1 %all_to_all.109.in_ref = f32[8,40,128]{2,1,0:T(8,128)} all-to-all(f32[8,40,128]{2,1,0:T(8,128)} %sum_parts.10), channel_id=1, replica_groups=mesh['z'=8,'c'=2,'t'=16] {'z'}, dimensions={0} | all-to-all | bytes 327680 | tf_op jit(solution)/shard_map/all_to_all | solution.py:309
  382.7 2.8 row_factor.10
  385.6 13.7 %all_to_all.110.refs_0_ = bf16[32,32,128]{2,1,0:T(8,128)(2,1)S(1)} all-to-all(bf16[32,32,128]{2,1,0:T(8,128)(2,1)} %row_factor.10), channel_id=1, replica_groups=mesh['z'=8,'c'=2,'t'=16] {'c','t'}, dimensions={0} | all-to-all | bytes 524288 | tf_op jit(solution)/shard_map/all_to_all | solution.py:311
  399.3 7.3 %sketch_and_hours.11 = (f32[32,40,128]{2,1,0:T(8,128)S(1)}, bf16[32,1024]{1,0:T(8,128)(2,1)}) custom-call(bf16[32,32,128]{2,1,0:T(8,128)(2,1)S(1)} %all_to_all.110.refs_0_, bf16[16,1056,256]{2,1,0:T(8,128)(2,1)} %all_to_all.95.refs_0_.refs_1_), custom_call_target="tpu_custom_call" | custom-call | tf_op jit(solution)/shard_map/sketch_and_hours/pallas_call | solution.py:166
  406.6 17.8 %all_to_all.111.in_ref = f32[32,40,128]{2,1,0:T(8,128)} all-to-all(f32[32,40,128]{2,1,0:T(8,128)S(1)} %get-tuple-element.7), channel_id=1, replica_groups=mesh['z'=8,'c'=2,'t'=16] {'c','t'}, dimensions={0} | all-to-all | bytes 1310720 | tf_op jit(solution)/shard_map/all_to_all | solution.py:307
  426.2 13.1 %all_to_all.112.in_ref = f32[8,40,128]{2,1,0:T(8,128)} all-to-all(f32[8,40,128]{2,1,0:T(8,128)} %sum_parts.11), channel_id=1, replica_groups=mesh['z'=8,'c'=2,'t'=16] {'z'}, dimensions={0} | all-to-all | bytes 327680 | tf_op jit(solution)/shard_map/all_to_all | solution.py:309
  439.3 3.0 row_factor.11
  442.3 8.1 %all-to-all-start.18 = ((f32[32,8,128]{2,1,0:T(8,128)}), f32[32,8,128]{2,1,0:T(8,128)S(1)}, u32[]{:S(2)}, u32[]{:S(2)}) async-start(f32[32,8,128]{2,1,0:T(8,128)} %get-tuple-element.10), calls=%async_computation.18 | async-start | bytes 262144 | tf_op jit(solution)/shard_map/all_to_all | solution.py:311
  451.9 3.0 all-to-all-done.18.gram_ref
  458.2 4.2 row_basis.1
  (20 shorter events, 22.1 us)
Async XLA Ops:
  7.2 451.0 %all-gather.3.cloned.1.call-start = ((), (), s32[]{:S(2)}) async-start(), calls=%async_computation.19 | async-start | bytes 1114112 | tf_op jit(solution)/shard_map/all_gather | solution.py:306
  7.2 0.7 copy-start
  442.3 12.6 %all-to-all-start.18 = ((f32[32,8,128]{2,1,0:T(8,128)}), f32[32,8,128]{2,1,0:T(8,128)S(1)}, u32[]{:S(2)}, u32[]{:S(2)}) async-start(f32[32,8,128]{2,1,0:T(8,128)} %get-tuple-element.10), calls=%async_computation.18 | async-start | bytes 262144 | tf_op jit(solution)/shard_map/all_to_all | solution.py:311
  450.4 1.5 collective-permute-start
  451.8 3.1 copy-start.2
  454.9 0.7 copy-start.1
Sparse Core Ops, SparseCore 0:
  406.7 40.6 all-gather.2

commit v3 on v2

--- a/solution.py
+++ b/solution.py
@@ -10,6 +10,8 @@
 LANES = 128
 EXTRA = RANK * RANK // LANES
 ROWS = RANK + EXTRA
+SMALL_BYTES = 4 * 1024 * 1024
+MID_BYTES = 20 * 1024 * 1024
 F32 = jnp.float32
 BF16 = jnp.bfloat16
 HIGH = lax.Precision.HIGHEST
@@ -84,98 +86,147 @@
 def append_basis(a, basis):
     blocks, depth, width = a.shape
 
-    def kernel(a_ref, basis_ref, out_ref, held, in_sems, out_sems):
+    def kernel(a_ref, basis_ref, out_ref, sems):
         def load(t):
-            return pltpu.make_async_copy(a_ref.at[t], held.at[t, 0:depth, :], in_sems.at[t])
-
-        def store(t):
-            return pltpu.make_async_copy(held.at[t], out_ref.at[t], out_sems.at[t])
+            return pltpu.make_async_copy(a_ref.at[t], out_ref.at[t, 0:depth, :], sems.at[t])
 
         for t in range(blocks):
             load(t).start()
         for t in range(blocks):
-            held[t, depth : depth + RANK, :] = basis_ref[...]
+            out_ref[t, depth : depth + RANK, :] = basis_ref[...]
+        for t in range(blocks):
             load(t).wait()
-            store(t).start()
-        for t in range(blocks):
-            store(t).wait()
 
     return pl.pallas_call(
         kernel,
         out_shape=jax.ShapeDtypeStruct((blocks, depth + RANK, width), BF16),
         in_specs=[pl.BlockSpec(memory_space=pl.ANY), pl.BlockSpec(memory_space=pltpu.VMEM)],
-        out_specs=pl.BlockSpec(memory_space=pl.ANY),
-        scratch_shapes=[
-            pltpu.VMEM((blocks, depth + RANK, width), BF16),
-            pltpu.SemaphoreType.DMA((blocks,)),
-            pltpu.SemaphoreType.DMA((blocks,)),
-        ],
-        compiler_params=pltpu.CompilerParams(vmem_limit_bytes=52 * 1024 * 1024),
+        out_specs=pl.BlockSpec(memory_space=pltpu.VMEM),
+        scratch_shapes=[pltpu.SemaphoreType.DMA((blocks,))],
+        compiler_params=pltpu.CompilerParams(vmem_limit_bytes=MID_BYTES),
         name="append_basis",
     )(a, basis)
 
 
-def main_step(hours, first, keep, h, a):
+def first_step(core, a):
     blocks, depth, width = a.shape
     depth -= RANK
-
-    def kernel(*refs):
-        h_ref, a_ref, out_ref, *refs = ([None] if first else []) + list(refs)
-        s_ref = refs[0] if keep else None
-        a_vmem, acc, sems = refs[-3:]
-        length = a_vmem.shape[1]
-
-        def copy(t):
-            return pltpu.make_async_copy(a_ref.at[t, 0:length, :], a_vmem.at[t], sems.at[t])
-
-        for t in range(blocks):
-            copy(t).start()
-        if not first:
-            parts = [jnp.concatenate([h_ref[t], h_ref[blocks + t]], axis=1) for t in range(blocks)]
-        for t in range(blocks):
-            copy(t).wait()
-            part = a_vmem[t, depth : depth + RANK, :] if first else parts[t]
-            term = lax.dot_general(part, a_vmem[t, 0:depth, :], NT, preferred_element_type=F32)
+    half = blocks // 2
+
+    def kernel(core_ref, a_ref, out_ref, send_ref, acc, send_sems):
+        def send(i):
+            t = (1 - core_ref[0]) * half + i
+            return pltpu.make_async_copy(a_ref.at[t, 0:depth, :], send_ref.at[i], send_sems.at[i])
+
+        for i in range(half):
+            send(i).start()
+        for t in range(blocks):
+            basis = a_ref[t, depth : depth + RANK, :]
+            term = lax.dot_general(basis, a_ref[t, 0:depth, :], NT, preferred_element_type=F32)
             if t == 0:
                 acc[...] = term
             else:
                 acc[...] += term
         sketch = acc[...]
-        if not first:
-            whole = jnp.concatenate(parts, axis=1)
-            tiled = jnp.concatenate([whole] * (LANES // RANK), axis=0)
-            gram = pack(lax.dot_general(whole, tiled, NT, preferred_element_type=F32))
-            v_inv = inverse_factor(gram, True) * float(hours) ** 0.5
-            sketch = jnp.dot(v_inv, sketch, precision=HIGH, preferred_element_type=F32)
-        if keep:
-            s_ref[...] = sketch.astype(BF16)
         gram = packed_gram(sketch)
         left = split_bf16(sketch)
         for t in range(blocks):
-            both = jnp.dot(left, a_vmem[t, 0:depth, :], preferred_element_type=F32)
-            part = both[0:RANK] + both[RANK : 2 * RANK]
-            out_ref[t, 0:RANK, :] = part[:, 0:LANES]
-            out_ref[blocks + t, 0:RANK, :] = part[:, LANES : 2 * LANES]
-            out_ref[t, RANK:ROWS, :] = gram
-            out_ref[blocks + t, RANK:ROWS, :] = gram
-
-    operands = (a,) if first else (h, a)
-    out_shape = [jax.ShapeDtypeStruct((2 * blocks, ROWS, LANES), F32)]
+            both = jnp.dot(left, a_ref[t, 0:depth, :], preferred_element_type=F32)
+            store_part(out_ref, t, both[0:RANK] + both[RANK : 2 * RANK], gram)
+        for i in range(half):
+            send(i).wait()
+
+    return pl.pallas_call(
+        kernel,
+        out_shape=[
+            jax.ShapeDtypeStruct((2 * blocks, ROWS, LANES), F32),
+            jax.ShapeDtypeStruct((half, depth, width), BF16),
+        ],
+        in_specs=[pl.BlockSpec(memory_space=pltpu.SMEM), pl.BlockSpec(memory_space=pltpu.VMEM)],
+        out_specs=[pl.BlockSpec(memory_space=pltpu.VMEM), pl.BlockSpec(memory_space=pl.ANY)],
+        scratch_shapes=[pltpu.VMEM((RANK, depth), F32), pltpu.SemaphoreType.DMA((half,))],
+        compiler_params=pltpu.CompilerParams(vmem_limit_bytes=MID_BYTES),
+        name="first_products",
+    )(core, a)
+
+
+def store_part(out_ref, block, part, gram):
+    for side in range(2):
+        out_ref[2 * block + side, 0:RANK, :] = part[:, side * LANES : (side + 1) * LANES]
+        out_ref[2 * block + side, RANK:ROWS, :] = gram
+
+
+def sketch_step(core, h, a, mate):
+    half, depth, width = mate.shape
+
+    def kernel(core_ref, h_ref, a_ref, mate_ref, out_ref):
+        parts = [jnp.concatenate([h_ref[2 * i], h_ref[2 * i + 1]], axis=1) for i in range(half)]
+        for side in range(2):
+            rows = slice(side * RANK, (side + 1) * RANK)
+            for i in range(half):
+                block = mate_ref[i] if side else a_ref[core_ref[0] * half + i, 0:depth, :]
+                term = lax.dot_general(parts[i], block, NT, preferred_element_type=F32)
+                if i == 0:
+                    out_ref[rows, :] = term
+                else:
+                    out_ref[rows, :] += term
+        whole = jnp.concatenate(parts, axis=1)
+        tiled = jnp.concatenate([whole] * (LANES // RANK), axis=0)
+        out_ref[2 * RANK :, :] = jnp.zeros((EXTRA, depth), F32)
+        out_ref[2 * RANK :, 0:LANES] = pack(lax.dot_general(whole, tiled, NT, preferred_element_type=F32))
+
+    return pl.pallas_call(
+        kernel,
+        out_shape=jax.ShapeDtypeStruct((2 * RANK + EXTRA, depth), F32),
+        in_specs=[
+            pl.BlockSpec(memory_space=pltpu.SMEM),
+            pl.BlockSpec(memory_space=pltpu.VMEM),
+            pl.BlockSpec(memory_space=pltpu.VMEM),
+            pl.BlockSpec(memory_space=pltpu.VMEM),
+        ],
+        out_specs=pl.BlockSpec(memory_space=pltpu.VMEM),
+        compiler_params=pltpu.CompilerParams(vmem_limit_bytes=MID_BYTES),
+        name="partial_sketch",
+    )(core, h, a, mate)
+
+
+def product_step(hours, keep, core, mine, other, a, mate):
+    half, depth, width = mate.shape
+
+    def kernel(core_ref, mine_ref, other_ref, a_ref, mate_ref, out_ref, *refs):
+        gram = mine_ref[2 * RANK :, 0:LANES] + other_ref[2 * RANK :, 0:LANES]
+        v_inv = inverse_factor(gram, True) * float(hours) ** 0.5
+        own = mine_ref[0:RANK, :] + other_ref[RANK : 2 * RANK, :]
+        own = jnp.dot(v_inv, own, precision=HIGH, preferred_element_type=F32)
+        if keep:
+            refs[0][...] = own.astype(BF16)
+        far = mine_ref[RANK : 2 * RANK, :] + other_ref[0:RANK, :]
+        far = jnp.dot(v_inv, far, precision=HIGH, preferred_element_type=F32)
+        gram = packed_gram(own) + packed_gram(far)
+        left = split_bf16(own)
+        right = split_bf16(far)
+        for i in range(half):
+            both = jnp.dot(left, a_ref[core_ref[0] * half + i, 0:depth, :], preferred_element_type=F32)
+            both = both + jnp.dot(right, mate_ref[i], preferred_element_type=F32)
+            store_part(out_ref, i, both[0:RANK] + both[RANK : 2 * RANK], gram)
+
+    out_shape = [jax.ShapeDtypeStruct((2 * half, ROWS, LANES), F32)]
     if keep:
         out_shape.append(jax.ShapeDtypeStruct((RANK, depth), BF16))
     return pl.pallas_call(
         kernel,
         out_shape=out_shape,
-        in_specs=[pl.BlockSpec(memory_space=pltpu.VMEM)] * len(operands[1:]) + [pl.BlockSpec(memory_space=pl.ANY)],
+        in_specs=[
+            pl.BlockSpec(memory_space=pltpu.SMEM),
+            pl.BlockSpec(memory_space=pltpu.VMEM),
+            pl.BlockSpec(memory_space=pltpu.VMEM),
+            pl.BlockSpec(memory_space=pltpu.VMEM),
+            pl.BlockSpec(memory_space=pltpu.VMEM),
+        ],
         out_specs=[pl.BlockSpec(memory_space=pltpu.VMEM)] * len(out_shape),
-        scratch_shapes=[
-            pltpu.VMEM((blocks, depth + (RANK if first else 0), width), BF16),
-            pltpu.VMEM((RANK, depth), F32),
-            pltpu.SemaphoreType.DMA((blocks,)),
-        ],
-        compiler_params=pltpu.CompilerParams(vmem_limit_bytes=52 * 1024 * 1024),
-        name="sketch_and_hours",
-    )(*operands)
+        compiler_params=pltpu.CompilerParams(vmem_limit_bytes=MID_BYTES),
+        name="hour_products",
+    )(core, mine, other, a, mate)
 
 
 def sum_step(parts, copies):
@@ -191,6 +242,7 @@
         out_shape=jax.ShapeDtypeStruct((copies,) + parts.shape[1:], F32),
         in_specs=[pl.BlockSpec(memory_space=pltpu.VMEM)],
         out_specs=pl.BlockSpec(memory_space=pltpu.VMEM),
+        compiler_params=pltpu.CompilerParams(vmem_limit_bytes=SMALL_BYTES),
         name="sum_parts",
     )(parts)
 
@@ -226,6 +278,7 @@
         out_shape=out_shape,
         in_specs=[pl.BlockSpec(memory_space=pltpu.VMEM)],
         out_specs=[pl.BlockSpec(memory_space=pltpu.VMEM)] * len(out_shape),
+        compiler_params=pltpu.CompilerParams(vmem_limit_bytes=SMALL_BYTES),
         name="row_factor",
     )(parts)
 
@@ -247,6 +300,7 @@
         out_shape=jax.ShapeDtypeStruct((RANK, 2 * LANES), F32),
         in_specs=[pl.BlockSpec(memory_space=pltpu.SMEM)] + [pl.BlockSpec(memory_space=pltpu.VMEM)] * 3,
         out_specs=pl.BlockSpec(memory_space=pltpu.VMEM),
+        compiler_params=pltpu.CompilerParams(vmem_limit_bytes=SMALL_BYTES),
         name="column_factor",
     )(core, grams, mine, other)
 
@@ -256,17 +310,10 @@
     group = 4
 
     def kernel(l_ref, s_ref, out_ref):
-        value = l_ref[...]
-        pieces = []
-        for _ in range(3):
-            piece = value.astype(BF16)
-            pieces.append(piece)
-            value = value - piece.astype(F32)
-        left = jnp.concatenate(pieces, axis=0)
+        left = split_bf16(l_ref[...])
         for k in range(group):
             out = jnp.dot(left, s_ref[k], preferred_element_type=F32)
-            out = out[0:RANK] + out[RANK : 2 * RANK] + out[2 * RANK : 3 * RANK]
-            out_ref[:, k * depth : (k + 1) * depth] = out
+            out_ref[:, k * depth : (k + 1) * depth] = out[0:RANK] + out[RANK : 2 * RANK]
 
     return pl.pallas_call(
         kernel,
@@ -280,6 +327,7 @@
         cost_estimate=pl.CostEstimate(
             flops=6 * RANK * RANK * blocks * depth, bytes_accessed=6 * RANK * blocks * depth, transcendentals=0
         ),
+        compiler_params=pltpu.CompilerParams(vmem_limit_bytes=SMALL_BYTES),
         name="row_basis",
     )(l_inv, sketch)
 
@@ -297,20 +345,29 @@
         hours = anomaly.shape[1] * tm_size
         depth = anomaly.shape[0] // tm_size
         core = lax.axis_index("c").reshape(1).astype(jnp.int32)
+        core, start_basis = lax.optimization_barrier((core, start_basis))
         a = append_basis(anomaly.reshape(tm_size, depth, anomaly.shape[1]), start_basis)
         a = lax.all_to_all(a, "t", 0, 0)
+        swap = ring(2, 1)
+        out, send = first_step(core, a)
+        mate = lax.ppermute(send, "c", swap)
+        part = lax.all_to_all(out, ("c", "t"), 0, 0)
         for step in range(ITERS):
             last = step == ITERS - 1
-            out = main_step(hours, step == 0, last, a if step == 0 else h, a)
-            if last:
-                rows = lax.all_gather(out[1], "t", axis=0)
-            part = lax.all_to_all(out[0], ("c", "t"), 0, 0)
+            if step:
+                sketch = sketch_step(core, h, a, mate)
+                other = lax.ppermute(sketch, "c", swap)
+                out = product_step(hours, last, core, sketch, other, a, mate)
+                if last:
+                    rows = lax.all_gather(out[1], "t", axis=0)
+                part = lax.all_to_all(out[0], "t", 0, 0)
             part = sum_step(part, grid_size // 2)
             part = lax.all_to_all(part, "z", 0, 0)
-            out = hour_step(part, 2 * tm_size, points, last)
-            h = lax.all_to_all(out[0], ("c", "t"), 0, 0)
-        mine = out[1]
-        other = lax.ppermute(mine, "c", ring(2, 1))
+            out = hour_step(part, (2 if last else 1) * tm_size, points, last)
+            h = lax.all_to_all(out[0], ("c", "t") if last else "t", 0, 0)
+        home = [(i, i % 2 * tm_size + i // 2) for i in range(2 * tm_size)]
+        mine = lax.ppermute(out[1], ("c", "t"), home)
+        other = lax.ppermute(mine, "c", swap)
         return row_step(out[2], rows), column_step(h, mine, other, core, hours)
 
     return jax.shard_map(

time: 475 us -> 412 us (0.87); the launches traced: 469 us -> 411 us
  blocking collectives: 357 us -> 294 us
  Pallas kernels: 83.7 us -> 50.2 us
  starting transfers between devices: 8.54 us -> 37.2 us
  waiting for transfers between devices: 4.12 us -> 10.5 us
    all_to_all x11, blocking collectives: 174 us -> 122 us  [the longest x5 56.3 us: shards(): part = lax.all_to_all(out[0], 't', 0, 0)]
    ppermute x1 -> x8, starting transfers between devices: 0.44 us -> 27.4 us  [the longest x5 19.3 us: shards(): other = lax.ppermute(sketch, 'c', swap)]
    all_to_all x6, blocking collectives: 82.2 us -> 70.3 us  [shards(): part = lax.all_to_all(part, 'z', 0, 0)]
    pallas_call x6, Pallas kernels: 10.8 us -> 0.19 us  [sum_step(): pl.pallas_call(kernel, out_shape=jax.ShapeDtypeStruct((copies,) + parts.s...]
    ppermute x1 -> x8, waiting for transfers between devices: 1.05 us -> 10.5 us  [the longest x5 6.04 us: shards(): other = lax.ppermute(sketch, 'c', swap)]
    pallas_call x6, Pallas kernels: 17.2 us -> 8.16 us  [hour_step(): pl.pallas_call(kernel, out_shape=out_shape, in_specs=[pl.BlockSpec(memory...]
    pallas_call x1, Pallas kernels: 6.58 us -> 0.75 us  [append_basis(): pl.pallas_call(kernel, out_shape=jax.ShapeDtypeStruct((blocks, depth + RA...]
    pallas_call x6 -> x11, Pallas kernels: 42.1 us -> 36.9 us  [the longest x5 18.7 us: product_step(): pl.pallas_call(kernel, out_shape=out_shape, in_specs=[pl.BlockSpec(memory...]
  transfers between devices with their start and end apart: 3 -> 10, of which waited for: 2 -> 7; matrix products, arithmetic and copies ran while one was open for 0% -> 0% of each run, Pallas kernels for 2% -> 1%
where the time goes in v3:
time: 412 us; the launch traced here: 411 us
  blocking collectives  294 us (71%)
  Pallas kernels  50.2 us (12%)
  starting transfers between devices  37.2 us (9%)
  between operations  14.2 us (3%)
  waiting for transfers between devices  10.5 us (3%)
  local copies, waits for them, and re-layouts  5.32 us (1%)
    all_to_all x1, blocking collectives, shards(): a = lax.all_to_all(a, 't', 0, 0)  101 us
    all_to_all x6, blocking collectives, shards(): part = lax.all_to_all(part, 'z', 0, 0)  70.3 us
    all_to_all x5, blocking collectives, shards(): part = lax.all_to_all(out[0], 't', 0, 0)  56.3 us
    all_to_all x5, blocking collectives, shards(): h = lax.all_to_all(out[0], ('c', 't') if last else 't', 0, 0)  49.9 us
    ppermute x5, starting transfers between devices, shards(): other = lax.ppermute(sketch, 'c', swap)  19.3 us
    pallas_call x5, Pallas kernels, product_step(): pl.pallas_call(kernel, out_shape=out_shape, in_specs=[pl.BlockSpec(memory...  18.7 us
    all_to_all x1, blocking collectives, shards(): part = lax.all_to_all(out, ('c', 't'), 0, 0)  16.2 us
    pallas_call x5, Pallas kernels, sketch_step(): pl.pallas_call(kernel, out_shape=jax.ShapeDtypeStruct((2 * RANK + EXTRA,...  13.4 us
  transfers between devices with their start and end apart: 10, of which 7 were waited for; matrix products, arithmetic and copies ran while one was open for 0% of the time, Pallas kernels for 1%

profile of v3, /device:TPU:13, one launch (start us, length us, event | category | flops | bytes accessed | tf_op | source)
XLA Modules:
  0.0 411.3 jit_solution(10094828277874659265)
XLA Ops:
  7.2 3.4 copy-done
  12.1 101.3 %all_to_all.95.a_ref = bf16[16,1056,256]{2,1,0:T(8,128)(2,1)S(1)} all-to-all(bf16[16,1056,256]{2,1,0:T(8,128)(2,1)S(1)} %append_basis.1), channel_id=1, replica_groups=mesh['z'=8,'c'=2,'t'=16] {'t'}, dimensions={0} | all-to-all | bytes 17301504 | tf_op jit(solution)/shard_map/all_to_all | solution.py:350
  113.4 4.9 %first_products.1 = (f32[32,40,128]{2,1,0:T(8,128)S(1)}, bf16[8,1024,256]{2,1,0:T(8,128)(2,1)S(1)}) custom-call(s32[1]{0:T(128)} %bitcast.core_ref, bf16[16,1056,256]{2,1,0:T(8,128)(2,1)S(1)} %all_to_all.95.a_ref), custom_call_target="tpu_custom_call" | custom-call | tf_op jit(solution)/shard_map/first_products/pallas_call | solution.py:139
  120.1 16.2 %all_to_all.96.in_ref = f32[32,40,128]{2,1,0:T(8,128)S(1)} all-to-all(f32[32,40,128]{2,1,0:T(8,128)S(1)} %get-tuple-element.13), channel_id=1, replica_groups=mesh['z'=8,'c'=2,'t'=16] {'c','t'}, dimensions={0} | all-to-all | bytes 1310720 | tf_op jit(solution)/shard_map/all_to_all | solution.py:354
  136.3 16.6 %all_to_all.97.in_ref = f32[8,40,128]{2,1,0:T(8,128)S(1)} all-to-all(f32[8,40,128]{2,1,0:T(8,128)S(1)} %sum_parts.6), channel_id=1, replica_groups=mesh['z'=8,'c'=2,'t'=16] {'z'}, dimensions={0} | all-to-all | bytes 327680 | tf_op jit(solution)/shard_map/all_to_all | solution.py:365
  154.1 10.6 %all_to_all.98.h_ref = bf16[16,32,128]{2,1,0:T(8,128)(2,1)S(1)} all-to-all(bf16[16,32,128]{2,1,0:T(8,128)(2,1)S(1)} %row_factor.6), channel_id=1, replica_groups=mesh['z'=8,'c'=2,'t'=16] {'t'}, dimensions={0} | all-to-all | bytes 262144 | tf_op jit(solution)/shard_map/all_to_all | solution.py:367
  171.4 3.7 hour_products.5
  175.1 11.2 %all_to_all.99.in_ref = f32[16,40,128]{2,1,0:T(8,128)S(1)} all-to-all(f32[16,40,128]{2,1,0:T(8,128)S(1)} %hour_products.5), channel_id=1, replica_groups=mesh['z'=8,'c'=2,'t'=16] {'t'}, dimensions={0} | all-to-all | bytes 655360 | tf_op jit(solution)/shard_map/all_to_all | solution.py:363
  186.4 10.8 %all_to_all.100.in_ref = f32[8,40,128]{2,1,0:T(8,128)S(1)} all-to-all(f32[8,40,128]{2,1,0:T(8,128)S(1)} %sum_parts.7), channel_id=1, replica_groups=mesh['z'=8,'c'=2,'t'=16] {'z'}, dimensions={0} | all-to-all | bytes 327680 | tf_op jit(solution)/shard_map/all_to_all | solution.py:365
  198.4 9.8 %all_to_all.101.h_ref = bf16[16,32,128]{2,1,0:T(8,128)(2,1)S(1)} all-to-all(bf16[16,32,128]{2,1,0:T(8,128)(2,1)S(1)} %row_factor.7), channel_id=1, replica_groups=mesh['z'=8,'c'=2,'t'=16] {'t'}, dimensions={0} | all-to-all | bytes 262144 | tf_op jit(solution)/shard_map/all_to_all | solution.py:367
  210.9 4.2 %collective-permute-start.2 = (f32[72,1024]{1,0:T(8,128)S(1)}, f32[72,1024]{1,0:T(8,128)S(1)}, u32[]{:S(2)}, u32[]{:S(2)}) collective-permute-start(f32[72,1024]{1,0:T(8,128)S(1)} %partial_sketch.6.mine_ref), channel_id=1, source_target_pairs={{0,16},{16,0},{1,17},{17,1},{2,18},{18,2},{3,19},{19,3},{4,20},{20... | collective-permute-start | bytes 884744 | tf_op jit(solution)/shard_map/ppermute | solution.py:359
  216.3 3.7 hour_products.6
  220.0 11.2 %all_to_all.102.in_ref = f32[16,40,128]{2,1,0:T(8,128)S(1)} all-to-all(f32[16,40,128]{2,1,0:T(8,128)S(1)} %hour_products.6), channel_id=1, replica_groups=mesh['z'=8,'c'=2,'t'=16] {'t'}, dimensions={0} | all-to-all | bytes 655360 | tf_op jit(solution)/shard_map/all_to_all | solution.py:363
  231.3 10.8 %all_to_all.103.in_ref = f32[8,40,128]{2,1,0:T(8,128)S(1)} all-to-all(f32[8,40,128]{2,1,0:T(8,128)S(1)} %sum_parts.8), channel_id=1, replica_groups=mesh['z'=8,'c'=2,'t'=16] {'z'}, dimensions={0} | all-to-all | bytes 327680 | tf_op jit(solution)/shard_map/all_to_all | solution.py:365
  243.3 9.8 %all_to_all.104.h_ref = bf16[16,32,128]{2,1,0:T(8,128)(2,1)S(1)} all-to-all(bf16[16,32,128]{2,1,0:T(8,128)(2,1)S(1)} %row_factor.8), channel_id=1, replica_groups=mesh['z'=8,'c'=2,'t'=16] {'t'}, dimensions={0} | all-to-all | bytes 262144 | tf_op jit(solution)/shard_map/all_to_all | solution.py:367
  255.8 4.0 collective-permute-start.3
  261.0 3.7 hour_products.7
  264.8 11.2 %all_to_all.105.in_ref = f32[16,40,128]{2,1,0:T(8,128)S(1)} all-to-all(f32[16,40,128]{2,1,0:T(8,128)S(1)} %hour_products.7), channel_id=1, replica_groups=mesh['z'=8,'c'=2,'t'=16] {'t'}, dimensions={0} | all-to-all | bytes 655360 | tf_op jit(solution)/shard_map/all_to_all | solution.py:363
  276.0 10.8 %all_to_all.106.in_ref = f32[8,40,128]{2,1,0:T(8,128)S(1)} all-to-all(f32[8,40,128]{2,1,0:T(8,128)S(1)} %sum_parts.9), channel_id=1, replica_groups=mesh['z'=8,'c'=2,'t'=16] {'z'}, dimensions={0} | all-to-all | bytes 327680 | tf_op jit(solution)/shard_map/all_to_all | solution.py:365
  288.0 9.8 %all_to_all.107.h_ref = bf16[16,32,128]{2,1,0:T(8,128)(2,1)S(1)} all-to-all(bf16[16,32,128]{2,1,0:T(8,128)(2,1)S(1)} %row_factor.9), channel_id=1, replica_groups=mesh['z'=8,'c'=2,'t'=16] {'t'}, dimensions={0} | all-to-all | bytes 262144 | tf_op jit(solution)/shard_map/all_to_all | solution.py:367
  300.5 4.2 %collective-permute-start.4 = (f32[72,1024]{1,0:T(8,128)S(1)}, f32[72,1024]{1,0:T(8,128)S(1)}, u32[]{:S(2)}, u32[]{:S(2)}) collective-permute-start(f32[72,1024]{1,0:T(8,128)S(1)} %partial_sketch.8.mine_ref), channel_id=1, source_target_pairs={{0,16},{16,0},{1,17},{17,1},{2,18},{18,2},{3,19},{19,3},{4,20},{20... | collective-permute-start | bytes 884744 | tf_op jit(solution)/shard_map/ppermute | solution.py:359
  306.0 3.7 hour_products.8
  309.7 11.2 %all_to_all.108.in_ref = f32[16,40,128]{2,1,0:T(8,128)S(1)} all-to-all(f32[16,40,128]{2,1,0:T(8,128)S(1)} %hour_products.8), channel_id=1, replica_groups=mesh['z'=8,'c'=2,'t'=16] {'t'}, dimensions={0} | all-to-all | bytes 655360 | tf_op jit(solution)/shard_map/all_to_all | solution.py:363
  321.0 10.8 %all_to_all.109.in_ref = f32[8,40,128]{2,1,0:T(8,128)S(1)} all-to-all(f32[8,40,128]{2,1,0:T(8,128)S(1)} %sum_parts.10), channel_id=1, replica_groups=mesh['z'=8,'c'=2,'t'=16] {'z'}, dimensions={0} | all-to-all | bytes 327680 | tf_op jit(solution)/shard_map/all_to_all | solution.py:365
  333.0 9.8 %all_to_all.110.h_ref = bf16[16,32,128]{2,1,0:T(8,128)(2,1)S(1)} all-to-all(bf16[16,32,128]{2,1,0:T(8,128)(2,1)S(1)} %row_factor.10), channel_id=1, replica_groups=mesh['z'=8,'c'=2,'t'=16] {'t'}, dimensions={0} | all-to-all | bytes 262144 | tf_op jit(solution)/shard_map/all_to_all | solution.py:367
  345.5 4.0 collective-permute-start.5
  350.7 3.7 hour_products.9
  354.5 11.3 %all_to_all.111.in_ref = f32[16,40,128]{2,1,0:T(8,128)S(1)} all-to-all(f32[16,40,128]{2,1,0:T(8,128)S(1)} %get-tuple-element.15), channel_id=1, replica_groups=mesh['z'=8,'c'=2,'t'=16] {'t'}, dimensions={0} | all-to-all | bytes 655360 | tf_op jit(solution)/shard_map/all_to_all | solution.py:363
  365.8 10.7 %all_to_all.112.in_ref = f32[8,40,128]{2,1,0:T(8,128)S(1)} all-to-all(f32[8,40,128]{2,1,0:T(8,128)S(1)} %sum_parts.11), channel_id=1, replica_groups=mesh['z'=8,'c'=2,'t'=16] {'z'}, dimensions={0} | all-to-all | bytes 327680 | tf_op jit(solution)/shard_map/all_to_all | solution.py:365
  378.6 9.8 %all-to-all-start.18 = ((f32[32,8,128]{2,1,0:T(8,128)}), f32[32,8,128]{2,1,0:T(8,128)S(1)}, u32[]{:S(2)}, u32[]{:S(2)}) async-start(f32[32,8,128]{2,1,0:T(8,128)} %get-tuple-element.18), calls=%async_computation.18 | async-start | bytes 262144 | tf_op jit(solution)/shard_map/all_to_all | solution.py:367
  388.4 3.9 collective-permute-start.6
  392.3 3.6 collective-permute-done.6.mine_ref
  (39 shorter events, 42.5 us)
Async XLA Ops:
  7.2 393.6 %all-gather.3.cloned.1.call-start = ((), (), s32[]{:S(2)}) async-start(), calls=%async_computation.19 | async-start | bytes 1114112 | tf_op jit(solution)/shard_map/all_gather | solution.py:362
  7.2 3.4 copy-start
  10.6 0.7 copy-start.2
  118.3 46.4 %collective-permute-start = (bf16[8,1024,256]{2,1,0:T(8,128)(2,1)S(1)}, bf16[8,1024,256]{2,1,0:T(8,128)(2,1)S(1)}, u32[]{:S(2)}, u32[]{:S(2)}) collective-permute-start(bf16[8,1024,256]{2,1,0:T(8,128)(2,1)S(1)} %get-tuple-element.14), channel_id=1, source_target_pairs={{0,16},{16,0},{1,17},{17,1},{2,18},{18,2},{3,19},{19,3},{4,20},{20... | collective-permute-start | bytes 12582920 | tf_op jit(solution)/shard_map/ppermute | solution.py:353
  167.3 4.1 collective-permute-start.1
  210.9 5.4 %collective-permute-start.2 = (f32[72,1024]{1,0:T(8,128)S(1)}, f32[72,1024]{1,0:T(8,128)S(1)}, u32[]{:S(2)}, u32[]{:S(2)}) collective-permute-start(f32[72,1024]{1,0:T(8,128)S(1)} %partial_sketch.6.mine_ref), channel_id=1, source_target_pairs={{0,16},{16,0},{1,17},{17,1},{2,18},{18,2},{3,19},{19,3},{4,20},{20... | collective-permute-start | bytes 884744 | tf_op jit(solution)/shard_map/ppermute | solution.py:359
  255.8 5.2 %collective-permute-start.3 = (f32[72,1024]{1,0:T(8,128)S(1)}, f32[72,1024]{1,0:T(8,128)S(1)}, u32[]{:S(2)}, u32[]{:S(2)}) collective-permute-start(f32[72,1024]{1,0:T(8,128)S(1)} %partial_sketch.7.mine_ref), channel_id=1, source_target_pairs={{0,16},{16,0},{1,17},{17,1},{2,18},{18,2},{3,19},{19,3},{4,20},{20... | collective-permute-start | bytes 884744 | tf_op jit(solution)/shard_map/ppermute | solution.py:359
  300.5 5.5 %collective-permute-start.4 = (f32[72,1024]{1,0:T(8,128)S(1)}, f32[72,1024]{1,0:T(8,128)S(1)}, u32[]{:S(2)}, u32[]{:S(2)}) collective-permute-start(f32[72,1024]{1,0:T(8,128)S(1)} %partial_sketch.8.mine_ref), channel_id=1, source_target_pairs={{0,16},{16,0},{1,17},{17,1},{2,18},{18,2},{3,19},{19,3},{4,20},{20... | collective-permute-start | bytes 884744 | tf_op jit(solution)/shard_map/ppermute | solution.py:359
  345.5 5.2 %collective-permute-start.5 = (f32[72,1024]{1,0:T(8,128)S(1)}, f32[72,1024]{1,0:T(8,128)S(1)}, u32[]{:S(2)}, u32[]{:S(2)}) collective-permute-start(f32[72,1024]{1,0:T(8,128)S(1)} %partial_sketch.9.mine_ref), channel_id=1, source_target_pairs={{0,16},{16,0},{1,17},{17,1},{2,18},{18,2},{3,19},{19,3},{4,20},{20... | collective-permute-start | bytes 884744 | tf_op jit(solution)/shard_map/ppermute | solution.py:359
  378.6 20.4 %all-to-all-start.18 = ((f32[32,8,128]{2,1,0:T(8,128)}), f32[32,8,128]{2,1,0:T(8,128)S(1)}, u32[]{:S(2)}, u32[]{:S(2)}) async-start(f32[32,8,128]{2,1,0:T(8,128)} %get-tuple-element.18), calls=%async_computation.18 | async-start | bytes 262144 | tf_op jit(solution)/shard_map/all_to_all | solution.py:367
  388.4 7.5 %collective-permute-start.6 = (f32[32,128]{1,0:T(8,128)S(1)}, f32[32,128]{1,0:T(8,128)S(1)}, u32[]{:S(2)}, u32[]{:S(2)}) collective-permute-start(f32[32,128]{1,0:T(8,128)S(1)} %get-tuple-element.19), channel_id=1, source_target_pairs={{0,0},{1,16},{2,1},{3,17},{4,2},{5,18},{6,3},{7,19},{8,4},{9,20},{... | collective-permute-start | bytes 49160 | tf_op jit(solution)/shard_map/ppermute | solution.py:369
  395.9 3.2 collective-permute-start.7
  400.8 1.2 copy-start.1
Sparse Core Ops, SparseCore 0:
  354.6 40.5 all-gather.2

commit v4 on v3

--- a/solution.py
+++ b/solution.py
@@ -10,6 +10,7 @@
 LANES = 128
 EXTRA = RANK * RANK // LANES
 ROWS = RANK + EXTRA
+HEAD = 2 * RANK + 4 * EXTRA
 SMALL_BYTES = 4 * 1024 * 1024
 MID_BYTES = 20 * 1024 * 1024
 F32 = jnp.float32
@@ -19,23 +20,26 @@
 TN = (((0,), (0,)), ((), ()))
 
 
+def split_f32(value):
+    high = value.astype(BF16)
+    return high, value - high.astype(F32)
+
+
 def split_bf16(value):
-    high = value.astype(BF16)
-    low = (value - high.astype(F32)).astype(BF16)
-    return jnp.concatenate([high, low], axis=0)
-
-
-def pack(wide):
-    lane = lax.broadcasted_iota(jnp.int32, (EXTRA, LANES), 1) // RANK
-    out = wide[0:EXTRA]
-    for b in range(1, LANES // RANK):
-        out = jnp.where(lane == b, wide[b * EXTRA : (b + 1) * EXTRA], out)
-    return out
+    high, low = split_f32(value)
+    return jnp.concatenate([high, low.astype(BF16)], axis=0)
+
+
+def pack(gram):
+    return jnp.concatenate([gram[b * EXTRA : (b + 1) * EXTRA] for b in range(RANK // EXTRA)], axis=1)
+
+
+def self_gram(block, precision=None):
+    return lax.dot_general(block, block, NT, precision=precision, preferred_element_type=F32)
 
 
 def packed_gram(block):
-    tiled = jnp.concatenate([block] * (LANES // RANK), axis=0)
-    return pack(lax.dot_general(block, tiled, NT, precision=HIGH, preferred_element_type=F32))
+    return pack(self_gram(block, HIGH))
 
 
 def inverse_factor(packed, upper):
@@ -108,14 +112,14 @@
     )(a, basis)
 
 
-def first_step(core, a):
+def first_step(a):
     blocks, depth, width = a.shape
     depth -= RANK
     half = blocks // 2
 
-    def kernel(core_ref, a_ref, out_ref, send_ref, acc, send_sems):
+    def kernel(a_ref, out_ref, send_ref, acc, send_sems):
         def send(i):
-            t = (1 - core_ref[0]) * half + i
+            t = (1 - lax.axis_index("c")) * half + i
             return pltpu.make_async_copy(a_ref.at[t, 0:depth, :], send_ref.at[i], send_sems.at[i])
 
         for i in range(half):
@@ -142,12 +146,12 @@
             jax.ShapeDtypeStruct((2 * blocks, ROWS, LANES), F32),
             jax.ShapeDtypeStruct((half, depth, width), BF16),
         ],
-        in_specs=[pl.BlockSpec(memory_space=pltpu.SMEM), pl.BlockSpec(memory_space=pltpu.VMEM)],
+        in_specs=[pl.BlockSpec(memory_space=pltpu.VMEM)],
         out_specs=[pl.BlockSpec(memory_space=pltpu.VMEM), pl.BlockSpec(memory_space=pl.ANY)],
         scratch_shapes=[pltpu.VMEM((RANK, depth), F32), pltpu.SemaphoreType.DMA((half,))],
         compiler_params=pltpu.CompilerParams(vmem_limit_bytes=MID_BYTES),
         name="first_products",
-    )(core, a)
+    )(a)
 
 
 def store_part(out_ref, block, part, gram):
@@ -156,30 +160,28 @@
         out_ref[2 * block + side, RANK:ROWS, :] = gram
 
 
-def sketch_step(core, h, a, mate):
+def sketch_step(h, a, mate):
     half, depth, width = mate.shape
 
-    def kernel(core_ref, h_ref, a_ref, mate_ref, out_ref):
+    def kernel(h_ref, a_ref, mate_ref, out_ref):
         parts = [jnp.concatenate([h_ref[2 * i], h_ref[2 * i + 1]], axis=1) for i in range(half)]
         for side in range(2):
             rows = slice(side * RANK, (side + 1) * RANK)
             for i in range(half):
-                block = mate_ref[i] if side else a_ref[core_ref[0] * half + i, 0:depth, :]
+                block = mate_ref[i] if side else a_ref[lax.axis_index("c") * half + i, 0:depth, :]
                 term = lax.dot_general(parts[i], block, NT, preferred_element_type=F32)
                 if i == 0:
                     out_ref[rows, :] = term
                 else:
                     out_ref[rows, :] += term
         whole = jnp.concatenate(parts, axis=1)
-        tiled = jnp.concatenate([whole] * (LANES // RANK), axis=0)
         out_ref[2 * RANK :, :] = jnp.zeros((EXTRA, depth), F32)
-        out_ref[2 * RANK :, 0:LANES] = pack(lax.dot_general(whole, tiled, NT, preferred_element_type=F32))
+        out_ref[2 * RANK :, 0:LANES] = pack(self_gram(whole))
 
     return pl.pallas_call(
         kernel,
         out_shape=jax.ShapeDtypeStruct((2 * RANK + EXTRA, depth), F32),
         in_specs=[
-            pl.BlockSpec(memory_space=pltpu.SMEM),
             pl.BlockSpec(memory_space=pltpu.VMEM),
             pl.BlockSpec(memory_space=pltpu.VMEM),
             pl.BlockSpec(memory_space=pltpu.VMEM),
@@ -187,59 +189,76 @@
         out_specs=pl.BlockSpec(memory_space=pltpu.VMEM),
         compiler_params=pltpu.CompilerParams(vmem_limit_bytes=MID_BYTES),
         name="partial_sketch",
-    )(core, h, a, mate)
-
-
-def product_step(hours, keep, core, mine, other, a, mate):
+    )(h, a, mate)
+
+
+def product_step(hours, keep, mine, other, a, mate):
     half, depth, width = mate.shape
 
-    def kernel(core_ref, mine_ref, other_ref, a_ref, mate_ref, out_ref, *refs):
+    def kernel(mine_ref, other_ref, a_ref, mate_ref, out_ref):
         gram = mine_ref[2 * RANK :, 0:LANES] + other_ref[2 * RANK :, 0:LANES]
         v_inv = inverse_factor(gram, True) * float(hours) ** 0.5
         own = mine_ref[0:RANK, :] + other_ref[RANK : 2 * RANK, :]
         own = jnp.dot(v_inv, own, precision=HIGH, preferred_element_type=F32)
-        if keep:
-            refs[0][...] = own.astype(BF16)
         far = mine_ref[RANK : 2 * RANK, :] + other_ref[0:RANK, :]
         far = jnp.dot(v_inv, far, precision=HIGH, preferred_element_type=F32)
-        gram = packed_gram(own) + packed_gram(far)
+        gram = pack(self_gram(own, HIGH) + self_gram(far, HIGH))
         left = split_bf16(own)
         right = split_bf16(far)
+        if keep:
+            high, low = split_f32(gram)
+            rest = split_bf16(low)
+            gram = jnp.concatenate([high, rest, jnp.zeros((EXTRA, LANES), BF16)], axis=0)
+            kept = own.astype(BF16)
         for i in range(half):
-            both = jnp.dot(left, a_ref[core_ref[0] * half + i, 0:depth, :], preferred_element_type=F32)
+            both = jnp.dot(left, a_ref[lax.axis_index("c") * half + i, 0:depth, :], preferred_element_type=F32)
             both = both + jnp.dot(right, mate_ref[i], preferred_element_type=F32)
-            store_part(out_ref, i, both[0:RANK] + both[RANK : 2 * RANK], gram)
-
-    out_shape = [jax.ShapeDtypeStruct((2 * half, ROWS, LANES), F32)]
+            part = both[0:RANK] + both[RANK : 2 * RANK]
+            if not keep:
+                store_part(out_ref, i, part, gram)
+                continue
+            for side in range(2):
+                k = 2 * i + side
+                out_ref[k, 0 : 2 * RANK, :] = split_bf16(part[:, side * LANES : (side + 1) * LANES])
+                out_ref[k, 2 * RANK : HEAD, :] = gram
+                for j in range(depth // LANES):
+                    out_ref[k, HEAD + j * RANK : HEAD + (j + 1) * RANK, :] = kept[:, j * LANES : (j + 1) * LANES]
+
+    out_shape = jax.ShapeDtypeStruct((2 * half, ROWS, LANES), F32)
     if keep:
-        out_shape.append(jax.ShapeDtypeStruct((RANK, depth), BF16))
+        out_shape = jax.ShapeDtypeStruct((2 * half, HEAD + RANK * depth // LANES, LANES), BF16)
     return pl.pallas_call(
         kernel,
         out_shape=out_shape,
         in_specs=[
-            pl.BlockSpec(memory_space=pltpu.SMEM),
             pl.BlockSpec(memory_space=pltpu.VMEM),
             pl.BlockSpec(memory_space=pltpu.VMEM),
             pl.BlockSpec(memory_space=pltpu.VMEM),
             pl.BlockSpec(memory_space=pltpu.VMEM),
         ],
-        out_specs=[pl.BlockSpec(memory_space=pltpu.VMEM)] * len(out_shape),
+        out_specs=pl.BlockSpec(memory_space=pltpu.VMEM),
         compiler_params=pltpu.CompilerParams(vmem_limit_bytes=MID_BYTES),
         name="hour_products",
-    )(core, mine, other, a, mate)
+    )(mine, other, a, mate)
 
 
 def sum_step(parts, copies):
+    plain = parts.dtype == F32
+
     def kernel(in_ref, out_ref):
-        total = in_ref[0]
+        total = in_ref[0] if plain else in_ref[0, 0:HEAD, :].astype(F32)
         for k in range(1, parts.shape[0]):
-            total = total + in_ref[k]
+            total = total + (in_ref[k] if plain else in_ref[k, 0:HEAD, :].astype(F32))
+        if not plain:
+            products = total[0:RANK] + total[RANK : 2 * RANK]
+            gram = [total[2 * RANK + p * EXTRA : 2 * RANK + (p + 1) * EXTRA] for p in range(3)]
+            total = jnp.concatenate([products, gram[0] + (gram[1] + gram[2])], axis=0)
         for k in range(copies):
             out_ref[k] = total
 
     return pl.pallas_call(
         kernel,
-        out_shape=jax.ShapeDtypeStruct((copies,) + parts.shape[1:], F32),
+        out_shape=jax.ShapeDtypeStruct((copies, ROWS, LANES), F32),
         in_specs=[pl.BlockSpec(memory_space=pltpu.VMEM)],
         out_specs=pl.BlockSpec(memory_space=pltpu.VMEM),
         compiler_params=pltpu.CompilerParams(vmem_limit_bytes=SMALL_BYTES),
@@ -283,13 +302,13 @@
     )(parts)
 
 
-def column_step(grams, mine, other, core, hours):
-    def kernel(core_ref, gram_ref, mine_ref, other_ref, out_ref):
+def column_step(grams, mine, other, hours):
+    def kernel(gram_ref, mine_ref, other_ref, out_ref):
         total = gram_ref[0]
         for k in range(1, grams.shape[0]):
             total = total + gram_ref[k]
         v_inv = inverse_factor(total, True) * float(hours) ** 0.5
-        first = core_ref[0] == 0
+        first = lax.axis_index("c") == 0
         low = jnp.where(first, mine_ref[...], other_ref[...])
         high = jnp.where(first, other_ref[...], mine_ref[...])
         block = jnp.concatenate([low, high], axis=1)
@@ -298,21 +317,24 @@
     return pl.pallas_call(
         kernel,
         out_shape=jax.ShapeDtypeStruct((RANK, 2 * LANES), F32),
-        in_specs=[pl.BlockSpec(memory_space=pltpu.SMEM)] + [pl.BlockSpec(memory_space=pltpu.VMEM)] * 3,
+        in_specs=[pl.BlockSpec(memory_space=pltpu.VMEM)] * 3,
         out_specs=pl.BlockSpec(memory_space=pltpu.VMEM),
         compiler_params=pltpu.CompilerParams(vmem_limit_bytes=SMALL_BYTES),
         name="column_factor",
-    )(core, grams, mine, other)
-
-
-def row_step(l_inv, sketch):
-    blocks, _, depth = sketch.shape
+    )(grams, mine, other)
+
+
+def row_step(l_inv, parts):
+    blocks, height, _ = parts.shape
+    pieces = (height - HEAD) // RANK
+    depth = pieces * LANES
     group = 4
 
     def kernel(l_ref, s_ref, out_ref):
         left = split_bf16(l_ref[...])
         for k in range(group):
-            out = jnp.dot(left, s_ref[k], preferred_element_type=F32)
+            rows = [s_ref[k, HEAD + j * RANK : HEAD + (j + 1) * RANK, :] for j in range(pieces)]
+            out = jnp.dot(left, jnp.concatenate(rows, axis=1), preferred_element_type=F32)
             out_ref[:, k * depth : (k + 1) * depth] = out[0:RANK] + out[RANK : 2 * RANK]
 
     return pl.pallas_call(
@@ -321,15 +343,15 @@
         out_shape=jax.ShapeDtypeStruct((RANK, blocks * depth), F32),
         in_specs=[
             pl.BlockSpec((RANK, RANK), lambda i: (0, 0)),
-            pl.BlockSpec((group, RANK, depth), lambda i: (i, 0, 0)),
+            pl.BlockSpec((group, height, LANES), lambda i: (i, 0, 0)),
         ],
         out_specs=pl.BlockSpec((RANK, group * depth), lambda i: (0, i)),
         cost_estimate=pl.CostEstimate(
-            flops=6 * RANK * RANK * blocks * depth, bytes_accessed=6 * RANK * blocks * depth, transcendentals=0
+            flops=4 * RANK * RANK * blocks * depth, bytes_accessed=6 * RANK * blocks * depth, transcendentals=0
         ),
         compiler_params=pltpu.CompilerParams(vmem_limit_bytes=SMALL_BYTES),
         name="row_basis",
-    )(l_inv, sketch)
+    )(l_inv, parts)
 
 
 def ring(size, shift):
@@ -344,23 +366,21 @@
         points = anomaly.shape[0] * grid_size
         hours = anomaly.shape[1] * tm_size
         depth = anomaly.shape[0] // tm_size
-        core = lax.axis_index("c").reshape(1).astype(jnp.int32)
-        core, start_basis = lax.optimization_barrier((core, start_basis))
         a = append_basis(anomaly.reshape(tm_size, depth, anomaly.shape[1]), start_basis)
         a = lax.all_to_all(a, "t", 0, 0)
         swap = ring(2, 1)
-        out, send = first_step(core, a)
+        out, send = first_step(a)
         mate = lax.ppermute(send, "c", swap)
         part = lax.all_to_all(out, ("c", "t"), 0, 0)
         for step in range(ITERS):
             last = step == ITERS - 1
             if step:
-                sketch = sketch_step(core, h, a, mate)
+                sketch = sketch_step(h, a, mate)
                 other = lax.ppermute(sketch, "c", swap)
-                out = product_step(hours, last, core, sketch, other, a, mate)
+                out = product_step(hours, last, sketch, other, a, mate)
+                part = lax.all_to_all(out, "t", 0, 0)
                 if last:
-                    rows = lax.all_gather(out[1], "t", axis=0)
-                part = lax.all_to_all(out[0], "t", 0, 0)
+                    rows = part
             part = sum_step(part, grid_size // 2)
             part = lax.all_to_all(part, "z", 0, 0)
             out = hour_step(part, (2 if last else 1) * tm_size, points, last)
@@ -368,7 +388,7 @@
         home = [(i, i % 2 * tm_size + i // 2) for i in range(2 * tm_size)]
         mine = lax.ppermute(out[1], ("c", "t"), home)
         other = lax.ppermute(mine, "c", swap)
-        return row_step(out[2], rows), column_step(h, mine, other, core, hours)
+        return row_step(out[2], rows), column_step(h, mine, other, hours)
 
     return jax.shard_map(
         shards,

time: 412 us -> 403 us (0.978)
  between operations: 14.2 us -> 0.79 us
  blocking collectives: 294 us -> 306 us
  Pallas kernels: 50.2 us -> 44.5 us
    all_to_all x5, blocking collectives: 56.3 us -> 68.4 us  [shards(): part = lax.all_to_all(out, 't', 0, 0)]
    pallas_call x5, Pallas kernels: 18.7 us -> 13.5 us  [product_step(): pl.pallas_call(kernel, out_shape=out_shape, in_specs=[pl.BlockSpec(memory...]
  transfers between devices with their start and end apart: 10 -> 9, of which waited for: 7 -> 6; matrix products, arithmetic and copies ran while one was open for 0% -> 0% of each run, Pallas kernels for 1% -> 1%
where the time goes in v4:
time: 403 us; the launch traced here: 402 us
  blocking collectives  306 us (76%)
  Pallas kernels  44.5 us (11%)
  starting transfers between devices  36.9 us (9%)
  waiting for transfers between devices  9.6 us (2%)
  local copies, waits for them, and re-layouts  4.09 us (1%)
    all_to_all x1, blocking collectives, shards(): a = lax.all_to_all(a, 't', 0, 0)  101 us
    all_to_all x6, blocking collectives, shards(): part = lax.all_to_all(part, 'z', 0, 0)  70.1 us
    all_to_all x5, blocking collectives, shards(): part = lax.all_to_all(out, 't', 0, 0)  68.4 us
    all_to_all x5, blocking collectives, shards(): h = lax.all_to_all(out[0], ('c', 't') if last else 't', 0, 0)  49.9 us
    ppermute x5, starting transfers between devices, shards(): other = lax.ppermute(sketch, 'c', swap)  19.3 us
    all_to_all x1, blocking collectives, shards(): part = lax.all_to_all(out, ('c', 't'), 0, 0)  16.1 us
    pallas_call x5, Pallas kernels, product_step(): pl.pallas_call(kernel, out_shape=out_shape, in_specs=[pl.BlockSpec(memory...  13.5 us
    pallas_call x5, Pallas kernels, sketch_step(): pl.pallas_call(kernel, out_shape=jax.ShapeDtypeStruct((2 * RANK + EXTRA,...  13.2 us
  transfers between devices with their start and end apart: 9, of which 6 were waited for; matrix products, arithmetic and copies ran while one was open for 0% of the time, Pallas kernels for 1%

profile of v4, /device:TPU:13, one launch (start us, length us, event | category | flops | bytes accessed | tf_op | source)
XLA Modules:
  0.0 401.6 jit_solution(10343892961198423392)
XLA Ops:
  0.6 3.4 copy-done
  5.5 101.3 %all_to_all.95.a_ref = bf16[16,1056,256]{2,1,0:T(8,128)(2,1)S(1)} all-to-all(bf16[16,1056,256]{2,1,0:T(8,128)(2,1)S(1)} %append_basis.1), channel_id=1, replica_groups=mesh['z'=8,'c'=2,'t'=16] {'t'}, dimensions={0} | all-to-all | bytes 17301504 | tf_op jit(solution)/shard_map/all_to_all | solution.py:370
  106.8 4.5 %first_products.1 = (f32[32,40,128]{2,1,0:T(8,128)S(1)}, bf16[8,1024,256]{2,1,0:T(8,128)(2,1)S(1)}) custom-call(bf16[16,1056,256]{2,1,0:T(8,128)(2,1)S(1)} %all_to_all.95.a_ref), custom_call_target="tpu_custom_call" | custom-call | tf_op jit(solution)/shard_map/first_products/pallas_call | solution.py:143
  113.1 16.1 %all_to_all.96.in_ref = f32[32,40,128]{2,1,0:T(8,128)S(1)} all-to-all(f32[32,40,128]{2,1,0:T(8,128)S(1)} %get-tuple-element.7), channel_id=1, replica_groups=mesh['z'=8,'c'=2,'t'=16] {'c','t'}, dimensions={0} | all-to-all | bytes 1310720 | tf_op jit(solution)/shard_map/all_to_all | solution.py:374
  129.3 16.6 %all_to_all.97.in_ref = f32[8,40,128]{2,1,0:T(8,128)S(1)} all-to-all(f32[8,40,128]{2,1,0:T(8,128)S(1)} %sum_parts.6), channel_id=1, replica_groups=mesh['z'=8,'c'=2,'t'=16] {'z'}, dimensions={0} | all-to-all | bytes 327680 | tf_op jit(solution)/shard_map/all_to_all | solution.py:385
  147.1 10.6 %all_to_all.98.h_ref = bf16[16,32,128]{2,1,0:T(8,128)(2,1)S(1)} all-to-all(bf16[16,32,128]{2,1,0:T(8,128)(2,1)S(1)} %row_factor.6), channel_id=1, replica_groups=mesh['z'=8,'c'=2,'t'=16] {'t'}, dimensions={0} | all-to-all | bytes 262144 | tf_op jit(solution)/shard_map/all_to_all | solution.py:387
  160.3 2.8 collective-permute-start.1
  164.4 2.7 hour_products.5
  167.1 11.2 %all_to_all.99.in_ref = f32[16,40,128]{2,1,0:T(8,128)S(1)} all-to-all(f32[16,40,128]{2,1,0:T(8,128)S(1)} %hour_products.5), channel_id=1, replica_groups=mesh['z'=8,'c'=2,'t'=16] {'t'}, dimensions={0} | all-to-all | bytes 655360 | tf_op jit(solution)/shard_map/all_to_all | solution.py:381
  178.3 10.8 %all_to_all.100.in_ref = f32[8,40,128]{2,1,0:T(8,128)S(1)} all-to-all(f32[8,40,128]{2,1,0:T(8,128)S(1)} %sum_parts.7), channel_id=1, replica_groups=mesh['z'=8,'c'=2,'t'=16] {'z'}, dimensions={0} | all-to-all | bytes 327680 | tf_op jit(solution)/shard_map/all_to_all | solution.py:385
  190.3 9.8 %all_to_all.101.h_ref = bf16[16,32,128]{2,1,0:T(8,128)(2,1)S(1)} all-to-all(bf16[16,32,128]{2,1,0:T(8,128)(2,1)S(1)} %row_factor.7), channel_id=1, replica_groups=mesh['z'=8,'c'=2,'t'=16] {'t'}, dimensions={0} | all-to-all | bytes 262144 | tf_op jit(solution)/shard_map/all_to_all | solution.py:387
  202.8 4.2 %collective-permute-start.2 = (f32[72,1024]{1,0:T(8,128)S(1)}, f32[72,1024]{1,0:T(8,128)S(1)}, u32[]{:S(2)}, u32[]{:S(2)}) collective-permute-start(f32[72,1024]{1,0:T(8,128)S(1)} %partial_sketch.6.mine_ref), channel_id=1, source_target_pairs={{0,16},{16,0},{1,17},{17,1},{2,18},{18,2},{3,19},{19,3},{4,20},{20... | collective-permute-start | bytes 884744 | tf_op jit(solution)/shard_map/ppermute | solution.py:379
  210.9 11.2 %all_to_all.102.in_ref = f32[16,40,128]{2,1,0:T(8,128)S(1)} all-to-all(f32[16,40,128]{2,1,0:T(8,128)S(1)} %hour_products.6), channel_id=1, replica_groups=mesh['z'=8,'c'=2,'t'=16] {'t'}, dimensions={0} | all-to-all | bytes 655360 | tf_op jit(solution)/shard_map/all_to_all | solution.py:381
  222.1 10.8 %all_to_all.103.in_ref = f32[8,40,128]{2,1,0:T(8,128)S(1)} all-to-all(f32[8,40,128]{2,1,0:T(8,128)S(1)} %sum_parts.8), channel_id=1, replica_groups=mesh['z'=8,'c'=2,'t'=16] {'z'}, dimensions={0} | all-to-all | bytes 327680 | tf_op jit(solution)/shard_map/all_to_all | solution.py:385
  234.1 9.8 %all_to_all.104.h_ref = bf16[16,32,128]{2,1,0:T(8,128)(2,1)S(1)} all-to-all(bf16[16,32,128]{2,1,0:T(8,128)(2,1)S(1)} %row_factor.8), channel_id=1, replica_groups=mesh['z'=8,'c'=2,'t'=16] {'t'}, dimensions={0} | all-to-all | bytes 262144 | tf_op jit(solution)/shard_map/all_to_all | solution.py:387
  246.6 4.0 %collective-permute-start.3 = (f32[72,1024]{1,0:T(8,128)S(1)}, f32[72,1024]{1,0:T(8,128)S(1)}, u32[]{:S(2)}, u32[]{:S(2)}) collective-permute-start(f32[72,1024]{1,0:T(8,128)S(1)} %partial_sketch.7.mine_ref), channel_id=1, source_target_pairs={{0,16},{16,0},{1,17},{17,1},{2,18},{18,2},{3,19},{19,3},{4,20},{20... | collective-permute-start | bytes 884744 | tf_op jit(solution)/shard_map/ppermute | solution.py:379
  251.8 2.7 hour_products.7
  254.5 11.2 %all_to_all.105.in_ref = f32[16,40,128]{2,1,0:T(8,128)S(1)} all-to-all(f32[16,40,128]{2,1,0:T(8,128)S(1)} %hour_products.7), channel_id=1, replica_groups=mesh['z'=8,'c'=2,'t'=16] {'t'}, dimensions={0} | all-to-all | bytes 655360 | tf_op jit(solution)/shard_map/all_to_all | solution.py:381
  265.8 10.8 %all_to_all.106.in_ref = f32[8,40,128]{2,1,0:T(8,128)S(1)} all-to-all(f32[8,40,128]{2,1,0:T(8,128)S(1)} %sum_parts.9), channel_id=1, replica_groups=mesh['z'=8,'c'=2,'t'=16] {'z'}, dimensions={0} | all-to-all | bytes 327680 | tf_op jit(solution)/shard_map/all_to_all | solution.py:385
  277.8 9.8 %all_to_all.107.h_ref = bf16[16,32,128]{2,1,0:T(8,128)(2,1)S(1)} all-to-all(bf16[16,32,128]{2,1,0:T(8,128)(2,1)S(1)} %row_factor.9), channel_id=1, replica_groups=mesh['z'=8,'c'=2,'t'=16] {'t'}, dimensions={0} | all-to-all | bytes 262144 | tf_op jit(solution)/shard_map/all_to_all | solution.py:387
  290.2 4.0 %collective-permute-start.4 = (f32[72,1024]{1,0:T(8,128)S(1)}, f32[72,1024]{1,0:T(8,128)S(1)}, u32[]{:S(2)}, u32[]{:S(2)}) collective-permute-start(f32[72,1024]{1,0:T(8,128)S(1)} %partial_sketch.8.mine_ref), channel_id=1, source_target_pairs={{0,16},{16,0},{1,17},{17,1},{2,18},{18,2},{3,19},{19,3},{4,20},{20... | collective-permute-start | bytes 884744 | tf_op jit(solution)/shard_map/ppermute | solution.py:379
  295.5 2.7 hour_products.8
  298.2 11.2 %all_to_all.108.in_ref = f32[16,40,128]{2,1,0:T(8,128)S(1)} all-to-all(f32[16,40,128]{2,1,0:T(8,128)S(1)} %hour_products.8), channel_id=1, replica_groups=mesh['z'=8,'c'=2,'t'=16] {'t'}, dimensions={0} | all-to-all | bytes 655360 | tf_op jit(solution)/shard_map/all_to_all | solution.py:381
  309.4 10.8 %all_to_all.109.in_ref = f32[8,40,128]{2,1,0:T(8,128)S(1)} all-to-all(f32[8,40,128]{2,1,0:T(8,128)S(1)} %sum_parts.10), channel_id=1, replica_groups=mesh['z'=8,'c'=2,'t'=16] {'z'}, dimensions={0} | all-to-all | bytes 327680 | tf_op jit(solution)/shard_map/all_to_all | solution.py:385
  321.4 9.8 %all_to_all.110.h_ref = bf16[16,32,128]{2,1,0:T(8,128)(2,1)S(1)} all-to-all(bf16[16,32,128]{2,1,0:T(8,128)(2,1)S(1)} %row_factor.10), channel_id=1, replica_groups=mesh['z'=8,'c'=2,'t'=16] {'t'}, dimensions={0} | all-to-all | bytes 262144 | tf_op jit(solution)/shard_map/all_to_all | solution.py:387
  333.9 4.2 %collective-permute-start.5 = (f32[72,1024]{1,0:T(8,128)S(1)}, f32[72,1024]{1,0:T(8,128)S(1)}, u32[]{:S(2)}, u32[]{:S(2)}) collective-permute-start(f32[72,1024]{1,0:T(8,128)S(1)} %partial_sketch.9.mine_ref), channel_id=1, source_target_pairs={{0,16},{16,0},{1,17},{17,1},{2,18},{18,2},{3,19},{19,3},{4,20},{20... | collective-permute-start | bytes 884744 | tf_op jit(solution)/shard_map/ppermute | solution.py:379
  339.3 2.8 hour_products.9
  342.1 23.5 %all_to_all.111.in_ref.s_ref = bf16[16,352,128]{2,1,0:T(8,128)(2,1)S(1)} all-to-all(bf16[16,352,128]{2,1,0:T(8,128)(2,1)S(1)} %hour_products.9), channel_id=1, replica_groups=mesh['z'=8,'c'=2,'t'=16] {'t'}, dimensions={0} | all-to-all | bytes 2883584 | tf_op jit(solution)/shard_map/all_to_all | solution.py:381
  365.6 10.4 %all_to_all.112.in_ref = f32[8,40,128]{2,1,0:T(8,128)S(1)} all-to-all(f32[8,40,128]{2,1,0:T(8,128)S(1)} %sum_parts.11), channel_id=1, replica_groups=mesh['z'=8,'c'=2,'t'=16] {'z'}, dimensions={0} | all-to-all | bytes 327680 | tf_op jit(solution)/shard_map/all_to_all | solution.py:385
  378.1 9.5 %all-to-all-start.18 = ((f32[32,8,128]{2,1,0:T(8,128)}), f32[32,8,128]{2,1,0:T(8,128)S(1)}, u32[]{:S(2)}, u32[]{:S(2)}) async-start(f32[32,8,128]{2,1,0:T(8,128)} %get-tuple-element.10), calls=%async_computation.18 | async-start | bytes 262144 | tf_op jit(solution)/shard_map/all_to_all | solution.py:387
  387.6 3.9 collective-permute-start.6
  391.6 3.6 collective-permute-done.6.mine_ref
  (34 shorter events, 40.1 us)
Async XLA Ops:
  0.6 3.4 copy-start
  4.0 0.7 copy-start.1
  111.3 46.4 %collective-permute-start = (bf16[8,1024,256]{2,1,0:T(8,128)(2,1)S(1)}, bf16[8,1024,256]{2,1,0:T(8,128)(2,1)S(1)}, u32[]{:S(2)}, u32[]{:S(2)}) collective-permute-start(bf16[8,1024,256]{2,1,0:T(8,128)(2,1)S(1)} %get-tuple-element.8), channel_id=1, source_target_pairs={{0,16},{16,0},{1,17},{17,1},{2,18},{18,2},{3,19},{19,3},{4,20},{20... | collective-permute-start | bytes 12582920 | tf_op jit(solution)/shard_map/ppermute | solution.py:373
  160.3 4.1 %collective-permute-start.1 = (f32[72,1024]{1,0:T(8,128)S(1)}, f32[72,1024]{1,0:T(8,128)S(1)}, u32[]{:S(2)}, u32[]{:S(2)}) collective-permute-start(f32[72,1024]{1,0:T(8,128)S(1)} %partial_sketch.5.mine_ref), channel_id=1, source_target_pairs={{0,16},{16,0},{1,17},{17,1},{2,18},{18,2},{3,19},{19,3},{4,20},{20... | collective-permute-start | bytes 884744 | tf_op jit(solution)/shard_map/ppermute | solution.py:379
  202.8 5.4 %collective-permute-start.2 = (f32[72,1024]{1,0:T(8,128)S(1)}, f32[72,1024]{1,0:T(8,128)S(1)}, u32[]{:S(2)}, u32[]{:S(2)}) collective-permute-start(f32[72,1024]{1,0:T(8,128)S(1)} %partial_sketch.6.mine_ref), channel_id=1, source_target_pairs={{0,16},{16,0},{1,17},{17,1},{2,18},{18,2},{3,19},{19,3},{4,20},{20... | collective-permute-start | bytes 884744 | tf_op jit(solution)/shard_map/ppermute | solution.py:379
  246.6 5.3 %collective-permute-start.3 = (f32[72,1024]{1,0:T(8,128)S(1)}, f32[72,1024]{1,0:T(8,128)S(1)}, u32[]{:S(2)}, u32[]{:S(2)}) collective-permute-start(f32[72,1024]{1,0:T(8,128)S(1)} %partial_sketch.7.mine_ref), channel_id=1, source_target_pairs={{0,16},{16,0},{1,17},{17,1},{2,18},{18,2},{3,19},{19,3},{4,20},{20... | collective-permute-start | bytes 884744 | tf_op jit(solution)/shard_map/ppermute | solution.py:379
  290.2 5.2 %collective-permute-start.4 = (f32[72,1024]{1,0:T(8,128)S(1)}, f32[72,1024]{1,0:T(8,128)S(1)}, u32[]{:S(2)}, u32[]{:S(2)}) collective-permute-start(f32[72,1024]{1,0:T(8,128)S(1)} %partial_sketch.8.mine_ref), channel_id=1, source_target_pairs={{0,16},{16,0},{1,17},{17,1},{2,18},{18,2},{3,19},{19,3},{4,20},{20... | collective-permute-start | bytes 884744 | tf_op jit(solution)/shard_map/ppermute | solution.py:379
  333.9 5.4 %collective-permute-start.5 = (f32[72,1024]{1,0:T(8,128)S(1)}, f32[72,1024]{1,0:T(8,128)S(1)}, u32[]{:S(2)}, u32[]{:S(2)}) collective-permute-start(f32[72,1024]{1,0:T(8,128)S(1)} %partial_sketch.9.mine_ref), channel_id=1, source_target_pairs={{0,16},{16,0},{1,17},{17,1},{2,18},{18,2},{3,19},{19,3},{4,20},{20... | collective-permute-start | bytes 884744 | tf_op jit(solution)/shard_map/ppermute | solution.py:379
  378.1 21.8 %all-to-all-start.18 = ((f32[32,8,128]{2,1,0:T(8,128)}), f32[32,8,128]{2,1,0:T(8,128)S(1)}, u32[]{:S(2)}, u32[]{:S(2)}) async-start(f32[32,8,128]{2,1,0:T(8,128)} %get-tuple-element.10), calls=%async_computation.18 | async-start | bytes 262144 | tf_op jit(solution)/shard_map/all_to_all | solution.py:387
  387.6 7.5 %collective-permute-start.6 = (f32[32,128]{1,0:T(8,128)S(1)}, f32[32,128]{1,0:T(8,128)S(1)}, u32[]{:S(2)}, u32[]{:S(2)}) collective-permute-start(f32[32,128]{1,0:T(8,128)S(1)} %get-tuple-element.11), channel_id=1, source_target_pairs={{0,0},{1,16},{2,1},{3,17},{4,2},{5,18},{6,3},{7,19},{8,4},{9,20},{... | collective-permute-start | bytes 49160 | tf_op jit(solution)/shard_map/ppermute | solution.py:389
  395.1 4.8 %collective-permute-start.7 = (f32[32,128]{1,0:T(8,128)S(1)}, f32[32,128]{1,0:T(8,128)S(1)}, u32[]{:S(2)}, u32[]{:S(2)}) collective-permute-start(f32[32,128]{1,0:T(8,128)S(1)} %collective-permute-done.6.mine_ref), channel_id=1, source_target_pairs={{0,16},{16,0},{1,17},{17,1},{2,18},{18,2},{3,19},{19,3},{4,20},{20... | collective-permute-start | bytes 49160 | tf_op jit(solution)/shard_map/ppermute | solution.py:390

commit v5 on v4

--- a/solution.py
+++ b/solution.py
@@ -10,6 +10,7 @@
 LANES = 128
 EXTRA = RANK * RANK // LANES
 ROWS = RANK + EXTRA
+NARROW = RANK + 2 * EXTRA
 HEAD = 2 * RANK + 4 * EXTRA
 SMALL_BYTES = 4 * 1024 * 1024
 MID_BYTES = 20 * 1024 * 1024
@@ -192,12 +193,17 @@
     )(h, a, mate)
 
 
-def product_step(hours, keep, mine, other, a, mate):
+def product_step(hours, keep, mine, other, a, mate, l_inv=None):
     half, depth, width = mate.shape
-
-    def kernel(mine_ref, other_ref, a_ref, mate_ref, out_ref):
+    narrow = l_inv is not None
+    operands = (mine, other, a, mate) + ((l_inv,) if narrow else ())
+
+    def kernel(mine_ref, other_ref, a_ref, mate_ref, *rest_refs):
+        out_ref = rest_refs[-1]
         gram = mine_ref[2 * RANK :, 0:LANES] + other_ref[2 * RANK :, 0:LANES]
         v_inv = inverse_factor(gram, True) * float(hours) ** 0.5
+        if narrow:
+            v_inv = jnp.dot(rest_refs[0][...], v_inv, precision=HIGH, preferred_element_type=F32)
         own = mine_ref[0:RANK, :] + other_ref[RANK : 2 * RANK, :]
         own = jnp.dot(v_inv, own, precision=HIGH, preferred_element_type=F32)
         far = mine_ref[RANK : 2 * RANK, :] + other_ref[0:RANK, :]
@@ -214,6 +220,12 @@
             both = jnp.dot(left, a_ref[lax.axis_index("c") * half + i, 0:depth, :], preferred_element_type=F32)
             both = both + jnp.dot(right, mate_ref[i], preferred_element_type=F32)
             part = both[0:RANK] + both[RANK : 2 * RANK]
+            if narrow:
+                for side in range(2):
+                    k = 2 * i + side
+                    out_ref[k, 0:RANK, :] = part[:, side * LANES : (side + 1) * LANES].astype(BF16)
+                    out_ref[k, RANK:NARROW, :] = split_bf16(gram)
+                continue
             if not keep:
                 store_part(out_ref, i, part, gram)
                 continue
@@ -227,38 +239,49 @@
     out_shape = jax.ShapeDtypeStruct((2 * half, ROWS, LANES), F32)
     if keep:
         out_shape = jax.ShapeDtypeStruct((2 * half, HEAD + RANK * depth // LANES, LANES), BF16)
+    if narrow:
+        out_shape = jax.ShapeDtypeStruct((2 * half, NARROW, LANES), BF16)
     return pl.pallas_call(
         kernel,
         out_shape=out_shape,
-        in_specs=[
-            pl.BlockSpec(memory_space=pltpu.VMEM),
-            pl.BlockSpec(memory_space=pltpu.VMEM),
-            pl.BlockSpec(memory_space=pltpu.VMEM),
-            pl.BlockSpec(memory_space=pltpu.VMEM),
-        ],
+        in_specs=[pl.BlockSpec(memory_space=pltpu.VMEM)] * len(operands),
         out_specs=pl.BlockSpec(memory_space=pltpu.VMEM),
         compiler_params=pltpu.CompilerParams(vmem_limit_bytes=MID_BYTES),
         name="hour_products",
-    )(mine, other, a, mate)
+    )(*operands)
+
+
+def widen(total):
+    if total.shape[0] == NARROW:
+        return jnp.concatenate([total[0:RANK], total[RANK:ROWS] + total[ROWS:NARROW]], axis=0)
+    products = total[0:RANK] + total[RANK : 2 * RANK]
+    gram = [total[2 * RANK + p * EXTRA : 2 * RANK + (p + 1) * EXTRA] for p in range(3)]
+    return jnp.concatenate([products, gram[0] + (gram[1] + gram[2])], axis=0)
+
+
+def sum_parts(ref):
+    rows = min(ref.shape[1], HEAD)
+    total = ref[0, 0:rows, :].astype(F32)
+    for k in range(1, ref.shape[0]):
+        total = total + ref[k, 0:rows, :].astype(F32)
+    return total if ref.dtype == F32 else widen(total)
 
 
 def sum_step(parts, copies):
-    plain = parts.dtype == F32
+    narrow = parts.shape[1] == NARROW
 
     def kernel(in_ref, out_ref):
-        total = in_ref[0] if plain else in_ref[0, 0:HEAD, :].astype(F32)
-        for k in range(1, parts.shape[0]):
-            total = total + (in_ref[k] if plain else in_ref[k, 0:HEAD, :].astype(F32))
-        if not plain:
-            products = total[0:RANK] + total[RANK : 2 * RANK]
-            gram = [total[2 * RANK + p * EXTRA : 2 * RANK + (p + 1) * EXTRA] for p in range(3)]
-            total = jnp.concatenate([products, gram[0] + (gram[1] + gram[2])], axis=0)
+        total = sum_parts(in_ref)
+        if narrow:
+            total = jnp.concatenate([total[0:RANK].astype(BF16), split_bf16(total[RANK:ROWS])], axis=0)
         for k in range(copies):
             out_ref[k] = total
 
     return pl.pallas_call(
         kernel,
-        out_shape=jax.ShapeDtypeStruct((copies, ROWS, LANES), F32),
+        out_shape=jax.ShapeDtypeStruct(
+            (copies, NARROW if narrow else ROWS, LANES), BF16 if narrow else F32
+        ),
         in_specs=[pl.BlockSpec(memory_space=pltpu.VMEM)],
         out_specs=pl.BlockSpec(memory_space=pltpu.VMEM),
         compiler_params=pltpu.CompilerParams(vmem_limit_bytes=SMALL_BYTES),
@@ -266,40 +289,42 @@
     )(parts)
 
 
-def hour_step(parts, copies, points, last):
-    def kernel(in_ref, *outs):
-        total = in_ref[0]
-        for k in range(1, parts.shape[0]):
-            total = total + in_ref[k]
+def hour_step(parts, copies, points, last, l_prev=None):
+    operands = (parts,) if l_prev is None else (parts, l_prev)
+
+    def kernel(in_ref, *refs):
+        outs = refs[len(operands) - 1 :]
+        total = sum_parts(in_ref)
         l_inv = inverse_factor(total[RANK:ROWS], False) * float(points) ** 0.5
         hours = jnp.dot(l_inv, total[0:RANK], precision=HIGH, preferred_element_type=F32)
+        if l_prev is not None:
+            l_inv = jnp.dot(l_inv, refs[0][...], precision=HIGH, preferred_element_type=F32)
+        outs[1][...] = l_inv
         hours = lax.dot_general(l_inv, hours, TN, precision=HIGH, preferred_element_type=F32)
         if last:
             gram = packed_gram(hours)
             for k in range(copies):
                 outs[0][k] = gram
-            outs[1][...] = hours
-            outs[2][...] = l_inv
+            outs[2][...] = hours
         else:
             rounded = hours.astype(BF16)
             for k in range(copies):
                 outs[0][k] = rounded
 
-    out_shape = [jax.ShapeDtypeStruct((copies, RANK, LANES), BF16)]
+    out_shape = [
+        jax.ShapeDtypeStruct((copies, EXTRA, LANES), F32) if last else jax.ShapeDtypeStruct((copies, RANK, LANES), BF16),
+        jax.ShapeDtypeStruct((RANK, RANK), F32),
+    ]
     if last:
-        out_shape = [
-            jax.ShapeDtypeStruct((copies, EXTRA, LANES), F32),
-            jax.ShapeDtypeStruct((RANK, LANES), F32),
-            jax.ShapeDtypeStruct((RANK, RANK), F32),
-        ]
+        out_shape.append(jax.ShapeDtypeStruct((RANK, LANES), F32))
     return pl.pallas_call(
         kernel,
         out_shape=out_shape,
-        in_specs=[pl.BlockSpec(memory_space=pltpu.VMEM)],
+        in_specs=[pl.BlockSpec(memory_space=pltpu.VMEM)] * len(operands),
         out_specs=[pl.BlockSpec(memory_space=pltpu.VMEM)] * len(out_shape),
         compiler_params=pltpu.CompilerParams(vmem_limit_bytes=SMALL_BYTES),
         name="row_factor",
-    )(parts)
+    )(*operands)
 
 
 def column_step(grams, mine, other, hours):
@@ -374,21 +399,22 @@
         part = lax.all_to_all(out, ("c", "t"), 0, 0)
         for step in range(ITERS):
             last = step == ITERS - 1
+            l_prev = l_inv if 1 < step < ITERS - 1 else None
             if step:
                 sketch = sketch_step(h, a, mate)
                 other = lax.ppermute(sketch, "c", swap)
-                out = product_step(hours, last, sketch, other, a, mate)
+                out = product_step(hours, last, sketch, other, a, mate, l_prev)
                 part = lax.all_to_all(out, "t", 0, 0)
                 if last:
                     rows = part
             part = sum_step(part, grid_size // 2)
             part = lax.all_to_all(part, "z", 0, 0)
-            out = hour_step(part, (2 if last else 1) * tm_size, points, last)
-            h = lax.all_to_all(out[0], ("c", "t") if last else "t", 0, 0)
+            h, l_inv, *whole = hour_step(part, (2 if last else 1) * tm_size, points, last, l_prev)
+            h = lax.all_to_all(h, ("c", "t") if last else "t", 0, 0)
         home = [(i, i % 2 * tm_size + i // 2) for i in range(2 * tm_size)]
-        mine = lax.ppermute(out[1], ("c", "t"), home)
+        mine = lax.ppermute(whole[0], ("c", "t"), home)
         other = lax.ppermute(mine, "c", swap)
-        return row_step(out[2], rows), column_step(h, mine, other, hours)
+        return row_step(l_inv, rows), column_step(h, mine, other, hours)
 
     return jax.shard_map(
         shards,

time: 403 us -> 398 us (0.988)
  blocking collectives: 306 us -> 300 us
where the time goes in v5:
time: 398 us; the launch traced here: 397 us
  blocking collectives  300 us (75%)
  Pallas kernels  46.1 us (12%)
  starting transfers between devices  37.2 us (9%)
  waiting for transfers between devices  9.6 us (2%)
  local copies, waits for them, and re-layouts  4.09 us (1%)
    all_to_all x1, blocking collectives, shards(): a = lax.all_to_all(a, 't', 0, 0)  101 us
    all_to_all x6, blocking collectives, shards(): part = lax.all_to_all(part, 'z', 0, 0)  67.6 us
    all_to_all x5, blocking collectives, shards(): part = lax.all_to_all(out, 't', 0, 0)  65.1 us
    all_to_all x5, blocking collectives, shards(): h = lax.all_to_all(h, ('c', 't') if last else 't', 0, 0)  49.4 us
    ppermute x5, starting transfers between devices, shards(): other = lax.ppermute(sketch, 'c', swap)  19.7 us
    all_to_all x1, blocking collectives, shards(): part = lax.all_to_all(out, ('c', 't'), 0, 0)  16.1 us
    pallas_call x5, Pallas kernels, product_step(): pl.pallas_call(kernel, out_shape=out_shape, in_specs=[pl.BlockSpec(memory...  14.1 us
    pallas_call x5, Pallas kernels, sketch_step(): pl.pallas_call(kernel, out_shape=jax.ShapeDtypeStruct((2 * RANK + EXTRA,...  13.2 us
  transfers between devices with their start and end apart: 9, of which 6 were waited for; matrix products, arithmetic and copies ran while one was open for 0% of the time, Pallas kernels for 1%

profile of v5, /device:TPU:13, one launch (start us, length us, event | category | flops | bytes accessed | tf_op | source)
XLA Modules:
  0.0 397.4 jit_solution(9110346081015564481)
XLA Ops:
  0.6 3.4 copy-done
  5.5 101.3 %all_to_all.95.a_ref = bf16[16,1056,256]{2,1,0:T(8,128)(2,1)S(1)} all-to-all(bf16[16,1056,256]{2,1,0:T(8,128)(2,1)S(1)} %append_basis.1), channel_id=1, replica_groups=mesh['z'=8,'c'=2,'t'=16] {'t'}, dimensions={0} | all-to-all | bytes 17301504 | tf_op jit(solution)/shard_map/all_to_all | solution.py:395
  106.8 4.5 %first_products.1 = (f32[32,40,128]{2,1,0:T(8,128)S(1)}, bf16[8,1024,256]{2,1,0:T(8,128)(2,1)S(1)}) custom-call(bf16[16,1056,256]{2,1,0:T(8,128)(2,1)S(1)} %all_to_all.95.a_ref), custom_call_target="tpu_custom_call" | custom-call | tf_op jit(solution)/shard_map/first_products/pallas_call | solution.py:144
  113.1 16.1 %all_to_all.96.in_ref = f32[32,40,128]{2,1,0:T(8,128)S(1)} all-to-all(f32[32,40,128]{2,1,0:T(8,128)S(1)} %get-tuple-element.15), channel_id=1, replica_groups=mesh['z'=8,'c'=2,'t'=16] {'c','t'}, dimensions={0} | all-to-all | bytes 1310720 | tf_op jit(solution)/shard_map/all_to_all | solution.py:399
  129.3 16.6 %all_to_all.97.in_ref = f32[8,40,128]{2,1,0:T(8,128)S(1)} all-to-all(f32[8,40,128]{2,1,0:T(8,128)S(1)} %sum_parts.6), channel_id=1, replica_groups=mesh['z'=8,'c'=2,'t'=16] {'z'}, dimensions={0} | all-to-all | bytes 327680 | tf_op jit(solution)/shard_map/all_to_all | solution.py:411
  147.4 10.6 %all_to_all.98.h_ref = bf16[16,32,128]{2,1,0:T(8,128)(2,1)S(1)} all-to-all(bf16[16,32,128]{2,1,0:T(8,128)(2,1)S(1)} %get-tuple-element.16), channel_id=1, replica_groups=mesh['z'=8,'c'=2,'t'=16] {'t'}, dimensions={0} | all-to-all | bytes 262144 | tf_op jit(solution)/shard_map/all_to_all | solution.py:413
  160.6 2.8 collective-permute-start.1
  167.3 11.2 %all_to_all.99.in_ref = f32[16,40,128]{2,1,0:T(8,128)S(1)} all-to-all(f32[16,40,128]{2,1,0:T(8,128)S(1)} %hour_products.5), channel_id=1, replica_groups=mesh['z'=8,'c'=2,'t'=16] {'t'}, dimensions={0} | all-to-all | bytes 655360 | tf_op jit(solution)/shard_map/all_to_all | solution.py:407
  178.6 10.8 %all_to_all.100.in_ref = f32[8,40,128]{2,1,0:T(8,128)S(1)} all-to-all(f32[8,40,128]{2,1,0:T(8,128)S(1)} %sum_parts.7), channel_id=1, replica_groups=mesh['z'=8,'c'=2,'t'=16] {'z'}, dimensions={0} | all-to-all | bytes 327680 | tf_op jit(solution)/shard_map/all_to_all | solution.py:411
  190.6 9.8 %all_to_all.101.h_ref = bf16[16,32,128]{2,1,0:T(8,128)(2,1)S(1)} all-to-all(bf16[16,32,128]{2,1,0:T(8,128)(2,1)S(1)} %get-tuple-element.18), channel_id=1, replica_groups=mesh['z'=8,'c'=2,'t'=16] {'t'}, dimensions={0} | all-to-all | bytes 262144 | tf_op jit(solution)/shard_map/all_to_all | solution.py:413
  203.0 4.2 %collective-permute-start.2 = (f32[72,1024]{1,0:T(8,128)S(1)}, f32[72,1024]{1,0:T(8,128)S(1)}, u32[]{:S(2)}, u32[]{:S(2)}) collective-permute-start(f32[72,1024]{1,0:T(8,128)S(1)} %partial_sketch.6.mine_ref), channel_id=1, source_target_pairs={{0,16},{16,0},{1,17},{17,1},{2,18},{18,2},{3,19},{19,3},{4,20},{20... | collective-permute-start | bytes 884744 | tf_op jit(solution)/shard_map/ppermute | solution.py:405
  208.5 2.9 hour_products.6
  211.3 10.1 %all_to_all.102.in_ref = bf16[16,48,128]{2,1,0:T(8,128)(2,1)S(1)} all-to-all(bf16[16,48,128]{2,1,0:T(8,128)(2,1)S(1)} %hour_products.6), channel_id=1, replica_groups=mesh['z'=8,'c'=2,'t'=16] {'t'}, dimensions={0} | all-to-all | bytes 393216 | tf_op jit(solution)/shard_map/all_to_all | solution.py:407
  221.5 10.0 %all_to_all.103.in_ref = bf16[8,48,128]{2,1,0:T(8,128)(2,1)S(1)} all-to-all(bf16[8,48,128]{2,1,0:T(8,128)(2,1)S(1)} %sum_parts.8), channel_id=1, replica_groups=mesh['z'=8,'c'=2,'t'=16] {'z'}, dimensions={0} | all-to-all | bytes 196608 | tf_op jit(solution)/shard_map/all_to_all | solution.py:411
  232.8 9.7 %all_to_all.104.h_ref = bf16[16,32,128]{2,1,0:T(8,128)(2,1)S(1)} all-to-all(bf16[16,32,128]{2,1,0:T(8,128)(2,1)S(1)} %get-tuple-element.20), channel_id=1, replica_groups=mesh['z'=8,'c'=2,'t'=16] {'t'}, dimensions={0} | all-to-all | bytes 262144 | tf_op jit(solution)/shard_map/all_to_all | solution.py:413
  245.1 4.1 %collective-permute-start.3 = (f32[72,1024]{1,0:T(8,128)S(1)}, f32[72,1024]{1,0:T(8,128)S(1)}, u32[]{:S(2)}, u32[]{:S(2)}) collective-permute-start(f32[72,1024]{1,0:T(8,128)S(1)} %partial_sketch.7.mine_ref), channel_id=1, source_target_pairs={{0,16},{16,0},{1,17},{17,1},{2,18},{18,2},{3,19},{19,3},{4,20},{20... | collective-permute-start | bytes 884744 | tf_op jit(solution)/shard_map/ppermute | solution.py:405
  250.5 2.9 hour_products.7
  253.3 10.1 %all_to_all.105.in_ref = bf16[16,48,128]{2,1,0:T(8,128)(2,1)S(1)} all-to-all(bf16[16,48,128]{2,1,0:T(8,128)(2,1)S(1)} %hour_products.7), channel_id=1, replica_groups=mesh['z'=8,'c'=2,'t'=16] {'t'}, dimensions={0} | all-to-all | bytes 393216 | tf_op jit(solution)/shard_map/all_to_all | solution.py:407
  263.5 10.0 %all_to_all.106.in_ref = bf16[8,48,128]{2,1,0:T(8,128)(2,1)S(1)} all-to-all(bf16[8,48,128]{2,1,0:T(8,128)(2,1)S(1)} %sum_parts.9), channel_id=1, replica_groups=mesh['z'=8,'c'=2,'t'=16] {'z'}, dimensions={0} | all-to-all | bytes 196608 | tf_op jit(solution)/shard_map/all_to_all | solution.py:411
  274.8 9.7 %all_to_all.107.h_ref = bf16[16,32,128]{2,1,0:T(8,128)(2,1)S(1)} all-to-all(bf16[16,32,128]{2,1,0:T(8,128)(2,1)S(1)} %get-tuple-element.22), channel_id=1, replica_groups=mesh['z'=8,'c'=2,'t'=16] {'t'}, dimensions={0} | all-to-all | bytes 262144 | tf_op jit(solution)/shard_map/all_to_all | solution.py:413
  287.1 4.3 %collective-permute-start.4 = (f32[72,1024]{1,0:T(8,128)S(1)}, f32[72,1024]{1,0:T(8,128)S(1)}, u32[]{:S(2)}, u32[]{:S(2)}) collective-permute-start(f32[72,1024]{1,0:T(8,128)S(1)} %partial_sketch.8.mine_ref), channel_id=1, source_target_pairs={{0,16},{16,0},{1,17},{17,1},{2,18},{18,2},{3,19},{19,3},{4,20},{20... | collective-permute-start | bytes 884744 | tf_op jit(solution)/shard_map/ppermute | solution.py:405
  292.7 2.9 hour_products.8
  295.6 10.1 %all_to_all.108.in_ref = bf16[16,48,128]{2,1,0:T(8,128)(2,1)S(1)} all-to-all(bf16[16,48,128]{2,1,0:T(8,128)(2,1)S(1)} %hour_products.8), channel_id=1, replica_groups=mesh['z'=8,'c'=2,'t'=16] {'t'}, dimensions={0} | all-to-all | bytes 393216 | tf_op jit(solution)/shard_map/all_to_all | solution.py:407
  305.8 10.0 %all_to_all.109.in_ref = bf16[8,48,128]{2,1,0:T(8,128)(2,1)S(1)} all-to-all(bf16[8,48,128]{2,1,0:T(8,128)(2,1)S(1)} %sum_parts.10), channel_id=1, replica_groups=mesh['z'=8,'c'=2,'t'=16] {'z'}, dimensions={0} | all-to-all | bytes 196608 | tf_op jit(solution)/shard_map/all_to_all | solution.py:411
  317.4 9.7 %all_to_all.110.h_ref = bf16[16,32,128]{2,1,0:T(8,128)(2,1)S(1)} all-to-all(bf16[16,32,128]{2,1,0:T(8,128)(2,1)S(1)} %get-tuple-element.24), channel_id=1, replica_groups=mesh['z'=8,'c'=2,'t'=16] {'t'}, dimensions={0} | all-to-all | bytes 262144 | tf_op jit(solution)/shard_map/all_to_all | solution.py:413
  329.7 4.1 %collective-permute-start.5 = (f32[72,1024]{1,0:T(8,128)S(1)}, f32[72,1024]{1,0:T(8,128)S(1)}, u32[]{:S(2)}, u32[]{:S(2)}) collective-permute-start(f32[72,1024]{1,0:T(8,128)S(1)} %partial_sketch.9.mine_ref), channel_id=1, source_target_pairs={{0,16},{16,0},{1,17},{17,1},{2,18},{18,2},{3,19},{19,3},{4,20},{20... | collective-permute-start | bytes 884744 | tf_op jit(solution)/shard_map/ppermute | solution.py:405
  335.0 2.8 hour_products.9
  337.8 23.5 %all_to_all.111.in_ref.s_ref = bf16[16,352,128]{2,1,0:T(8,128)(2,1)S(1)} all-to-all(bf16[16,352,128]{2,1,0:T(8,128)(2,1)S(1)} %hour_products.9), channel_id=1, replica_groups=mesh['z'=8,'c'=2,'t'=16] {'t'}, dimensions={0} | all-to-all | bytes 2883584 | tf_op jit(solution)/shard_map/all_to_all | solution.py:407
  361.3 10.4 %all_to_all.112.in_ref = f32[8,40,128]{2,1,0:T(8,128)S(1)} all-to-all(f32[8,40,128]{2,1,0:T(8,128)S(1)} %sum_parts.11), channel_id=1, replica_groups=mesh['z'=8,'c'=2,'t'=16] {'z'}, dimensions={0} | all-to-all | bytes 327680 | tf_op jit(solution)/shard_map/all_to_all | solution.py:411
  373.9 9.5 %all-to-all-start.18 = ((f32[32,8,128]{2,1,0:T(8,128)}), f32[32,8,128]{2,1,0:T(8,128)S(1)}, u32[]{:S(2)}, u32[]{:S(2)}) async-start(f32[32,8,128]{2,1,0:T(8,128)} %get-tuple-element.26), calls=%async_computation.18 | async-start | bytes 262144 | tf_op jit(solution)/shard_map/all_to_all | solution.py:413
  383.4 3.9 collective-permute-start.6
  387.3 3.6 collective-permute-done.6.mine_ref
  (34 shorter events, 41.1 us)
Async XLA Ops:
  0.6 3.4 copy-start
  4.0 0.7 copy-start.1
  111.3 46.6 %collective-permute-start = (bf16[8,1024,256]{2,1,0:T(8,128)(2,1)S(1)}, bf16[8,1024,256]{2,1,0:T(8,128)(2,1)S(1)}, u32[]{:S(2)}, u32[]{:S(2)}) collective-permute-start(bf16[8,1024,256]{2,1,0:T(8,128)(2,1)S(1)} %get-tuple-element.17), channel_id=1, source_target_pairs={{0,16},{16,0},{1,17},{17,1},{2,18},{18,2},{3,19},{19,3},{4,20},{20... | collective-permute-start | bytes 12582920 | tf_op jit(solution)/shard_map/ppermute | solution.py:398
  160.6 4.0 %collective-permute-start.1 = (f32[72,1024]{1,0:T(8,128)S(1)}, f32[72,1024]{1,0:T(8,128)S(1)}, u32[]{:S(2)}, u32[]{:S(2)}) collective-permute-start(f32[72,1024]{1,0:T(8,128)S(1)} %partial_sketch.5.mine_ref), channel_id=1, source_target_pairs={{0,16},{16,0},{1,17},{17,1},{2,18},{18,2},{3,19},{19,3},{4,20},{20... | collective-permute-start | bytes 884744 | tf_op jit(solution)/shard_map/ppermute | solution.py:405
  203.0 5.4 %collective-permute-start.2 = (f32[72,1024]{1,0:T(8,128)S(1)}, f32[72,1024]{1,0:T(8,128)S(1)}, u32[]{:S(2)}, u32[]{:S(2)}) collective-permute-start(f32[72,1024]{1,0:T(8,128)S(1)} %partial_sketch.6.mine_ref), channel_id=1, source_target_pairs={{0,16},{16,0},{1,17},{17,1},{2,18},{18,2},{3,19},{19,3},{4,20},{20... | collective-permute-start | bytes 884744 | tf_op jit(solution)/shard_map/ppermute | solution.py:405
  245.1 5.3 %collective-permute-start.3 = (f32[72,1024]{1,0:T(8,128)S(1)}, f32[72,1024]{1,0:T(8,128)S(1)}, u32[]{:S(2)}, u32[]{:S(2)}) collective-permute-start(f32[72,1024]{1,0:T(8,128)S(1)} %partial_sketch.7.mine_ref), channel_id=1, source_target_pairs={{0,16},{16,0},{1,17},{17,1},{2,18},{18,2},{3,19},{19,3},{4,20},{20... | collective-permute-start | bytes 884744 | tf_op jit(solution)/shard_map/ppermute | solution.py:405
  287.1 5.6 %collective-permute-start.4 = (f32[72,1024]{1,0:T(8,128)S(1)}, f32[72,1024]{1,0:T(8,128)S(1)}, u32[]{:S(2)}, u32[]{:S(2)}) collective-permute-start(f32[72,1024]{1,0:T(8,128)S(1)} %partial_sketch.8.mine_ref), channel_id=1, source_target_pairs={{0,16},{16,0},{1,17},{17,1},{2,18},{18,2},{3,19},{19,3},{4,20},{20... | collective-permute-start | bytes 884744 | tf_op jit(solution)/shard_map/ppermute | solution.py:405
  329.7 5.3 %collective-permute-start.5 = (f32[72,1024]{1,0:T(8,128)S(1)}, f32[72,1024]{1,0:T(8,128)S(1)}, u32[]{:S(2)}, u32[]{:S(2)}) collective-permute-start(f32[72,1024]{1,0:T(8,128)S(1)} %partial_sketch.9.mine_ref), channel_id=1, source_target_pairs={{0,16},{16,0},{1,17},{17,1},{2,18},{18,2},{3,19},{19,3},{4,20},{20... | collective-permute-start | bytes 884744 | tf_op jit(solution)/shard_map/ppermute | solution.py:405
  373.9 21.8 %all-to-all-start.18 = ((f32[32,8,128]{2,1,0:T(8,128)}), f32[32,8,128]{2,1,0:T(8,128)S(1)}, u32[]{:S(2)}, u32[]{:S(2)}) async-start(f32[32,8,128]{2,1,0:T(8,128)} %get-tuple-element.26), calls=%async_computation.18 | async-start | bytes 262144 | tf_op jit(solution)/shard_map/all_to_all | solution.py:413
  383.4 7.5 %collective-permute-start.6 = (f32[32,128]{1,0:T(8,128)S(1)}, f32[32,128]{1,0:T(8,128)S(1)}, u32[]{:S(2)}, u32[]{:S(2)}) collective-permute-start(f32[32,128]{1,0:T(8,128)S(1)} %get-tuple-element.27), channel_id=1, source_target_pairs={{0,0},{1,16},{2,1},{3,17},{4,2},{5,18},{6,3},{7,19},{8,4},{9,20},{... | collective-permute-start | bytes 49160 | tf_op jit(solution)/shard_map/ppermute | solution.py:415
  390.9 4.8 %collective-permute-start.7 = (f32[32,128]{1,0:T(8,128)S(1)}, f32[32,128]{1,0:T(8,128)S(1)}, u32[]{:S(2)}, u32[]{:S(2)}) collective-permute-start(f32[32,128]{1,0:T(8,128)S(1)} %collective-permute-done.6.mine_ref), channel_id=1, source_target_pairs={{0,16},{16,0},{1,17},{17,1},{2,18},{18,2},{3,19},{19,3},{4,20},{20... | collective-permute-start | bytes 49160 | tf_op jit(solution)/shard_map/ppermute | solution.py:416

commit v6 on v5

--- a/solution.py
+++ b/solution.py
@@ -11,7 +11,6 @@
 EXTRA = RANK * RANK // LANES
 ROWS = RANK + EXTRA
 NARROW = RANK + 2 * EXTRA
-HEAD = 2 * RANK + 4 * EXTRA
 SMALL_BYTES = 4 * 1024 * 1024
 MID_BYTES = 20 * 1024 * 1024
 F32 = jnp.float32
@@ -211,36 +210,26 @@
         gram = pack(self_gram(own, HIGH) + self_gram(far, HIGH))
         left = split_bf16(own)
         right = split_bf16(far)
-        if keep:
-            high, low = split_f32(gram)
-            rest = split_bf16(low)
-            gram = jnp.concatenate([high, rest, jnp.zeros((EXTRA, LANES), BF16)], axis=0)
-            kept = own.astype(BF16)
+        kept = own.astype(BF16)
         for i in range(half):
             both = jnp.dot(left, a_ref[lax.axis_index("c") * half + i, 0:depth, :], preferred_element_type=F32)
             both = both + jnp.dot(right, mate_ref[i], preferred_element_type=F32)
             part = both[0:RANK] + both[RANK : 2 * RANK]
-            if narrow:
-                for side in range(2):
-                    k = 2 * i + side
-                    out_ref[k, 0:RANK, :] = part[:, side * LANES : (side + 1) * LANES].astype(BF16)
-                    out_ref[k, RANK:NARROW, :] = split_bf16(gram)
-                continue
-            if not keep:
+            if not narrow:
                 store_part(out_ref, i, part, gram)
                 continue
             for side in range(2):
                 k = 2 * i + side
-                out_ref[k, 0 : 2 * RANK, :] = split_bf16(part[:, side * LANES : (side + 1) * LANES])
-                out_ref[k, 2 * RANK : HEAD, :] = gram
-                for j in range(depth // LANES):
-                    out_ref[k, HEAD + j * RANK : HEAD + (j + 1) * RANK, :] = kept[:, j * LANES : (j + 1) * LANES]
+                out_ref[k, 0:RANK, :] = part[:, side * LANES : (side + 1) * LANES].astype(BF16)
+                out_ref[k, RANK:NARROW, :] = split_bf16(gram)
+                for j in range(depth // LANES if keep else 0):
+                    rows = slice(NARROW + j * RANK, NARROW + (j + 1) * RANK)
+                    out_ref[k, rows, :] = kept[:, j * LANES : (j + 1) * LANES]
 
     out_shape = jax.ShapeDtypeStruct((2 * half, ROWS, LANES), F32)
-    if keep:
-        out_shape = jax.ShapeDtypeStruct((2 * half, HEAD + RANK * depth // LANES, LANES), BF16)
     if narrow:
-        out_shape = jax.ShapeDtypeStruct((2 * half, NARROW, LANES), BF16)
+        height = NARROW + (RANK * depth // LANES if keep else 0)
+        out_shape = jax.ShapeDtypeStruct((2 * half, height, LANES), BF16)
     return pl.pallas_call(
         kernel,
         out_shape=out_shape,
@@ -251,24 +240,18 @@
     )(*operands)
 
 
-def widen(total):
-    if total.shape[0] == NARROW:
-        return jnp.concatenate([total[0:RANK], total[RANK:ROWS] + total[ROWS:NARROW]], axis=0)
-    products = total[0:RANK] + total[RANK : 2 * RANK]
-    gram = [total[2 * RANK + p * EXTRA : 2 * RANK + (p + 1) * EXTRA] for p in range(3)]
-    return jnp.concatenate([products, gram[0] + (gram[1] + gram[2])], axis=0)
-
-
 def sum_parts(ref):
-    rows = min(ref.shape[1], HEAD)
+    rows = ROWS if ref.dtype == F32 else NARROW
     total = ref[0, 0:rows, :].astype(F32)
     for k in range(1, ref.shape[0]):
         total = total + ref[k, 0:rows, :].astype(F32)
-    return total if ref.dtype == F32 else widen(total)
+    if rows == ROWS:
+        return total
+    return jnp.concatenate([total[0:RANK], total[RANK:ROWS] + total[ROWS:NARROW]], axis=0)
 
 
 def sum_step(parts, copies):
-    narrow = parts.shape[1] == NARROW
+    narrow = parts.dtype == BF16
 
     def kernel(in_ref, out_ref):
         total = sum_parts(in_ref)
@@ -297,9 +280,12 @@
         total = sum_parts(in_ref)
         l_inv = inverse_factor(total[RANK:ROWS], False) * float(points) ** 0.5
         hours = jnp.dot(l_inv, total[0:RANK], precision=HIGH, preferred_element_type=F32)
+        if last:
+            outs[1][...] = l_inv
         if l_prev is not None:
             l_inv = jnp.dot(l_inv, refs[0][...], precision=HIGH, preferred_element_type=F32)
-        outs[1][...] = l_inv
+        if not last:
+            outs[1][...] = l_inv
         hours = lax.dot_general(l_inv, hours, TN, precision=HIGH, preferred_element_type=F32)
         if last:
             gram = packed_gram(hours)
@@ -351,14 +337,14 @@
 
 def row_step(l_inv, parts):
     blocks, height, _ = parts.shape
-    pieces = (height - HEAD) // RANK
+    pieces = (height - NARROW) // RANK
     depth = pieces * LANES
     group = 4
 
     def kernel(l_ref, s_ref, out_ref):
         left = split_bf16(l_ref[...])
         for k in range(group):
-            rows = [s_ref[k, HEAD + j * RANK : HEAD + (j + 1) * RANK, :] for j in range(pieces)]
+            rows = [s_ref[k, NARROW + j * RANK : NARROW + (j + 1) * RANK, :] for j in range(pieces)]
             out = jnp.dot(left, jnp.concatenate(rows, axis=1), preferred_element_type=F32)
             out_ref[:, k * depth : (k + 1) * depth] = out[0:RANK] + out[RANK : 2 * RANK]
 
@@ -399,7 +385,7 @@
         part = lax.all_to_all(out, ("c", "t"), 0, 0)
         for step in range(ITERS):
             last = step == ITERS - 1
-            l_prev = l_inv if 1 < step < ITERS - 1 else None
+            l_prev = l_inv if step > 1 else None
             if step:
                 sketch = sketch_step(h, a, mate)
                 other = lax.ppermute(sketch, "c", swap)

time: 398 us -> 395 us (level)
  no operation moved by 1% of the time
where the time goes in v6:
time: 395 us; the launch traced here: 394 us
  blocking collectives  297 us (75%)
  Pallas kernels  45.9 us (12%)
  starting transfers between devices  36.5 us (9%)
  waiting for transfers between devices  9.6 us (2%)
  local copies, waits for them, and re-layouts  4.09 us (1%)
    all_to_all x1, blocking collectives, shards(): a = lax.all_to_all(a, 't', 0, 0)  101 us
    all_to_all x6, blocking collectives, shards(): part = lax.all_to_all(part, 'z', 0, 0)  67.2 us
    all_to_all x5, blocking collectives, shards(): part = lax.all_to_all(out, 't', 0, 0)  63.4 us
    all_to_all x5, blocking collectives, shards(): h = lax.all_to_all(h, ('c', 't') if last else 't', 0, 0)  49.4 us
    ppermute x5, starting transfers between devices, shards(): other = lax.ppermute(sketch, 'c', swap)  19.7 us
    all_to_all x1, blocking collectives, shards(): part = lax.all_to_all(out, ('c', 't'), 0, 0)  16.1 us
    pallas_call x5, Pallas kernels, product_step(): pl.pallas_call(kernel, out_shape=out_shape, in_specs=[pl.BlockSpec(memory...  14.2 us
    pallas_call x5, Pallas kernels, sketch_step(): pl.pallas_call(kernel, out_shape=jax.ShapeDtypeStruct((2 * RANK + EXTRA,...  13.2 us
  transfers between devices with their start and end apart: 9, of which 6 were waited for; matrix products, arithmetic and copies ran while one was open for 0% of the time, Pallas kernels for 1%

profile of v6, /device:TPU:13, one launch (start us, length us, event | category | flops | bytes accessed | tf_op | source)
XLA Modules:
  0.0 394.4 jit_solution(7654586365458294738)
XLA Ops:
  0.6 3.4 copy-done
  5.5 101.3 %all_to_all.95.a_ref = bf16[16,1056,256]{2,1,0:T(8,128)(2,1)S(1)} all-to-all(bf16[16,1056,256]{2,1,0:T(8,128)(2,1)S(1)} %append_basis.1), channel_id=1, replica_groups=mesh['z'=8,'c'=2,'t'=16] {'t'}, dimensions={0} | all-to-all | bytes 17301504 | tf_op jit(solution)/shard_map/all_to_all | solution.py:381
  106.8 4.5 %first_products.1 = (f32[32,40,128]{2,1,0:T(8,128)S(1)}, bf16[8,1024,256]{2,1,0:T(8,128)(2,1)S(1)}) custom-call(bf16[16,1056,256]{2,1,0:T(8,128)(2,1)S(1)} %all_to_all.95.a_ref), custom_call_target="tpu_custom_call" | custom-call | tf_op jit(solution)/shard_map/first_products/pallas_call | solution.py:143
  113.1 16.1 %all_to_all.96.in_ref = f32[32,40,128]{2,1,0:T(8,128)S(1)} all-to-all(f32[32,40,128]{2,1,0:T(8,128)S(1)} %get-tuple-element.16), channel_id=1, replica_groups=mesh['z'=8,'c'=2,'t'=16] {'c','t'}, dimensions={0} | all-to-all | bytes 1310720 | tf_op jit(solution)/shard_map/all_to_all | solution.py:385
  129.3 16.6 %all_to_all.97.in_ref = f32[8,40,128]{2,1,0:T(8,128)S(1)} all-to-all(f32[8,40,128]{2,1,0:T(8,128)S(1)} %sum_parts.6), channel_id=1, replica_groups=mesh['z'=8,'c'=2,'t'=16] {'z'}, dimensions={0} | all-to-all | bytes 327680 | tf_op jit(solution)/shard_map/all_to_all | solution.py:397
  147.4 10.6 %all_to_all.98.h_ref = bf16[16,32,128]{2,1,0:T(8,128)(2,1)S(1)} all-to-all(bf16[16,32,128]{2,1,0:T(8,128)(2,1)S(1)} %get-tuple-element.17), channel_id=1, replica_groups=mesh['z'=8,'c'=2,'t'=16] {'t'}, dimensions={0} | all-to-all | bytes 262144 | tf_op jit(solution)/shard_map/all_to_all | solution.py:399
  160.6 2.8 collective-permute-start.1
  167.3 11.2 %all_to_all.99.in_ref = f32[16,40,128]{2,1,0:T(8,128)S(1)} all-to-all(f32[16,40,128]{2,1,0:T(8,128)S(1)} %hour_products.5), channel_id=1, replica_groups=mesh['z'=8,'c'=2,'t'=16] {'t'}, dimensions={0} | all-to-all | bytes 655360 | tf_op jit(solution)/shard_map/all_to_all | solution.py:393
  178.6 10.8 %all_to_all.100.in_ref = f32[8,40,128]{2,1,0:T(8,128)S(1)} all-to-all(f32[8,40,128]{2,1,0:T(8,128)S(1)} %sum_parts.7), channel_id=1, replica_groups=mesh['z'=8,'c'=2,'t'=16] {'z'}, dimensions={0} | all-to-all | bytes 327680 | tf_op jit(solution)/shard_map/all_to_all | solution.py:397
  190.6 9.8 %all_to_all.101.h_ref = bf16[16,32,128]{2,1,0:T(8,128)(2,1)S(1)} all-to-all(bf16[16,32,128]{2,1,0:T(8,128)(2,1)S(1)} %get-tuple-element.19), channel_id=1, replica_groups=mesh['z'=8,'c'=2,'t'=16] {'t'}, dimensions={0} | all-to-all | bytes 262144 | tf_op jit(solution)/shard_map/all_to_all | solution.py:399
  203.0 4.2 %collective-permute-start.2 = (f32[72,1024]{1,0:T(8,128)S(1)}, f32[72,1024]{1,0:T(8,128)S(1)}, u32[]{:S(2)}, u32[]{:S(2)}) collective-permute-start(f32[72,1024]{1,0:T(8,128)S(1)} %partial_sketch.6.mine_ref), channel_id=1, source_target_pairs={{0,16},{16,0},{1,17},{17,1},{2,18},{18,2},{3,19},{19,3},{4,20},{20... | collective-permute-start | bytes 884744 | tf_op jit(solution)/shard_map/ppermute | solution.py:391
  208.5 2.9 hour_products.6
  211.3 10.1 %all_to_all.102.in_ref = bf16[16,48,128]{2,1,0:T(8,128)(2,1)S(1)} all-to-all(bf16[16,48,128]{2,1,0:T(8,128)(2,1)S(1)} %hour_products.6), channel_id=1, replica_groups=mesh['z'=8,'c'=2,'t'=16] {'t'}, dimensions={0} | all-to-all | bytes 393216 | tf_op jit(solution)/shard_map/all_to_all | solution.py:393
  221.5 10.0 %all_to_all.103.in_ref = bf16[8,48,128]{2,1,0:T(8,128)(2,1)S(1)} all-to-all(bf16[8,48,128]{2,1,0:T(8,128)(2,1)S(1)} %sum_parts.8), channel_id=1, replica_groups=mesh['z'=8,'c'=2,'t'=16] {'z'}, dimensions={0} | all-to-all | bytes 196608 | tf_op jit(solution)/shard_map/all_to_all | solution.py:397
  232.8 9.7 %all_to_all.104.h_ref = bf16[16,32,128]{2,1,0:T(8,128)(2,1)S(1)} all-to-all(bf16[16,32,128]{2,1,0:T(8,128)(2,1)S(1)} %get-tuple-element.21), channel_id=1, replica_groups=mesh['z'=8,'c'=2,'t'=16] {'t'}, dimensions={0} | all-to-all | bytes 262144 | tf_op jit(solution)/shard_map/all_to_all | solution.py:399
  245.1 4.1 %collective-permute-start.3 = (f32[72,1024]{1,0:T(8,128)S(1)}, f32[72,1024]{1,0:T(8,128)S(1)}, u32[]{:S(2)}, u32[]{:S(2)}) collective-permute-start(f32[72,1024]{1,0:T(8,128)S(1)} %partial_sketch.7.mine_ref), channel_id=1, source_target_pairs={{0,16},{16,0},{1,17},{17,1},{2,18},{18,2},{3,19},{19,3},{4,20},{20... | collective-permute-start | bytes 884744 | tf_op jit(solution)/shard_map/ppermute | solution.py:391
  250.5 2.9 hour_products.7
  253.3 10.1 %all_to_all.105.in_ref = bf16[16,48,128]{2,1,0:T(8,128)(2,1)S(1)} all-to-all(bf16[16,48,128]{2,1,0:T(8,128)(2,1)S(1)} %hour_products.7), channel_id=1, replica_groups=mesh['z'=8,'c'=2,'t'=16] {'t'}, dimensions={0} | all-to-all | bytes 393216 | tf_op jit(solution)/shard_map/all_to_all | solution.py:393
  263.5 10.0 %all_to_all.106.in_ref = bf16[8,48,128]{2,1,0:T(8,128)(2,1)S(1)} all-to-all(bf16[8,48,128]{2,1,0:T(8,128)(2,1)S(1)} %sum_parts.9), channel_id=1, replica_groups=mesh['z'=8,'c'=2,'t'=16] {'z'}, dimensions={0} | all-to-all | bytes 196608 | tf_op jit(solution)/shard_map/all_to_all | solution.py:397
  274.8 9.7 %all_to_all.107.h_ref = bf16[16,32,128]{2,1,0:T(8,128)(2,1)S(1)} all-to-all(bf16[16,32,128]{2,1,0:T(8,128)(2,1)S(1)} %get-tuple-element.23), channel_id=1, replica_groups=mesh['z'=8,'c'=2,'t'=16] {'t'}, dimensions={0} | all-to-all | bytes 262144 | tf_op jit(solution)/shard_map/all_to_all | solution.py:399
  287.1 4.3 %collective-permute-start.4 = (f32[72,1024]{1,0:T(8,128)S(1)}, f32[72,1024]{1,0:T(8,128)S(1)}, u32[]{:S(2)}, u32[]{:S(2)}) collective-permute-start(f32[72,1024]{1,0:T(8,128)S(1)} %partial_sketch.8.mine_ref), channel_id=1, source_target_pairs={{0,16},{16,0},{1,17},{17,1},{2,18},{18,2},{3,19},{19,3},{4,20},{20... | collective-permute-start | bytes 884744 | tf_op jit(solution)/shard_map/ppermute | solution.py:391
  292.7 2.9 hour_products.8
  295.6 10.1 %all_to_all.108.in_ref = bf16[16,48,128]{2,1,0:T(8,128)(2,1)S(1)} all-to-all(bf16[16,48,128]{2,1,0:T(8,128)(2,1)S(1)} %hour_products.8), channel_id=1, replica_groups=mesh['z'=8,'c'=2,'t'=16] {'t'}, dimensions={0} | all-to-all | bytes 393216 | tf_op jit(solution)/shard_map/all_to_all | solution.py:393
  305.8 10.0 %all_to_all.109.in_ref = bf16[8,48,128]{2,1,0:T(8,128)(2,1)S(1)} all-to-all(bf16[8,48,128]{2,1,0:T(8,128)(2,1)S(1)} %sum_parts.10), channel_id=1, replica_groups=mesh['z'=8,'c'=2,'t'=16] {'z'}, dimensions={0} | all-to-all | bytes 196608 | tf_op jit(solution)/shard_map/all_to_all | solution.py:397
  317.0 9.7 %all_to_all.110.h_ref = bf16[16,32,128]{2,1,0:T(8,128)(2,1)S(1)} all-to-all(bf16[16,32,128]{2,1,0:T(8,128)(2,1)S(1)} %get-tuple-element.25), channel_id=1, replica_groups=mesh['z'=8,'c'=2,'t'=16] {'t'}, dimensions={0} | all-to-all | bytes 262144 | tf_op jit(solution)/shard_map/all_to_all | solution.py:399
  329.3 4.1 %collective-permute-start.5 = (f32[72,1024]{1,0:T(8,128)S(1)}, f32[72,1024]{1,0:T(8,128)S(1)}, u32[]{:S(2)}, u32[]{:S(2)}) collective-permute-start(f32[72,1024]{1,0:T(8,128)S(1)} %partial_sketch.9.mine_ref), channel_id=1, source_target_pairs={{0,16},{16,0},{1,17},{17,1},{2,18},{18,2},{3,19},{19,3},{4,20},{20... | collective-permute-start | bytes 884744 | tf_op jit(solution)/shard_map/ppermute | solution.py:391
  334.7 2.9 hour_products.9
  337.6 21.7 %all_to_all.111.in_ref.s_ref = bf16[16,304,128]{2,1,0:T(8,128)(2,1)S(1)} all-to-all(bf16[16,304,128]{2,1,0:T(8,128)(2,1)S(1)} %hour_products.9), channel_id=1, replica_groups=mesh['z'=8,'c'=2,'t'=16] {'t'}, dimensions={0} | all-to-all | bytes 2490368 | tf_op jit(solution)/shard_map/all_to_all | solution.py:393
  359.4 10.1 %all_to_all.112.in_ref = bf16[8,48,128]{2,1,0:T(8,128)(2,1)S(1)} all-to-all(bf16[8,48,128]{2,1,0:T(8,128)(2,1)S(1)} %sum_parts.11), channel_id=1, replica_groups=mesh['z'=8,'c'=2,'t'=16] {'z'}, dimensions={0} | all-to-all | bytes 196608 | tf_op jit(solution)/shard_map/all_to_all | solution.py:397
  371.6 8.8 %all-to-all-start.18 = ((f32[32,8,128]{2,1,0:T(8,128)}), f32[32,8,128]{2,1,0:T(8,128)S(1)}, u32[]{:S(2)}, u32[]{:S(2)}) async-start(f32[32,8,128]{2,1,0:T(8,128)} %get-tuple-element.28), calls=%async_computation.18 | async-start | bytes 262144 | tf_op jit(solution)/shard_map/all_to_all | solution.py:399
  380.4 3.9 collective-permute-start.6
  384.3 3.6 collective-permute-done.6.mine_ref
  (34 shorter events, 40.9 us)
Async XLA Ops:
  0.6 3.4 copy-start
  4.0 0.7 copy-start.1
  111.3 46.6 %collective-permute-start = (bf16[8,1024,256]{2,1,0:T(8,128)(2,1)S(1)}, bf16[8,1024,256]{2,1,0:T(8,128)(2,1)S(1)}, u32[]{:S(2)}, u32[]{:S(2)}) collective-permute-start(bf16[8,1024,256]{2,1,0:T(8,128)(2,1)S(1)} %get-tuple-element.18), channel_id=1, source_target_pairs={{0,16},{16,0},{1,17},{17,1},{2,18},{18,2},{3,19},{19,3},{4,20},{20... | collective-permute-start | bytes 12582920 | tf_op jit(solution)/shard_map/ppermute | solution.py:384
  160.6 4.0 %collective-permute-start.1 = (f32[72,1024]{1,0:T(8,128)S(1)}, f32[72,1024]{1,0:T(8,128)S(1)}, u32[]{:S(2)}, u32[]{:S(2)}) collective-permute-start(f32[72,1024]{1,0:T(8,128)S(1)} %partial_sketch.5.mine_ref), channel_id=1, source_target_pairs={{0,16},{16,0},{1,17},{17,1},{2,18},{18,2},{3,19},{19,3},{4,20},{20... | collective-permute-start | bytes 884744 | tf_op jit(solution)/shard_map/ppermute | solution.py:391
  203.0 5.4 %collective-permute-start.2 = (f32[72,1024]{1,0:T(8,128)S(1)}, f32[72,1024]{1,0:T(8,128)S(1)}, u32[]{:S(2)}, u32[]{:S(2)}) collective-permute-start(f32[72,1024]{1,0:T(8,128)S(1)} %partial_sketch.6.mine_ref), channel_id=1, source_target_pairs={{0,16},{16,0},{1,17},{17,1},{2,18},{18,2},{3,19},{19,3},{4,20},{20... | collective-permute-start | bytes 884744 | tf_op jit(solution)/shard_map/ppermute | solution.py:391
  245.1 5.3 %collective-permute-start.3 = (f32[72,1024]{1,0:T(8,128)S(1)}, f32[72,1024]{1,0:T(8,128)S(1)}, u32[]{:S(2)}, u32[]{:S(2)}) collective-permute-start(f32[72,1024]{1,0:T(8,128)S(1)} %partial_sketch.7.mine_ref), channel_id=1, source_target_pairs={{0,16},{16,0},{1,17},{17,1},{2,18},{18,2},{3,19},{19,3},{4,20},{20... | collective-permute-start | bytes 884744 | tf_op jit(solution)/shard_map/ppermute | solution.py:391
  287.1 5.6 %collective-permute-start.4 = (f32[72,1024]{1,0:T(8,128)S(1)}, f32[72,1024]{1,0:T(8,128)S(1)}, u32[]{:S(2)}, u32[]{:S(2)}) collective-permute-start(f32[72,1024]{1,0:T(8,128)S(1)} %partial_sketch.8.mine_ref), channel_id=1, source_target_pairs={{0,16},{16,0},{1,17},{17,1},{2,18},{18,2},{3,19},{19,3},{4,20},{20... | collective-permute-start | bytes 884744 | tf_op jit(solution)/shard_map/ppermute | solution.py:391
  329.3 5.3 %collective-permute-start.5 = (f32[72,1024]{1,0:T(8,128)S(1)}, f32[72,1024]{1,0:T(8,128)S(1)}, u32[]{:S(2)}, u32[]{:S(2)}) collective-permute-start(f32[72,1024]{1,0:T(8,128)S(1)} %partial_sketch.9.mine_ref), channel_id=1, source_target_pairs={{0,16},{16,0},{1,17},{17,1},{2,18},{18,2},{3,19},{19,3},{4,20},{20... | collective-permute-start | bytes 884744 | tf_op jit(solution)/shard_map/ppermute | solution.py:391
  371.6 21.1 %all-to-all-start.18 = ((f32[32,8,128]{2,1,0:T(8,128)}), f32[32,8,128]{2,1,0:T(8,128)S(1)}, u32[]{:S(2)}, u32[]{:S(2)}) async-start(f32[32,8,128]{2,1,0:T(8,128)} %get-tuple-element.28), calls=%async_computation.18 | async-start | bytes 262144 | tf_op jit(solution)/shard_map/all_to_all | solution.py:399
  380.4 7.5 %collective-permute-start.6 = (f32[32,128]{1,0:T(8,128)S(1)}, f32[32,128]{1,0:T(8,128)S(1)}, u32[]{:S(2)}, u32[]{:S(2)}) collective-permute-start(f32[32,128]{1,0:T(8,128)S(1)} %get-tuple-element.29), channel_id=1, source_target_pairs={{0,0},{1,16},{2,1},{3,17},{4,2},{5,18},{6,3},{7,19},{8,4},{9,20},{... | collective-permute-start | bytes 49160 | tf_op jit(solution)/shard_map/ppermute | solution.py:401
  387.9 4.8 %collective-permute-start.7 = (f32[32,128]{1,0:T(8,128)S(1)}, f32[32,128]{1,0:T(8,128)S(1)}, u32[]{:S(2)}, u32[]{:S(2)}) collective-permute-start(f32[32,128]{1,0:T(8,128)S(1)} %collective-permute-done.6.mine_ref), channel_id=1, source_target_pairs={{0,16},{16,0},{1,17},{17,1},{2,18},{18,2},{3,19},{19,3},{4,20},{20... | collective-permute-start | bytes 49160 | tf_op jit(solution)/shard_map/ppermute | solution.py:402

commit v7 on v6

--- a/solution.py
+++ b/solution.py
@@ -164,17 +164,15 @@
     half, depth, width = mate.shape
 
     def kernel(h_ref, a_ref, mate_ref, out_ref):
-        parts = [jnp.concatenate([h_ref[2 * i], h_ref[2 * i + 1]], axis=1) for i in range(half)]
-        for side in range(2):
-            rows = slice(side * RANK, (side + 1) * RANK)
-            for i in range(half):
-                block = mate_ref[i] if side else a_ref[lax.axis_index("c") * half + i, 0:depth, :]
-                term = lax.dot_general(parts[i], block, NT, preferred_element_type=F32)
-                if i == 0:
-                    out_ref[rows, :] = term
-                else:
-                    out_ref[rows, :] += term
-        whole = jnp.concatenate(parts, axis=1)
+        whole = jnp.concatenate([h_ref[k] for k in range(2 * half)], axis=1)
+        base = lax.axis_index("c") * half
+        span = depth // 4
+        for start in range(0, depth, span):
+            rows = slice(start, start + span)
+            own = jnp.concatenate([a_ref[base + i, rows, :] for i in range(half)], axis=1)
+            far = jnp.concatenate([mate_ref[i, rows, :] for i in range(half)], axis=1)
+            out_ref[0:RANK, rows] = lax.dot_general(whole, own, NT, preferred_element_type=F32)
+            out_ref[RANK : 2 * RANK, rows] = lax.dot_general(far, whole, NT, preferred_element_type=F32).T
         out_ref[2 * RANK :, :] = jnp.zeros((EXTRA, depth), F32)
         out_ref[2 * RANK :, 0:LANES] = pack(self_gram(whole))
 

time: 395 us -> 394 us (level)
  no operation moved by 1% of the time
where the time goes in v7:
time: 394 us; the launch traced here: 393 us
  blocking collectives  298 us (76%)
  Pallas kernels  44.3 us (11%)
  starting transfers between devices  36.8 us (9%)
  waiting for transfers between devices  9.6 us (2%)
  local copies, waits for them, and re-layouts  4.09 us (1%)
    all_to_all x1, blocking collectives, shards(): a = lax.all_to_all(a, 't', 0, 0)  101 us
    all_to_all x6, blocking collectives, shards(): part = lax.all_to_all(part, 'z', 0, 0)  67.2 us
    all_to_all x5, blocking collectives, shards(): part = lax.all_to_all(out, 't', 0, 0)  63.4 us
    all_to_all x5, blocking collectives, shards(): h = lax.all_to_all(h, ('c', 't') if last else 't', 0, 0)  49.4 us
    ppermute x5, starting transfers between devices, shards(): other = lax.ppermute(sketch, 'c', swap)  19.9 us
    all_to_all x1, blocking collectives, shards(): part = lax.all_to_all(out, ('c', 't'), 0, 0)  16.1 us
    pallas_call x5, Pallas kernels, product_step(): pl.pallas_call(kernel, out_shape=out_shape, in_specs=[pl.BlockSpec(memory...  14.2 us
    pallas_call x5, Pallas kernels, sketch_step(): pl.pallas_call(kernel, out_shape=jax.ShapeDtypeStruct((2 * RANK + EXTRA,...  11.6 us
  transfers between devices with their start and end apart: 9, of which 6 were waited for; matrix products, arithmetic and copies ran while one was open for 0% of the time, Pallas kernels for 1%

profile of v7, /device:TPU:13, one launch (start us, length us, event | category | flops | bytes accessed | tf_op | source)
XLA Modules:
  0.0 393.0 jit_solution(2774125880297965275)
XLA Ops:
  0.6 3.4 copy-done
  5.5 101.3 %all_to_all.95.a_ref = bf16[16,1056,256]{2,1,0:T(8,128)(2,1)S(1)} all-to-all(bf16[16,1056,256]{2,1,0:T(8,128)(2,1)S(1)} %append_basis.1), channel_id=1, replica_groups=mesh['z'=8,'c'=2,'t'=16] {'t'}, dimensions={0} | all-to-all | bytes 17301504 | tf_op jit(solution)/shard_map/all_to_all | solution.py:379
  106.8 4.5 %first_products.1 = (f32[32,40,128]{2,1,0:T(8,128)S(1)}, bf16[8,1024,256]{2,1,0:T(8,128)(2,1)S(1)}) custom-call(bf16[16,1056,256]{2,1,0:T(8,128)(2,1)S(1)} %all_to_all.95.a_ref), custom_call_target="tpu_custom_call" | custom-call | tf_op jit(solution)/shard_map/first_products/pallas_call | solution.py:143
  113.1 16.1 %all_to_all.96.in_ref = f32[32,40,128]{2,1,0:T(8,128)S(1)} all-to-all(f32[32,40,128]{2,1,0:T(8,128)S(1)} %get-tuple-element.16), channel_id=1, replica_groups=mesh['z'=8,'c'=2,'t'=16] {'c','t'}, dimensions={0} | all-to-all | bytes 1310720 | tf_op jit(solution)/shard_map/all_to_all | solution.py:383
  129.3 16.6 %all_to_all.97.in_ref = f32[8,40,128]{2,1,0:T(8,128)S(1)} all-to-all(f32[8,40,128]{2,1,0:T(8,128)S(1)} %sum_parts.6), channel_id=1, replica_groups=mesh['z'=8,'c'=2,'t'=16] {'z'}, dimensions={0} | all-to-all | bytes 327680 | tf_op jit(solution)/shard_map/all_to_all | solution.py:395
  147.4 10.6 %all_to_all.98.h_ref = bf16[16,32,128]{2,1,0:T(8,128)(2,1)S(1)} all-to-all(bf16[16,32,128]{2,1,0:T(8,128)(2,1)S(1)} %get-tuple-element.17), channel_id=1, replica_groups=mesh['z'=8,'c'=2,'t'=16] {'t'}, dimensions={0} | all-to-all | bytes 262144 | tf_op jit(solution)/shard_map/all_to_all | solution.py:397
  160.2 2.9 collective-permute-start.1
  167.1 11.2 %all_to_all.99.in_ref = f32[16,40,128]{2,1,0:T(8,128)S(1)} all-to-all(f32[16,40,128]{2,1,0:T(8,128)S(1)} %hour_products.5), channel_id=1, replica_groups=mesh['z'=8,'c'=2,'t'=16] {'t'}, dimensions={0} | all-to-all | bytes 655360 | tf_op jit(solution)/shard_map/all_to_all | solution.py:391
  178.3 10.8 %all_to_all.100.in_ref = f32[8,40,128]{2,1,0:T(8,128)S(1)} all-to-all(f32[8,40,128]{2,1,0:T(8,128)S(1)} %sum_parts.7), channel_id=1, replica_groups=mesh['z'=8,'c'=2,'t'=16] {'z'}, dimensions={0} | all-to-all | bytes 327680 | tf_op jit(solution)/shard_map/all_to_all | solution.py:395
  190.3 9.8 %all_to_all.101.h_ref = bf16[16,32,128]{2,1,0:T(8,128)(2,1)S(1)} all-to-all(bf16[16,32,128]{2,1,0:T(8,128)(2,1)S(1)} %get-tuple-element.19), channel_id=1, replica_groups=mesh['z'=8,'c'=2,'t'=16] {'t'}, dimensions={0} | all-to-all | bytes 262144 | tf_op jit(solution)/shard_map/all_to_all | solution.py:397
  202.4 4.3 %collective-permute-start.2 = (f32[72,1024]{1,0:T(8,128)S(1)}, f32[72,1024]{1,0:T(8,128)S(1)}, u32[]{:S(2)}, u32[]{:S(2)}) collective-permute-start(f32[72,1024]{1,0:T(8,128)S(1)} %partial_sketch.6.mine_ref), channel_id=1, source_target_pairs={{0,16},{16,0},{1,17},{17,1},{2,18},{18,2},{3,19},{19,3},{4,20},{20... | collective-permute-start | bytes 884744 | tf_op jit(solution)/shard_map/ppermute | solution.py:389
  207.9 2.9 hour_products.6
  210.8 10.1 %all_to_all.102.in_ref = bf16[16,48,128]{2,1,0:T(8,128)(2,1)S(1)} all-to-all(bf16[16,48,128]{2,1,0:T(8,128)(2,1)S(1)} %hour_products.6), channel_id=1, replica_groups=mesh['z'=8,'c'=2,'t'=16] {'t'}, dimensions={0} | all-to-all | bytes 393216 | tf_op jit(solution)/shard_map/all_to_all | solution.py:391
  221.0 10.0 %all_to_all.103.in_ref = bf16[8,48,128]{2,1,0:T(8,128)(2,1)S(1)} all-to-all(bf16[8,48,128]{2,1,0:T(8,128)(2,1)S(1)} %sum_parts.8), channel_id=1, replica_groups=mesh['z'=8,'c'=2,'t'=16] {'z'}, dimensions={0} | all-to-all | bytes 196608 | tf_op jit(solution)/shard_map/all_to_all | solution.py:395
  232.2 9.7 %all_to_all.104.h_ref = bf16[16,32,128]{2,1,0:T(8,128)(2,1)S(1)} all-to-all(bf16[16,32,128]{2,1,0:T(8,128)(2,1)S(1)} %get-tuple-element.21), channel_id=1, replica_groups=mesh['z'=8,'c'=2,'t'=16] {'t'}, dimensions={0} | all-to-all | bytes 262144 | tf_op jit(solution)/shard_map/all_to_all | solution.py:397
  244.2 4.2 %collective-permute-start.3 = (f32[72,1024]{1,0:T(8,128)S(1)}, f32[72,1024]{1,0:T(8,128)S(1)}, u32[]{:S(2)}, u32[]{:S(2)}) collective-permute-start(f32[72,1024]{1,0:T(8,128)S(1)} %partial_sketch.7.mine_ref), channel_id=1, source_target_pairs={{0,16},{16,0},{1,17},{17,1},{2,18},{18,2},{3,19},{19,3},{4,20},{20... | collective-permute-start | bytes 884744 | tf_op jit(solution)/shard_map/ppermute | solution.py:389
  249.6 2.9 hour_products.7
  252.5 10.1 %all_to_all.105.in_ref = bf16[16,48,128]{2,1,0:T(8,128)(2,1)S(1)} all-to-all(bf16[16,48,128]{2,1,0:T(8,128)(2,1)S(1)} %hour_products.7), channel_id=1, replica_groups=mesh['z'=8,'c'=2,'t'=16] {'t'}, dimensions={0} | all-to-all | bytes 393216 | tf_op jit(solution)/shard_map/all_to_all | solution.py:391
  262.7 10.0 %all_to_all.106.in_ref = bf16[8,48,128]{2,1,0:T(8,128)(2,1)S(1)} all-to-all(bf16[8,48,128]{2,1,0:T(8,128)(2,1)S(1)} %sum_parts.9), channel_id=1, replica_groups=mesh['z'=8,'c'=2,'t'=16] {'z'}, dimensions={0} | all-to-all | bytes 196608 | tf_op jit(solution)/shard_map/all_to_all | solution.py:395
  274.0 9.7 %all_to_all.107.h_ref = bf16[16,32,128]{2,1,0:T(8,128)(2,1)S(1)} all-to-all(bf16[16,32,128]{2,1,0:T(8,128)(2,1)S(1)} %get-tuple-element.23), channel_id=1, replica_groups=mesh['z'=8,'c'=2,'t'=16] {'t'}, dimensions={0} | all-to-all | bytes 262144 | tf_op jit(solution)/shard_map/all_to_all | solution.py:397
  285.9 4.4 %collective-permute-start.4 = (f32[72,1024]{1,0:T(8,128)S(1)}, f32[72,1024]{1,0:T(8,128)S(1)}, u32[]{:S(2)}, u32[]{:S(2)}) collective-permute-start(f32[72,1024]{1,0:T(8,128)S(1)} %partial_sketch.8.mine_ref), channel_id=1, source_target_pairs={{0,16},{16,0},{1,17},{17,1},{2,18},{18,2},{3,19},{19,3},{4,20},{20... | collective-permute-start | bytes 884744 | tf_op jit(solution)/shard_map/ppermute | solution.py:389
  291.6 2.9 hour_products.8
  294.4 10.1 %all_to_all.108.in_ref = bf16[16,48,128]{2,1,0:T(8,128)(2,1)S(1)} all-to-all(bf16[16,48,128]{2,1,0:T(8,128)(2,1)S(1)} %hour_products.8), channel_id=1, replica_groups=mesh['z'=8,'c'=2,'t'=16] {'t'}, dimensions={0} | all-to-all | bytes 393216 | tf_op jit(solution)/shard_map/all_to_all | solution.py:391
  304.6 10.0 %all_to_all.109.in_ref = bf16[8,48,128]{2,1,0:T(8,128)(2,1)S(1)} all-to-all(bf16[8,48,128]{2,1,0:T(8,128)(2,1)S(1)} %sum_parts.10), channel_id=1, replica_groups=mesh['z'=8,'c'=2,'t'=16] {'z'}, dimensions={0} | all-to-all | bytes 196608 | tf_op jit(solution)/shard_map/all_to_all | solution.py:395
  315.9 9.7 %all_to_all.110.h_ref = bf16[16,32,128]{2,1,0:T(8,128)(2,1)S(1)} all-to-all(bf16[16,32,128]{2,1,0:T(8,128)(2,1)S(1)} %get-tuple-element.25), channel_id=1, replica_groups=mesh['z'=8,'c'=2,'t'=16] {'t'}, dimensions={0} | all-to-all | bytes 262144 | tf_op jit(solution)/shard_map/all_to_all | solution.py:397
  327.9 4.2 %collective-permute-start.5 = (f32[72,1024]{1,0:T(8,128)S(1)}, f32[72,1024]{1,0:T(8,128)S(1)}, u32[]{:S(2)}, u32[]{:S(2)}) collective-permute-start(f32[72,1024]{1,0:T(8,128)S(1)} %partial_sketch.9.mine_ref), channel_id=1, source_target_pairs={{0,16},{16,0},{1,17},{17,1},{2,18},{18,2},{3,19},{19,3},{4,20},{20... | collective-permute-start | bytes 884744 | tf_op jit(solution)/shard_map/ppermute | solution.py:389
  333.3 2.9 hour_products.9
  336.2 21.7 %all_to_all.111.in_ref.s_ref = bf16[16,304,128]{2,1,0:T(8,128)(2,1)S(1)} all-to-all(bf16[16,304,128]{2,1,0:T(8,128)(2,1)S(1)} %hour_products.9), channel_id=1, replica_groups=mesh['z'=8,'c'=2,'t'=16] {'t'}, dimensions={0} | all-to-all | bytes 2490368 | tf_op jit(solution)/shard_map/all_to_all | solution.py:391
  358.0 10.1 %all_to_all.112.in_ref = bf16[8,48,128]{2,1,0:T(8,128)(2,1)S(1)} all-to-all(bf16[8,48,128]{2,1,0:T(8,128)(2,1)S(1)} %sum_parts.11), channel_id=1, replica_groups=mesh['z'=8,'c'=2,'t'=16] {'z'}, dimensions={0} | all-to-all | bytes 196608 | tf_op jit(solution)/shard_map/all_to_all | solution.py:395
  370.2 8.8 %all-to-all-start.18 = ((f32[32,8,128]{2,1,0:T(8,128)}), f32[32,8,128]{2,1,0:T(8,128)S(1)}, u32[]{:S(2)}, u32[]{:S(2)}) async-start(f32[32,8,128]{2,1,0:T(8,128)} %get-tuple-element.28), calls=%async_computation.18 | async-start | bytes 262144 | tf_op jit(solution)/shard_map/all_to_all | solution.py:397
  379.0 3.9 collective-permute-start.6
  382.9 3.6 collective-permute-done.6.mine_ref
  (34 shorter events, 39.2 us)
Async XLA Ops:
  0.6 3.4 copy-start
  4.0 0.7 copy-start.1
  111.3 46.6 %collective-permute-start = (bf16[8,1024,256]{2,1,0:T(8,128)(2,1)S(1)}, bf16[8,1024,256]{2,1,0:T(8,128)(2,1)S(1)}, u32[]{:S(2)}, u32[]{:S(2)}) collective-permute-start(bf16[8,1024,256]{2,1,0:T(8,128)(2,1)S(1)} %get-tuple-element.18), channel_id=1, source_target_pairs={{0,16},{16,0},{1,17},{17,1},{2,18},{18,2},{3,19},{19,3},{4,20},{20... | collective-permute-start | bytes 12582920 | tf_op jit(solution)/shard_map/ppermute | solution.py:382
  160.2 4.1 %collective-permute-start.1 = (f32[72,1024]{1,0:T(8,128)S(1)}, f32[72,1024]{1,0:T(8,128)S(1)}, u32[]{:S(2)}, u32[]{:S(2)}) collective-permute-start(f32[72,1024]{1,0:T(8,128)S(1)} %partial_sketch.5.mine_ref), channel_id=1, source_target_pairs={{0,16},{16,0},{1,17},{17,1},{2,18},{18,2},{3,19},{19,3},{4,20},{20... | collective-permute-start | bytes 884744 | tf_op jit(solution)/shard_map/ppermute | solution.py:389
  202.4 5.5 %collective-permute-start.2 = (f32[72,1024]{1,0:T(8,128)S(1)}, f32[72,1024]{1,0:T(8,128)S(1)}, u32[]{:S(2)}, u32[]{:S(2)}) collective-permute-start(f32[72,1024]{1,0:T(8,128)S(1)} %partial_sketch.6.mine_ref), channel_id=1, source_target_pairs={{0,16},{16,0},{1,17},{17,1},{2,18},{18,2},{3,19},{19,3},{4,20},{20... | collective-permute-start | bytes 884744 | tf_op jit(solution)/shard_map/ppermute | solution.py:389
  244.2 5.4 %collective-permute-start.3 = (f32[72,1024]{1,0:T(8,128)S(1)}, f32[72,1024]{1,0:T(8,128)S(1)}, u32[]{:S(2)}, u32[]{:S(2)}) collective-permute-start(f32[72,1024]{1,0:T(8,128)S(1)} %partial_sketch.7.mine_ref), channel_id=1, source_target_pairs={{0,16},{16,0},{1,17},{17,1},{2,18},{18,2},{3,19},{19,3},{4,20},{20... | collective-permute-start | bytes 884744 | tf_op jit(solution)/shard_map/ppermute | solution.py:389
  285.9 5.6 %collective-permute-start.4 = (f32[72,1024]{1,0:T(8,128)S(1)}, f32[72,1024]{1,0:T(8,128)S(1)}, u32[]{:S(2)}, u32[]{:S(2)}) collective-permute-start(f32[72,1024]{1,0:T(8,128)S(1)} %partial_sketch.8.mine_ref), channel_id=1, source_target_pairs={{0,16},{16,0},{1,17},{17,1},{2,18},{18,2},{3,19},{19,3},{4,20},{20... | collective-permute-start | bytes 884744 | tf_op jit(solution)/shard_map/ppermute | solution.py:389
  327.9 5.4 %collective-permute-start.5 = (f32[72,1024]{1,0:T(8,128)S(1)}, f32[72,1024]{1,0:T(8,128)S(1)}, u32[]{:S(2)}, u32[]{:S(2)}) collective-permute-start(f32[72,1024]{1,0:T(8,128)S(1)} %partial_sketch.9.mine_ref), channel_id=1, source_target_pairs={{0,16},{16,0},{1,17},{17,1},{2,18},{18,2},{3,19},{19,3},{4,20},{20... | collective-permute-start | bytes 884744 | tf_op jit(solution)/shard_map/ppermute | solution.py:389
  370.2 21.1 %all-to-all-start.18 = ((f32[32,8,128]{2,1,0:T(8,128)}), f32[32,8,128]{2,1,0:T(8,128)S(1)}, u32[]{:S(2)}, u32[]{:S(2)}) async-start(f32[32,8,128]{2,1,0:T(8,128)} %get-tuple-element.28), calls=%async_computation.18 | async-start | bytes 262144 | tf_op jit(solution)/shard_map/all_to_all | solution.py:397
  379.0 7.5 %collective-permute-start.6 = (f32[32,128]{1,0:T(8,128)S(1)}, f32[32,128]{1,0:T(8,128)S(1)}, u32[]{:S(2)}, u32[]{:S(2)}) collective-permute-start(f32[32,128]{1,0:T(8,128)S(1)} %get-tuple-element.29), channel_id=1, source_target_pairs={{0,0},{1,16},{2,1},{3,17},{4,2},{5,18},{6,3},{7,19},{8,4},{9,20},{... | collective-permute-start | bytes 49160 | tf_op jit(solution)/shard_map/ppermute | solution.py:399
  386.5 4.8 %collective-permute-start.7 = (f32[32,128]{1,0:T(8,128)S(1)}, f32[32,128]{1,0:T(8,128)S(1)}, u32[]{:S(2)}, u32[]{:S(2)}) collective-permute-start(f32[32,128]{1,0:T(8,128)S(1)} %collective-permute-done.6.mine_ref), channel_id=1, source_target_pairs={{0,16},{16,0},{1,17},{17,1},{2,18},{18,2},{3,19},{19,3},{4,20},{20... | collective-permute-start | bytes 49160 | tf_op jit(solution)/shard_map/ppermute | solution.py:400
